TPU v7x, 512 devices: a whole 4x8x8 slice. The times are simulated.
512 devices in a mesh: lon: 32 (over z_lo, x, core), lat: 16 (over z_hi, y).
Axes of the slice: x: 4, y: 8, z: 8 (z_hi: 2, z_lo: 4; z = z_hi * 4 + z_lo), core: 2. Of those that a mesh axis runs over, the one named last changes fastest.
Arguments:
- tokens: bfloat16 [96, 768, 512], P('lat', 'lon'), may hold values from -10 to 10
- land_mask: int32 [96, 768], P('lat', 'lon'), may hold values 0 or 1
- keep_rows: int32 [96], replicated, may hold values from 0 to 1, as said below
- land_embed: float32 [2, 512], replicated, may hold values from -4 to 4
- norm_gains: float32 [2, 512], replicated, may hold values from 0.1 to 1.9
- w_qkv: bfloat16 [2, 512, 768], replicated, may hold values from -0.25 to 0.25
- w_proj: bfloat16 [2, 256, 512], replicated, may hold values from -0.375 to 0.375
- rel_bias: float32 [2, 8, 253], replicated, may hold values from -6 to 330
- cotangent: bfloat16 [96, 768, 512], P('lat', 'lon'), may hold values from -6 to 6
Outputs:
- output: float32 [96, 768, 512], P('lat', 'lon')
- grad_tokens: bfloat16 [96, 768, 512], P('lat', 'lon')
- grad_proj: bfloat16 [2, 256, 512], replicated
- grad_gains: float32 [2, 512], replicated
Inputs may be any that keep to these rules, and one draw needn't show every extreme that they name: keep_rows[i] = 1 wherever i % 3 == 1, and wherever 96 // 4 <= i < 72.
All inputs are finite; a program needn't handle non-finite values. No bound on the sum of `land_mask` on one device may be relied on, other than what follows from the above.
Results may differ from a plain program's by a relative error of at most 0.015.
Values may be sent and summed in bfloat16 or wider, within the bound.
No kernel may reach another device: no remote copies, remote signals or barrier semaphores. Data moves between devices by JAX's collectives and lax.ppermute only.
A program may use at most 64 MiB of HBM per device.

v0:
```python
import jax
import jax.numpy as jnp
from jax import lax
from jax.sharding import PartitionSpec as P

HEAD_DIM = 32
HEADS = 8
WIN_LAT = 6
WIN_LON = 12


NORM_EPS = 1e-05


def passed_along(array, axis, by):
    length = lax.axis_size(axis)
    return lax.ppermute(array, axis, [(i, (i + by) % length) for i in range(length)])


def layer_norm(values, gain_row):
    row_mean = jnp.mean(values, axis=-1, keepdims=True)
    centred = values - row_mean
    row_var = jnp.mean(centred * centred, axis=-1, keepdims=True)
    inv_std = lax.rsqrt(row_var + NORM_EPS)
    unit_rows = centred * inv_std
    return ((unit_rows * gain_row).astype(jnp.bfloat16), unit_rows, inv_std)


def norm_back(d_normed, unit_rows, inv_std, gain_row):
    d_float = d_normed.astype(jnp.float32)
    d_unit = d_float * gain_row
    mean_grad = jnp.mean(d_unit, axis=-1, keepdims=True)
    mean_proj = jnp.mean(d_unit * unit_rows, axis=-1, keepdims=True)
    d_input = inv_std * (d_unit - mean_grad - unit_rows * mean_proj)
    return (d_input, jnp.sum(d_float * unit_rows, axis=(0, 1)))


def to_windows(field_grid):
    rows_all, cols_all = (field_grid.shape[0], field_grid.shape[1])
    trailing = tuple(field_grid.shape[2:])
    blocked = field_grid.reshape(
        (rows_all // WIN_LAT, WIN_LAT, cols_all // WIN_LON, WIN_LON) + trailing
    )
    blocked = jnp.swapaxes(blocked, 1, 2)
    return blocked.reshape(
        (rows_all // WIN_LAT * (cols_all // WIN_LON), WIN_LAT * WIN_LON) + trailing
    )


def from_windows(windows_in, rows_all, cols_all):
    trailing = tuple(windows_in.shape[2:])
    reshaped = windows_in.reshape(
        (rows_all // WIN_LAT, cols_all // WIN_LON, WIN_LAT, WIN_LON) + trailing
    )
    reshaped = jnp.swapaxes(reshaped, 1, 2)
    return reshaped.reshape((rows_all, cols_all) + trailing)


def relative_table(rel_bias):
    span_lat = 2 * WIN_LAT - 1
    span_lon = 2 * WIN_LON - 1
    table = rel_bias.reshape(rel_bias.shape[0], rel_bias.shape[1], span_lat, span_lon)
    lat_pos = jnp.arange(WIN_LAT, dtype=jnp.int32)
    lon_pos = jnp.arange(WIN_LON, dtype=jnp.int32)
    pick_lat = (
        lat_pos[:, None, None] - lat_pos[None, :, None] + WIN_LAT - 1
        == jnp.arange(span_lat, dtype=jnp.int32)[None, None, :]
    ).astype(jnp.float32)
    pick_lon = (
        lon_pos[:, None, None] - lon_pos[None, :, None] + WIN_LON - 1
        == jnp.arange(span_lon, dtype=jnp.int32)[None, None, :]
    ).astype(jnp.float32)
    spread_full = jnp.einsum(
        "gnab,pqa,rsb->gnprqs", table, pick_lat, pick_lon, precision=lax.Precision.HIGHEST
    )
    win_size = WIN_LAT * WIN_LON
    return spread_full.reshape(table.shape[0], table.shape[1], win_size, win_size)


def row_lookup(keep_rows, row_index, cols_here):
    matches = row_index[:, None] == jnp.arange(keep_rows.shape[0], dtype=jnp.int32)[None, :]
    picked = jnp.sum(jnp.where(matches, keep_rows[None, :], 0), axis=1)
    return jnp.broadcast_to(picked[:, None], (row_index.shape[0], cols_here))


def key_allowed(keep_win, region_win):
    same_region = region_win[:, :, None] == region_win[:, None, :]
    return same_region & (keep_win[:, None, :] == 1)


def split_heads(qkv_win):
    pieces = qkv_win.reshape(qkv_win.shape[0], qkv_win.shape[1], 3, HEADS, HEAD_DIM)
    return (pieces[:, :, 0], pieces[:, :, 1], pieces[:, :, 2])


def attend(qkv_win, pos_bias, allowed):
    queries, keys_in, values = split_heads(qkv_win)
    scores = (
        jnp.einsum("wqhd,wkhd->whqk", queries, keys_in, preferred_element_type=jnp.float32)
        * HEAD_DIM ** (-0.5)
        + pos_bias[None]
    )
    scores = jnp.where(allowed[:, None], scores, -jnp.inf)
    row_max = jnp.max(scores, axis=-1, keepdims=True)
    exp_scores = jnp.exp(scores - row_max)
    attn_probs = exp_scores / jnp.sum(exp_scores, axis=-1, keepdims=True)
    head_out = jnp.einsum(
        "whqk,wkhd->wqhd",
        attn_probs.astype(jnp.bfloat16),
        values,
        preferred_element_type=jnp.float32,
    )
    head_out = head_out.astype(jnp.bfloat16)
    return (head_out.reshape(qkv_win.shape[0], qkv_win.shape[1], HEADS * HEAD_DIM), attn_probs)


def attend_back(d_out, qkv_win, attn_probs):
    queries, keys_in, values = split_heads(qkv_win)
    window_count, win_size = (qkv_win.shape[0], qkv_win.shape[1])
    d_heads = d_out.reshape(window_count, win_size, HEADS, HEAD_DIM)
    probs_low = attn_probs.astype(jnp.bfloat16)
    d_values = jnp.einsum(
        "whqk,wqhd->wkhd", probs_low, d_heads, preferred_element_type=jnp.float32
    ).astype(jnp.bfloat16)
    d_probs = jnp.einsum("wqhd,wkhd->whqk", d_heads, values, preferred_element_type=jnp.float32)
    d_scores = (
        attn_probs
        * (d_probs - jnp.sum(d_probs * attn_probs, axis=-1, keepdims=True))
        * HEAD_DIM ** (-0.5)
    )
    d_low = d_scores.astype(jnp.bfloat16)
    d_queries = jnp.einsum(
        "whqk,wkhd->wqhd", d_low, keys_in, preferred_element_type=jnp.float32
    ).astype(jnp.bfloat16)
    d_keys = jnp.einsum(
        "whqk,wqhd->wkhd", d_low, queries, preferred_element_type=jnp.float32
    ).astype(jnp.bfloat16)
    stacked = jnp.stack([d_queries, d_keys, d_values], axis=2)
    return stacked.reshape(window_count, win_size, 3 * HEADS * HEAD_DIM)


def local_attention(qkv_grid, pos_bias, keep_grid, region_grid):
    rows_here, cols_here = (qkv_grid.shape[0], qkv_grid.shape[1])
    allowed = key_allowed(to_windows(keep_grid), to_windows(region_grid))
    heads_win, attn_probs = attend(to_windows(qkv_grid), pos_bias, allowed)
    return (from_windows(heads_win, rows_here, cols_here), attn_probs)


def local_attention_back(d_grid, qkv_grid, attn_probs):
    rows_here, cols_here = (qkv_grid.shape[0], qkv_grid.shape[1])
    d_win = attend_back(to_windows(d_grid), to_windows(qkv_grid), attn_probs)
    return from_windows(d_win, rows_here, cols_here)


def project(field_grid, weight):
    return jnp.dot(field_grid, weight, preferred_element_type=jnp.float32).astype(jnp.bfloat16)


def project_back(field_grid, weight):
    product = lax.dot_general(
        field_grid, weight, (((2,), (1,)), ((), ())), preferred_element_type=jnp.float32
    )
    return product.astype(jnp.bfloat16)


def outer_sum(left_grid, right_grid):
    left_flat = left_grid.reshape(-1, left_grid.shape[-1])
    right_flat = right_grid.reshape(-1, right_grid.shape[-1])
    return lax.dot_general(
        left_flat, right_flat, (((0,), (0,)), ((), ())), preferred_element_type=jnp.float32
    )


def roll_grid(field_grid, direction):
    half_lat = WIN_LAT // 2
    half_lon = WIN_LON // 2
    if direction > 0:
        edge_cols = field_grid[:, :half_lon]
    else:
        edge_cols = field_grid[:, -half_lon:]
    landed = passed_along(edge_cols, "lon", -direction)
    if direction > 0:
        moved = jnp.concatenate([field_grid[:, half_lon:], landed], axis=1)
        edge_rows = moved[:half_lat]
    else:
        moved = jnp.concatenate([landed, field_grid[:, :-half_lon]], axis=1)
        edge_rows = moved[-half_lat:]
    arrived = passed_along(edge_rows, "lat", -direction)
    if direction > 0:
        return jnp.concatenate([moved[half_lat:], arrived], axis=0)
    return jnp.concatenate([arrived, moved[:-half_lat]], axis=0)


def local(tokens, land_mask, keep_rows, land_embed, norm_gains, w_qkv, w_proj, rel_bias, cotangent):
    rows_here, cols_here = (tokens.shape[0], tokens.shape[1])
    half_lat = WIN_LAT // 2
    lat_count = rows_here * lax.axis_size("lat")
    scale_out = float(lat_count * cols_here * lax.axis_size("lon")) ** (-0.5)
    pos_bias = relative_table(rel_bias)
    row_global = lax.axis_index("lat") * rows_here + jnp.arange(rows_here, dtype=jnp.int32)
    keep_one = row_lookup(keep_rows, row_global, cols_here)
    region_one = jnp.zeros((rows_here, cols_here), jnp.int32)
    source_rows = (row_global + half_lat) % lat_count
    keep_two = row_lookup(keep_rows, source_rows, cols_here)
    region_two = jnp.broadcast_to(
        (row_global >= lat_count - half_lat).astype(jnp.int32)[:, None], (rows_here, cols_here)
    )
    embedded = tokens.astype(jnp.float32) + jnp.where(
        land_mask[:, :, None] == 1, land_embed[1], land_embed[0]
    )
    normed_one, unit_one, inv_one = layer_norm(embedded, norm_gains[0])
    qkv_one = project(normed_one, w_qkv[0])
    heads_one, probs_one = local_attention(qkv_one, pos_bias[0], keep_one, region_one)
    branch_one = project(heads_one, w_proj[0])
    stream = embedded + branch_one.astype(jnp.float32)
    normed_two, unit_two, inv_two = layer_norm(stream, norm_gains[1])
    rolled_normed = roll_grid(normed_two, 1)
    qkv_two = project(rolled_normed, w_qkv[1])
    heads_two, probs_two = local_attention(qkv_two, pos_bias[1], keep_two, region_two)
    branch_two = roll_grid(project(heads_two, w_proj[1]), -1)
    output = stream + branch_two.astype(jnp.float32)
    carried_moved = roll_grid(cotangent, 1)
    proj_two = outer_sum(heads_two, carried_moved)
    d_heads_two = project_back(carried_moved, w_proj[1])
    d_qkv_two = local_attention_back(d_heads_two, qkv_two, probs_two)
    d_normed_two = roll_grid(project_back(d_qkv_two, w_qkv[1]), -1)
    d_branch_two, gain_two = norm_back(d_normed_two, unit_two, inv_two, norm_gains[1])
    d_stream = (cotangent.astype(jnp.float32) + d_branch_two).astype(jnp.bfloat16)
    proj_one = outer_sum(heads_one, d_stream)
    d_heads_one = project_back(d_stream, w_proj[0])
    d_qkv_one = local_attention_back(d_heads_one, qkv_one, probs_one)
    d_normed_one = project_back(d_qkv_one, w_qkv[0])
    d_branch_one, gain_one = norm_back(d_normed_one, unit_one, inv_one, norm_gains[0])
    grad_tokens = (d_stream.astype(jnp.float32) + d_branch_one).astype(jnp.bfloat16)
    early_proj, late_proj, early_gain, late_gain = lax.psum(
        (proj_one, proj_two, gain_one, gain_two), ("lon", "lat")
    )
    grad_proj = (jnp.stack([early_proj, late_proj]) * scale_out).astype(jnp.bfloat16)
    grad_gains = jnp.stack([early_gain, late_gain]) * scale_out
    return (output, grad_tokens, grad_proj, grad_gains)


def solution(mesh):
    in_specs = (
        P("lat", "lon", None),
        P("lat", "lon"),
        P(),
        P(),
        P(),
        P(),
        P(),
        P(),
        P("lat", "lon", None),
    )
    out_specs = (P("lat", "lon", None), P("lat", "lon", None), P(), P())
    return jax.shard_map(local, mesh=mesh, in_specs=in_specs, out_specs=out_specs, check_vma=False)
```

profile of v0, /device:TPU:1, one launch (start us, length us, event | category | flops | bytes accessed | tf_op | source)
XLA Modules:
  0.0 482.8 jit_solution(9034411736497324124)
XLA Ops:
  7.2 0.8 fusion.149
  8.0 0.7 broadcast_compare_fusion
  8.7 1.1 fusion.63
  9.8 1.1 multiply_reduce_fusion.5
  10.9 0.8 fusion.148
  11.7 1.6 convolution_convert_fusion.1
  15.3 0.8 fusion.103
  16.1 6.9 %convolution_bitcast_fusion = f32[2,8,6,12,6,12]{5,4,2,1,0,3:T(8,128)S(1)} fusion(f32[12,12,2,8,11]{4,1,3,2,0:T(8,128)S(1)} %fusion.103, s32[6,6]{1,0:T(8,128)S(1)} %subtract_add_fusion.1), kind=kOutput, calls=%fused_computation.4 | convolution fusion | flops 10949004 | bytes 433296 | tf_op jit(solution)/shard_map/gnab,pqa,rsb->gnprqs/dot_general | solution.py:73
  23.1 2.6 fusion.145
  25.7 3.8 copy.108
  29.5 0.5 reshape.193
  30.3 0.5 fusion.150
  32.7 0.6 slice.147
  33.3 8.8 %collective-permute-start = (bf16[6,6,512]{2,1,0:T(8,128)(2,1)}, bf16[6,6,512]{2,1,0:T(8,128)(2,1)}, u32[]{:S(2)}, u32[]{:S(2)}) collective-permute-start(bf16[6,6,512]{2,1,0:T(8,128)(2,1)} %slice.147), channel_id=1, source_target_pairs={{0,496},{16,0},{32,16},{48,32},{64,48},{80,64},{96,80},{112,96},{1... | collective-permute-start | bytes 110600 | tf_op jit(solution)/shard_map/ppermute | solution.py:17
  42.1 4.2 collective-permute-start.4
  46.6 0.7 compare_and_fusion
  47.5 3.8 copy.109
  51.3 1.2 reshape.194
  52.5 0.8 fusion.108
  53.3 10.8 %collective-permute-start.1 = (bf16[3,24,512]{2,1,0:T(8,128)(2,1)S(1)}, bf16[3,24,512]{2,1,0:T(8,128)(2,1)S(1)}, u32[]{:S(2)}, u32[]{:S(2)}) collective-permute-start(bf16[3,24,512]{2,1,0:T(8,128)(2,1)S(1)} %get-tuple-element.30), channel_id=1, source_target_pairs={{0,15},{1,0},{2,1},{3,2},{4,3},{5,4},{6,5},{7,6},{8,7},{9,8},{10,9... | collective-permute-start | bytes 221192 | tf_op jit(solution)/shard_map/ppermute | solution.py:17
  64.1 0.8 fusion.106
  64.9 3.1 collective-permute-start.5
  68.1 1.4 convolution_convert_fusion
  72.5 1.2 fusion.156
  73.7 1.3 fusion.25
  75.4 1.0 fusion.27
  77.4 1.9 collective-permute-start.2
  79.5 0.7 copy.85
  80.2 0.6 reshape_reshape.37
  80.9 1.5 convolution_convert_fusion.3
  82.5 1.9 collective-permute-start.6
  84.4 1.1 convolution_bitcast_fusion.1
  85.5 0.9 collective-permute-done.6
  86.4 2.3 collective-permute-start.7
  88.7 1.9 collective-permute-start.3
  90.7 7.5 %collective-permute-done.7 = bf16[3,24,512]{2,1,0:T(8,128)(2,1)S(1)} collective-permute-done((bf16[3,24,512]{2,1,0:T(8,128)(2,1)S(1)}, bf16[3,24,512]{2,1,0:T(8,128)(2,1)S(1)}, u32[]{:S(2)}, u32[]{:S(2)}) %collective-permute-start.7) | collective-permute-done | bytes 73760 | tf_op jit(solution)/shard_map/ppermute | solution.py:17
  98.4 2.1 collective-permute-done.3
  100.6 0.8 fusion.55
  102.6 1.6 fusion.29
  104.9 0.7 copy.93
  105.6 0.6 reshape_reshape.39
  106.4 1.6 multiply_reduce_fusion.2
  108.0 99.0 %all-reduce = (f32[1,512]{1,0:T(1,128)S(1)}, f32[1,512]{1,0:T(1,128)S(1)}) all-reduce(f32[1,512]{1,0:T(1,128)S(1)} %bitcast.220, f32[1,512]{1,0:T(1,128)S(1)} %bitcast.224), channel_id=1, replica_groups=mesh['lon'=32,'lat'=16] {'lon','lat'}, use_global_device_ids=true, to_apply=%region_21.22 | all-reduce | flops 1024 | bytes 8192 | tf_op jit(solution)/shard_map/psum | solution.py:235
  207.0 1.1 convolution_bitcast_fusion.2
  208.1 0.6 maximum_multiply_fusion.1
  208.7 0.9 add_convert_fusion
  209.6 264.3 %all-reduce.4.cloned.1.call-done = (f32[1,256,512]{2,1,0:T(8,128)}, f32[1,256,512]{2,1,0:T(8,128)}) async-done(((f32[1,256,512]{2,1,0:T(8,128)}, f32[1,256,512]{2,1,0:T(8,128)}), (f32[1,256,512]{2,1,0:T(8,128)}, f32[1,256,512]{2,1,0:T(8,128)})) %all-reduce.4.cloned.1.call-update) | async-done | bytes 1048592 | tf_op jit(solution)/shard_map/psum | solution.py:235
  473.9 2.1 fusion.32
  (129 shorter events, 11.2 us)
Async XLA Ops:
  7.2 466.7 %all-reduce.4.cloned.1.call-start = ((), (), s32[]{:S(2)}) async-start(), calls=%async_computation | async-start | bytes 2097152 | tf_op jit(solution)/shard_map/psum | solution.py:235
  11.7 1.8 copy-start.12
  14.0 0.8 copy-start.14
  14.0 1.2 copy-start.11
  14.5 15.8 %copy-start.5 = (bf16[2,72,1,8,32]{1,4,3,0,2:T(8,128)(2,1)}, bf16[2,72,1,8,32]{1,4,3,0,2:T(8,128)(2,1)S(1)}, u32[]{:S(2)}) copy-start(bf16[2,72,1,8,32]{1,4,3,0,2:T(8,128)(2,1)S(1)} %copy.113) | copy-start | bytes 221188
  14.8 15.5 %copy-start.7 = (bf16[2,72,1,8,32]{1,4,3,0,2:T(8,128)(2,1)}, bf16[2,72,1,8,32]{1,4,3,0,2:T(8,128)(2,1)S(1)}, u32[]{:S(2)}) copy-start(bf16[2,72,1,8,32]{1,4,3,0,2:T(8,128)(2,1)S(1)} %copy.114) | copy-start | bytes 221188
  30.7 0.8 copy-start.18
  30.8 16.7 %copy-start.15 = (f32[2,8,72,72]{2,3,1,0:T(8,128)}, f32[2,8,72,72]{2,3,1,0:T(8,128)S(1)}, u32[]{:S(2)}) copy-start(f32[2,8,72,72]{2,3,1,0:T(8,128)S(1)} %get-tuple-element.36) | copy-start | bytes 995332
  30.8 1.1 copy-start
  30.8 1.3 copy-start.2
  31.0 11.1 %copy-start.1 = (bf16[6,24,512]{2,1,0:T(8,128)(2,1)S(1)}, bf16[6,24,512]{2,1,0:T(8,128)(2,1)}, u32[]{:S(2)}) copy-start(bf16[6,24,512]{2,1,0:T(8,128)(2,1)} %param.17) | copy-start | bytes 442372
  33.3 19.2 %collective-permute-start = (bf16[6,6,512]{2,1,0:T(8,128)(2,1)}, bf16[6,6,512]{2,1,0:T(8,128)(2,1)}, u32[]{:S(2)}, u32[]{:S(2)}) collective-permute-start(bf16[6,6,512]{2,1,0:T(8,128)(2,1)} %slice.147), channel_id=1, source_target_pairs={{0,496},{16,0},{32,16},{48,32},{64,48},{80,64},{96,80},{112,96},{1... | collective-permute-start | bytes 110600 | tf_op jit(solution)/shard_map/ppermute | solution.py:17
  42.1 22.0 %collective-permute-start.4 = (bf16[6,6,512]{2,1,0:T(8,128)(2,1)S(1)}, bf16[6,6,512]{2,1,0:T(8,128)(2,1)}, u32[]{:S(2)}, u32[]{:S(2)}) collective-permute-start(bf16[6,6,512]{2,1,0:T(8,128)(2,1)S(1)} %slice.135), channel_id=1, source_target_pairs={{0,496},{16,0},{32,16},{48,32},{64,48},{80,64},{96,80},{112,96},{1... | collective-permute-start | bytes 110600 | tf_op jit(solution)/shard_map/ppermute | solution.py:17
  53.3 14.8 %collective-permute-start.1 = (bf16[3,24,512]{2,1,0:T(8,128)(2,1)S(1)}, bf16[3,24,512]{2,1,0:T(8,128)(2,1)S(1)}, u32[]{:S(2)}, u32[]{:S(2)}) collective-permute-start(bf16[3,24,512]{2,1,0:T(8,128)(2,1)S(1)} %get-tuple-element.30), channel_id=1, source_target_pairs={{0,15},{1,0},{2,1},{3,2},{4,3},{5,4},{6,5},{7,6},{8,7},{9,8},{10,9... | collective-permute-start | bytes 221192 | tf_op jit(solution)/shard_map/ppermute | solution.py:17
  64.9 6.3 %collective-permute-start.5 = (bf16[3,24,512]{2,1,0:T(8,128)(2,1)S(1)}, bf16[3,24,512]{2,1,0:T(8,128)(2,1)S(1)}, u32[]{:S(2)}, u32[]{:S(2)}) collective-permute-start(bf16[3,24,512]{2,1,0:T(8,128)(2,1)S(1)} %get-tuple-element.28), channel_id=1, source_target_pairs={{0,15},{1,0},{2,1},{3,2},{4,3},{5,4},{6,5},{7,6},{8,7},{9,8},{10,9... | collective-permute-start | bytes 221192 | tf_op jit(solution)/shard_map/ppermute | solution.py:17
  70.2 1.1 copy-start.3
  71.0 1.5 copy-start.4
  71.0 1.5 copy-start.10
  73.7 1.3 copy-start.17
  76.4 3.0 copy-start.9
  77.4 11.3 %collective-permute-start.2 = (bf16[6,6,512]{2,1,0:T(8,128)(2,1)S(1)}, bf16[6,6,512]{2,1,0:T(8,128)(2,1)S(1)}, u32[]{:S(2)}, u32[]{:S(2)}) collective-permute-start(bf16[6,6,512]{2,1,0:T(8,128)(2,1)S(1)} %slice.154), channel_id=1, source_target_pairs={{0,16},{16,32},{32,48},{48,64},{64,80},{80,96},{96,112},{112,128},... | collective-permute-start | bytes 110600 | tf_op jit(solution)/shard_map/ppermute | solution.py:17
  82.5 3.9 collective-permute-start.6
  86.4 11.8 %collective-permute-start.7 = (bf16[3,24,512]{2,1,0:T(8,128)(2,1)S(1)}, bf16[3,24,512]{2,1,0:T(8,128)(2,1)S(1)}, u32[]{:S(2)}, u32[]{:S(2)}) collective-permute-start(bf16[3,24,512]{2,1,0:T(8,128)(2,1)S(1)} %fusion.105), channel_id=1, source_target_pairs={{0,1},{1,2},{2,3},{3,4},{4,5},{5,6},{6,7},{7,8},{8,9},{9,10},{10,1... | collective-permute-start | bytes 221192 | tf_op jit(solution)/shard_map/ppermute | solution.py:17
  88.7 11.8 %collective-permute-start.3 = (bf16[3,24,512]{2,1,0:T(8,128)(2,1)S(1)}, bf16[3,24,512]{2,1,0:T(8,128)(2,1)S(1)}, u32[]{:S(2)}, u32[]{:S(2)}) collective-permute-start(bf16[3,24,512]{2,1,0:T(8,128)(2,1)S(1)} %fusion.107), channel_id=1, source_target_pairs={{0,1},{1,2},{2,3},{3,4},{4,5},{5,6},{6,7},{7,8},{8,9},{9,10},{10,1... | collective-permute-start | bytes 221192 | tf_op jit(solution)/shard_map/ppermute | solution.py:17
  100.6 2.0 copy-start.8
  100.6 2.0 copy-start.19
  102.5 1.7 copy-start.6
  102.6 1.7 copy-start.16
  104.9 1.5 copy-start.13
Sparse Core Ops, SparseCore 0:
  208.2 265.6 all-reduce.3
where the time goes:
time: 484 us; the launch traced here: 483 us
  waiting for transfers between devices  275 us (57%)
  blocking collectives  99 us (20%)
  starting transfers between devices  35 us (7%)
  matrix products  24.7 us (5%)
  local copies, waits for them, and re-layouts  23.7 us (5%)
  between operations  15 us (3%)
  other arithmetic  10.6 us (2%)
    psum x1, waiting for transfers between devices, local(): lax.psum((proj_one, proj_two, gain_one, gain_two), ('lon', 'lat'))  264 us
    psum x1, blocking collectives, local(): lax.psum((proj_one, proj_two, gain_one, gain_two), ('lon', 'lat'))  99 us
    ppermute x8, starting transfers between devices, passed_along(): lax.ppermute(array, axis, [(i, (i + by) % length) for i in range(length)])  35 us
    ppermute x8, waiting for transfers between devices, passed_along(): lax.ppermute(array, axis, [(i, (i + by) % length) for i in range(length)])  10.5 us
  transfers between devices with their start and end apart: 9, of which 4 were waited for; matrix products, arithmetic and copies ran while one was open for 3% of the time, Pallas kernels for 0%

commit v1 on v0

v1 whole, which is shorter than its diff:
```python
import functools

import jax
import jax.numpy as jnp
import numpy as np
from jax import lax
from jax.experimental import pallas as pl
from jax.experimental.pallas import tpu as pltpu
from jax.sharding import PartitionSpec as P

D = 512
HEAD_DIM = 32
HEADS = 8
INNER = HEADS * HEAD_DIM
WIN_LAT = 6
WIN_LON = 12
HALF_LAT = WIN_LAT // 2
HALF_LON = WIN_LON // 2
WIN = WIN_LAT * WIN_LON
SPAN_LON = 2 * WIN_LON - 1
REACH = WIN_LAT * SPAN_LON
QPAD = 128
STACK = WIN * HEADS
GAIN_ROWS = 8

NORM_EPS = 1e-05
SCALE = HEAD_DIM ** (-0.5)
SHUT = -1e30

F32 = jnp.float32
BF16 = jnp.bfloat16


def dot_nn(left, right):
    return lax.dot_general(left, right, (((1,), (0,)), ((), ())), preferred_element_type=F32)


def dot_nt(left, right):
    return lax.dot_general(left, right, (((1,), (1,)), ((), ())), preferred_element_type=F32)


def dot_tn(left, right):
    return lax.dot_general(left, right, (((0,), (0,)), ((), ())), preferred_element_type=F32)


def window_matrices(cols):
    cells, count = WIN_LAT * cols, cols // WIN_LON
    order = np.zeros((count, QPAD, cells), np.float32)
    spread = np.zeros((count, WIN, HEADS, cells), np.float32)
    for w in range(count):
        for a in range(WIN_LAT):
            for e in range(WIN_LON):
                cell = a * cols + w * WIN_LON + e
                order[w, e * WIN_LAT + a, cell] = 1
                spread[w, e * WIN_LAT + a, :, cell] = 1
    return order.reshape(-1, cells), spread.reshape(-1, cells)


def reach_matrix():
    reach = np.zeros((REACH, WIN_LON, QPAD), np.float32)
    for e2 in range(WIN_LON):
        for a in range(WIN_LAT):
            for e in range(WIN_LON):
                reach[a * SPAN_LON + e - e2 + WIN_LON - 1, e2, e * WIN_LAT + a] = 1
    return reach.reshape(REACH, -1)


def roll_matrices(cols, direction):
    cells = WIN_LAT * cols
    own = np.zeros((cells, cells), np.float32)
    side = np.zeros((cells, WIN_LAT * HALF_LON), np.float32)
    far = np.zeros((cells, HALF_LAT * cols), np.float32)
    for i in range(WIN_LAT):
        for j in range(cols):
            row = i * cols + j
            from_i, from_j = i + direction * HALF_LAT, j + direction * HALF_LON
            if not 0 <= from_i < WIN_LAT:
                far[row, (from_i % WIN_LAT - (0 if direction > 0 else HALF_LAT)) * cols + j] = 1
            elif not 0 <= from_j < cols:
                side[row, from_i * HALF_LON + (from_j - cols if direction > 0 else from_j + HALF_LON)] = 1
            else:
                own[row, from_i * cols + from_j] = 1
    return own, side, far


def edge_matrix(cols, direction):
    edge = np.zeros((WIN_LAT, HALF_LON, WIN_LAT * cols), np.float32)
    for i in range(WIN_LAT):
        for j in range(HALF_LON):
            edge[i, j, i * cols + (j if direction > 0 else cols - HALF_LON + j)] = 1
    return edge.reshape(-1, WIN_LAT * cols)


def fixed(matrix):
    return jnp.asarray(matrix, BF16)


def norm_stats(values):
    row_mean = jnp.sum(values, axis=-1, keepdims=True) * (1.0 / D)
    centred = values - row_mean
    row_var = jnp.sum(centred * centred, axis=-1, keepdims=True) * (1.0 / D)
    inv_std = lax.rsqrt(row_var + NORM_EPS)
    return centred * inv_std, inv_std


def norm_back(d_float, unit_rows, inv_std, gain_row):
    d_unit = d_float * gain_row
    mean_grad = jnp.sum(d_unit, axis=-1, keepdims=True) * (1.0 / D)
    mean_proj = jnp.sum(d_unit * unit_rows, axis=-1, keepdims=True) * (1.0 / D)
    d_input = inv_std * (d_unit - mean_grad - unit_rows * mean_proj)
    return d_input, jnp.sum(d_float * unit_rows, axis=0, keepdims=True)


def masked_bias(table, reach, keep_of, split_rows):
    shifted = jnp.concatenate(
        [
            table[:, (WIN_LAT - 1 - a2) * SPAN_LON : (WIN_LAT - 1 - a2) * SPAN_LON + REACH]
            for a2 in range(WIN_LAT)
        ],
        axis=0,
    )
    high = shifted.astype(BF16)
    rest = shifted - high.astype(F32)
    middle = rest.astype(BF16)
    low = (rest - middle.astype(F32)).astype(BF16)
    spread = dot_nn(high, reach) + (dot_nn(middle, reach) + dot_nn(low, reach))
    place = lax.broadcasted_iota(jnp.int32, (HEADS, QPAD), 1)
    query_late = jnp.where(place % WIN_LAT >= HALF_LAT, 1, 0)
    tiles = []
    for a2 in range(WIN_LAT):
        key_late = 1 if a2 >= HALF_LAT else 0
        apart = jnp.where(query_late == key_late, 0, 1) * split_rows
        shut = apart + jnp.where(keep_of(a2) == 1, 0, 1)
        tiles.append(jnp.where(shut > 0, SHUT, 0.0).astype(F32))
    tile = jnp.concatenate(tiles, axis=0)
    blocks = [spread[:, QPAD * e2 : QPAD * (e2 + 1)] + tile for e2 in range(WIN_LON)]
    return jnp.concatenate(blocks, axis=0).reshape(WIN, HEADS, QPAD)


def lay_out(qkv, order, spread):
    count = order.shape[0] // QPAD
    queries = dot_nn(order, qkv[:, :INNER]).astype(BF16)
    stacked = dot_nn(spread, qkv[:, INNER:])
    head = lax.broadcasted_iota(jnp.int32, (HEADS, 2 * INNER), 0)
    lane = lax.broadcasted_iota(jnp.int32, (HEADS, 2 * INNER), 1)
    own = jnp.where((lane // HEAD_DIM) % HEADS == head, 1.0, 0.0).astype(F32)
    stacked = stacked.reshape(count * WIN, HEADS, 2 * INNER) * own[None]
    stacked = stacked.reshape(count * STACK, 2 * INNER).astype(BF16)
    return queries, stacked[:, :INNER], stacked[:, INNER:], own


def attend(queries, keys, values, bias, order_back):
    count = queries.shape[0] // QPAD
    all_probs, outs = [], []
    for w in range(count):
        rows = slice(w * STACK, (w + 1) * STACK)
        scores = dot_nt(keys[rows], queries[w * QPAD : (w + 1) * QPAD])
        scores = scores.reshape(WIN, HEADS, QPAD) * SCALE + bias
        exp_scores = jnp.exp(scores - jnp.max(scores, axis=0, keepdims=True))
        probs = exp_scores * (1.0 / jnp.sum(exp_scores, axis=0, keepdims=True))
        all_probs.append(probs)
        low = probs.reshape(STACK, QPAD).astype(BF16)
        outs.append(dot_tn(low, values[rows]).astype(BF16))
    heads = dot_nn(order_back, jnp.concatenate(outs, axis=0)).astype(BF16)
    return heads, all_probs


def attend_back(d_heads, all_probs, queries, keys, values, own, order, order_back, spread_back):
    d_out = dot_nn(order, d_heads).astype(BF16)
    d_queries, d_stack = [], []
    for w, probs in enumerate(all_probs):
        rows = slice(w * STACK, (w + 1) * STACK)
        here = slice(w * QPAD, (w + 1) * QPAD)
        d_probs = dot_nt(values[rows], d_out[here]).reshape(WIN, HEADS, QPAD)
        total = jnp.sum(d_probs * probs, axis=0, keepdims=True)
        d_low = (probs * (d_probs - total) * SCALE).reshape(STACK, QPAD).astype(BF16)
        low = probs.reshape(STACK, QPAD).astype(BF16)
        d_queries.append(dot_tn(d_low, keys[rows]).astype(BF16))
        d_keys = dot_nn(d_low, queries[here])
        d_values = dot_nn(low, d_out[here])
        both = jnp.concatenate([d_keys, d_values], axis=1).reshape(WIN, HEADS, 2 * INNER) * own[None]
        d_stack.append(both.reshape(STACK, 2 * INNER).astype(BF16))
    d_query_grid = dot_nn(order_back, jnp.concatenate(d_queries, axis=0)).astype(BF16)
    d_rest = dot_nn(spread_back, jnp.concatenate(d_stack, axis=0)).astype(BF16)
    return jnp.concatenate([d_query_grid, d_rest], axis=1)


def first_kernel(
    row_ref, keep_ref, tokens_ref, mask_ref, embed_ref, gains_ref, w_qkv_ref, w_proj_ref, table_ref, cot_ref,
    order_ref, order_back_ref, spread_ref, reach_ref, edge_ref,
    stream_ref, unit_one_ref, inv_one_ref, qkv_ref, heads_ref, probs_ref, normed_ref, strip_ref,
):
    rows, cols = mask_ref.shape
    mask = mask_ref[...].astype(F32)
    spread_mask = jnp.concatenate([jnp.broadcast_to(mask[r : r + 1], (cols, cols)) for r in range(rows)], axis=0)
    cell = lax.broadcasted_iota(jnp.int32, (rows * cols, cols), 0)
    lane = lax.broadcasted_iota(jnp.int32, (rows * cols, cols), 1)
    land = jnp.sum(jnp.where(cell % cols == lane, spread_mask, 0.0), axis=1, keepdims=True)
    embedded = tokens_ref[...].astype(F32) + jnp.where(land == 1.0, embed_ref[1:2], embed_ref[0:1])
    unit_one, inv_one = norm_stats(embedded)
    unit_one_ref[...] = unit_one
    inv_one_ref[...] = jnp.broadcast_to(inv_one, inv_one_ref.shape)
    normed_one = (unit_one * gains_ref[0:1]).astype(BF16)
    qkv = dot_nn(normed_one, w_qkv_ref[0]).astype(BF16)
    qkv_ref[...] = qkv
    bias = masked_bias(table_ref[0], reach_ref[...], lambda a2: keep_ref[row_ref[0] + a2], 0)
    queries, keys, values, own = lay_out(qkv, order_ref[...], spread_ref[...])
    heads, all_probs = attend(queries, keys, values, bias, order_back_ref[...])
    for w, probs in enumerate(all_probs):
        probs_ref[w] = probs
    heads_ref[...] = heads
    branch = dot_nn(heads, w_proj_ref[0]).astype(BF16)
    stream = embedded + branch.astype(F32)
    stream_ref[...] = stream
    unit_two, _ = norm_stats(stream)
    normed_two = (unit_two * gains_ref[1:2]).astype(BF16)
    normed_ref[...] = normed_two
    edge = edge_ref[...]
    strip_ref[:, :D] = dot_nn(edge, normed_two).astype(BF16)
    strip_ref[:, D:] = dot_nn(edge, cot_ref[...]).astype(BF16)


def second_kernel(
    row_ref, keep_ref, normed_ref, cot_ref, landed_ref, arrived_ref, w_qkv_ref, w_proj_ref, table_ref,
    order_ref, order_back_ref, spread_ref, spread_back_ref, reach_ref, own_ref, side_ref, far_ref, edge_ref,
    back_ref, strip_ref, proj_ref,
):
    lat_count = keep_ref.shape[0]
    far_part = dot_nn(side_ref[...], landed_ref[...]) + dot_nn(far_ref[...], arrived_ref[...])
    normed = (dot_nn(own_ref[...], normed_ref[...]) + far_part[:, :D]).astype(BF16)
    carried = (dot_nn(own_ref[...], cot_ref[...]) + far_part[:, D:]).astype(BF16)
    last_band = jnp.where(row_ref[0] + WIN_LAT >= lat_count, 1, 0)

    def keep_of(a2):
        place = row_ref[0] + (a2 + HALF_LAT)
        return keep_ref[jnp.where(place >= lat_count, place - lat_count, place)]

    bias = masked_bias(table_ref[0], reach_ref[...], keep_of, last_band)
    order, order_back = order_ref[...], order_back_ref[...]
    qkv = dot_nn(normed, w_qkv_ref[0]).astype(BF16)
    d_heads = dot_nt(carried, w_proj_ref[0]).astype(BF16)
    queries, keys, values, own = lay_out(qkv, order, spread_ref[...])
    heads, all_probs = attend(queries, keys, values, bias, order_back)
    branch = dot_nn(heads, w_proj_ref[0]).astype(BF16)
    proj_ref[...] = dot_tn(heads, carried).astype(BF16)
    d_qkv = attend_back(d_heads, all_probs, queries, keys, values, own, order, order_back, spread_back_ref[...])
    d_normed = dot_nt(d_qkv, w_qkv_ref[0]).astype(BF16)
    both = jnp.concatenate([branch, d_normed], axis=1)
    back_ref[...] = both
    strip_ref[...] = dot_nn(edge_ref[...], both).astype(BF16)


def third_kernel(
    stream_ref, unit_one_ref, inv_one_ref, qkv_ref, heads_ref, probs_ref, cot_ref, back_ref, landed_ref, arrived_ref,
    gains_ref, w_qkv_ref, w_proj_ref, proj_two_ref,
    order_ref, order_back_ref, spread_ref, spread_back_ref, own_ref, side_ref, far_ref,
    output_ref, grad_ref, sums_ref,
):
    unrolled = (
        dot_nn(own_ref[...], back_ref[...])
        + dot_nn(side_ref[...], landed_ref[...])
        + dot_nn(far_ref[...], arrived_ref[...])
    )
    stream = stream_ref[...]
    output_ref[...] = stream + unrolled[:, :D]
    unit_two, inv_two = norm_stats(stream)
    d_branch, gain_two = norm_back(unrolled[:, D:], unit_two, inv_two, gains_ref[1:2])
    d_stream = (cot_ref[...].astype(F32) + d_branch).astype(BF16)
    proj_one = dot_tn(heads_ref[...], d_stream)
    d_heads = dot_nt(d_stream, w_proj_ref[0]).astype(BF16)
    order = order_ref[...]
    queries, keys, values, own = lay_out(qkv_ref[...], order, spread_ref[...])
    all_probs = [probs_ref[w] for w in range(probs_ref.shape[0])]
    d_qkv = attend_back(
        d_heads, all_probs, queries, keys, values, own, order, order_back_ref[...], spread_back_ref[...]
    )
    d_normed = dot_nt(d_qkv, w_qkv_ref[0]).astype(BF16)
    d_branch, gain_one = norm_back(d_normed.astype(F32), unit_one_ref[...], inv_one_ref[:, 0:1], gains_ref[0:1])
    grad_ref[...] = (d_stream.astype(F32) + d_branch).astype(BF16)
    shards, share = sums_ref.shape[0], sums_ref.shape[1]
    half = shards // 2
    sums_ref[:half, :, :D] = proj_one.reshape(half, share, D).astype(BF16)
    sums_ref[half:, :, :D] = proj_two_ref[...].astype(F32).reshape(half, share, D).astype(BF16)
    gain = jnp.concatenate(
        [row[:, 128 * j : 128 * (j + 1)] for row in (gain_one, gain_two) for j in range(D // 128)], axis=0
    )
    pair = gain_pair(gain, share)
    for s in range(shards):
        sums_ref[s, :, D:] = pair


def gain_pair(gain, share):
    high = gain.astype(BF16).astype(F32)
    parts = [high, gain - high]
    if share > 2 * GAIN_ROWS:
        parts.append(jnp.zeros((share - 2 * GAIN_ROWS, 128), F32))
    return jnp.concatenate(parts, axis=0).astype(BF16)


def added(parts_ref):
    total = parts_ref[0].astype(F32)
    for s in range(1, parts_ref.shape[0]):
        total = total + parts_ref[s].astype(F32)
    gain = total[:GAIN_ROWS, D:] + total[GAIN_ROWS : 2 * GAIN_ROWS, D:]
    return total[:, :D], gain


def lon_sum_kernel(parts_ref, out_ref):
    proj, gain = added(parts_ref)
    low = proj.astype(BF16)
    pair = gain_pair(gain, parts_ref.shape[1])
    for s in range(out_ref.shape[0]):
        out_ref[s, :, :D] = low
        out_ref[s, :, D:] = pair


def lat_sum_kernel(scale, parts_ref, proj_ref, gains_ref):
    proj, gain = added(parts_ref)
    low = (proj * scale).astype(BF16)
    for s in range(proj_ref.shape[0]):
        proj_ref[s] = low
    gain = gain * scale
    per_row = D // 128
    for r in range(GAIN_ROWS):
        gains_ref[r // per_row : r // per_row + 1, 128 * (r % per_row) : 128 * (r % per_row + 1)] = gain[r : r + 1]


def call(kernel, outs, operands):
    specs, arrays = [], []
    for operand in operands:
        if not isinstance(operand, tuple):
            specs.append(pl.BlockSpec(memory_space=pltpu.VMEM))
            arrays.append(operand)
        elif operand[0] == "scalars":
            specs.append(pl.BlockSpec(memory_space=pltpu.SMEM))
            arrays.append(operand[1])
        else:
            layer, array = operand
            rest = tuple(array.shape[1:])
            specs.append(pl.BlockSpec((1,) + rest, functools.partial(lambda b, i: (b,) + (0,) * 2, layer)))
            arrays.append(array)
    whole = [
        spec if spec.block_shape is not None or spec.memory_space == pltpu.SMEM
        else pl.BlockSpec(array.shape, functools.partial(lambda n, i: (0,) * n, array.ndim))
        for spec, array in zip(specs, arrays)
    ]
    out_specs = [pl.BlockSpec(o.shape, functools.partial(lambda n, i: (0,) * n, len(o.shape))) for o in outs]
    return pl.pallas_call(
        kernel,
        grid=(1,),
        in_specs=whole,
        out_specs=out_specs,
        out_shape=outs,
        compiler_params=pltpu.CompilerParams(vmem_limit_bytes=50 * 1024 * 1024),
    )(*arrays)


def passed_along(array, axis, by):
    length = lax.axis_size(axis)
    return lax.ppermute(array, axis, [(i, (i + by) % length) for i in range(length)])


def shape(*dims, dtype=BF16):
    return jax.ShapeDtypeStruct(dims, dtype)


def local(tokens, land_mask, keep_rows, land_embed, norm_gains, w_qkv, w_proj, rel_bias, cotangent):
    rows, cols = tokens.shape[0], tokens.shape[1]
    cells, count = rows * cols, cols // WIN_LON
    lon_size, lat_size = lax.axis_size("lon"), lax.axis_size("lat")
    scale_out = float(rows * lat_size * cols * lon_size) ** (-0.5)
    share = 2 * INNER // lon_size
    row_first = (lax.axis_index("lat") * rows).astype(jnp.int32).reshape(1)
    order, spread = window_matrices(cols)
    order, order_back, spread, spread_back = (fixed(m) for m in (order, order.T, spread, spread.T))
    reach = fixed(reach_matrix())
    cot_flat = cotangent.reshape(cells, D)
    rows_in, keep_in = ("scalars", row_first), ("scalars", keep_rows)

    stream, unit_one, inv_one, qkv_one, heads_one, probs_one, normed_two, strip = call(
        first_kernel,
        [
            shape(cells, D, dtype=F32), shape(cells, D, dtype=F32), shape(cells, 128, dtype=F32),
            shape(cells, 3 * INNER), shape(cells, INNER), shape(count, WIN, HEADS, QPAD, dtype=F32),
            shape(cells, D), shape(rows * HALF_LON, 2 * D),
        ],
        [
            rows_in, keep_in, tokens.reshape(cells, D), land_mask, land_embed, norm_gains, (0, w_qkv), (0, w_proj),
            (0, rel_bias), cot_flat, order, order_back, spread, reach, fixed(edge_matrix(cols, 1)),
        ],
    )

    landed = passed_along(strip, "lon", -1)
    inside = slice(HALF_LON, None)
    own_edge = jnp.concatenate(
        [normed_two.reshape(rows, cols, D)[:HALF_LAT, inside], cotangent[:HALF_LAT, inside]], axis=2
    )
    edge_rows = jnp.concatenate([own_edge, landed.reshape(rows, HALF_LON, 2 * D)[:HALF_LAT]], axis=1)
    arrived = passed_along(edge_rows, "lat", -1).reshape(HALF_LAT * cols, 2 * D)

    back, strip, proj_two = call(
        second_kernel,
        [shape(cells, 2 * D), shape(rows * HALF_LON, 2 * D), shape(INNER, D)],
        [
            rows_in, keep_in, normed_two, cot_flat, landed, arrived, (1, w_qkv), (1, w_proj), (1, rel_bias),
            order, order_back, spread, spread_back, reach, *(fixed(m) for m in roll_matrices(cols, 1)),
            fixed(edge_matrix(cols, -1)),
        ],
    )

    landed = passed_along(strip, "lon", 1)
    own_edge = back.reshape(rows, cols, 2 * D)[HALF_LAT:, : cols - HALF_LON]
    edge_rows = jnp.concatenate([landed.reshape(rows, HALF_LON, 2 * D)[HALF_LAT:], own_edge], axis=1)
    arrived = passed_along(edge_rows, "lat", 1).reshape(HALF_LAT * cols, 2 * D)

    output, grad_tokens, sums = call(
        third_kernel,
        [shape(cells, D, dtype=F32), shape(cells, D), shape(lon_size, share, D + 128)],
        [
            stream, unit_one, inv_one, qkv_one, heads_one, probs_one, cot_flat, back, landed, arrived, norm_gains,
            (0, w_qkv), (0, w_proj), proj_two, order, order_back, spread, spread_back,
            *(fixed(m) for m in roll_matrices(cols, -1)),
        ],
    )

    parts = lax.all_to_all(sums, "lon", 0, 0, tiled=True)
    (lon_sums,) = call(lon_sum_kernel, [shape(lat_size, share, D + 128)], [parts])
    parts = lax.all_to_all(lon_sums, "lat", 0, 0, tiled=True)
    proj, grad_gains = call(
        functools.partial(lat_sum_kernel, scale_out), [shape(lon_size, share, D), shape(2, D, dtype=F32)], [parts]
    )
    grad_proj = lax.all_to_all(proj, "lon", 0, 0, tiled=True).reshape(2, INNER, D)
    return output.reshape(rows, cols, D), grad_tokens.reshape(rows, cols, D), grad_proj, grad_gains


def solution(mesh):
    in_specs = (
        P("lat", "lon", None),
        P("lat", "lon"),
        P(),
        P(),
        P(),
        P(),
        P(),
        P(),
        P("lat", "lon", None),
    )
    out_specs = (P("lat", "lon", None), P("lat", "lon", None), P(), P())
    return jax.shard_map(local, mesh=mesh, in_specs=in_specs, out_specs=out_specs, check_vma=False)
```

time: 484 us -> 157 us (0.32)
  waiting for transfers between devices: 275 us -> 18.1 us
  blocking collectives: 99 us -> 69.9 us
  matrix products: 24.7 us -> 0 us
  Pallas kernels: 0 us -> 15.3 us
  between operations: 15 us -> 0.89 us
  other arithmetic: 10.6 us -> 0.08 us
  starting transfers between devices: 35 us -> 25.2 us
    psum x1 -> x0, waiting for transfers between devices: 264 us -> none  [local(): lax.psum((proj_one, proj_two, gain_one, gain_two), ('lon', 'lat'))]
    psum x1 -> x0, blocking collectives: 99 us -> none  [local(): lax.psum((proj_one, proj_two, gain_one, gain_two), ('lon', 'lat'))]
    all_to_all x0 -> x3, blocking collectives: none -> 69.9 us  [the longest x1 30.9 us: local(): parts = lax.all_to_all(sums, 'lon', 0, 0, tiled=True)]
    unnamed x46 -> x85, local copies, waits for them, and re-layouts: 2.38 us -> 26.2 us
    dot_general x22 -> x0, matrix products: 23 us -> none  [the longest x2 7.77 us: relative_table(): jnp.einsum('gnab,pqa,rsb->gnprqs', table, pick_lat, pick_lon, precision=l...]
    pallas_call x0 -> x5, Pallas kernels: none -> 15.3 us  [call(): pl.pallas_call(kernel, grid=(1,), in_specs=whole, out_specs=out_specs, ou...]
    ppermute x8 -> x4, starting transfers between devices: 35 us -> 25.2 us  [passed_along(): lax.ppermute(array, axis, [(i, (i + by) % length) for i in range(length)])]
    add x4 -> x0, local copies, waits for them, and re-layouts: 9.31 us -> none  [attend(): jnp.einsum('wqhd,wkhd->whqk', queries, keys_in, preferred_element_type=jn...]
  transfers between devices with their start and end apart: 9 -> 4, of which waited for: 4 -> 4; matrix products, arithmetic and copies ran while one was open for 3% -> 0% of each run, Pallas kernels for 0% -> 0%
where the time goes in v1:
time: 157 us; the launch traced here: 156 us
  blocking collectives  69.9 us (45%)
  local copies, waits for them, and re-layouts  26.3 us (17%)
  starting transfers between devices  25.2 us (16%)
  waiting for transfers between devices  18.1 us (12%)
  Pallas kernels  15.3 us (10%)
    all_to_all x1, blocking collectives, local(): parts = lax.all_to_all(sums, 'lon', 0, 0, tiled=True)  30.9 us
    unnamed x85, local copies, waits for them, and re-layouts  26.2 us
    ppermute x4, starting transfers between devices, passed_along(): lax.ppermute(array, axis, [(i, (i + by) % length) for i in range(length)])  25.2 us
    all_to_all x1, blocking collectives, local(): lax.all_to_all(proj, 'lon', 0, 0, tiled=True).reshape(2, INNER, D)  20.9 us
    all_to_all x1, blocking collectives, local(): parts = lax.all_to_all(lon_sums, 'lat', 0, 0, tiled=True)  18.1 us
    ppermute x4, waiting for transfers between devices, passed_along(): lax.ppermute(array, axis, [(i, (i + by) % length) for i in range(length)])  18.1 us
    pallas_call x5, Pallas kernels, call(): pl.pallas_call(kernel, grid=(1,), in_specs=whole, out_specs=out_specs, ou...  15.3 us
  transfers between devices with their start and end apart: 4, of which 4 were waited for; matrix products, arithmetic and copies ran while one was open for 0% of the time, Pallas kernels for 0%

profile of v1, /device:TPU:1, one launch (start us, length us, event | category | flops | bytes accessed | tf_op | source)
XLA Modules:
  0.0 155.7 jit_solution(7140608463283873179)
XLA Ops:
  0.6 1.1 copy-done
  1.7 1.0 copy-done.2
  2.7 0.9 copy-done.4
  3.7 1.0 copy-done.6
  4.7 0.9 copy-done.9
  5.6 0.9 copy-done.11
  6.5 0.9 copy-done.21
  7.4 0.7 copy-done.28
  8.1 0.7 copy-done.35
  8.8 0.7 copy-done.36
  9.5 0.7 copy-done.38
  10.2 0.7 copy-done.39
  10.9 0.7 copy-done.40
  11.6 3.6 %shard_map.237 = (f32[144,512]{1,0:T(8,128)S(1)}, f32[144,512]{1,0:T(8,128)S(1)}, f32[144,128]{1,0:T(8,128)S(1)}, bf16[144,768]{1,0:T(8,128)(2,1)S(1)}, bf16[144...) custom-call(s32[1]{0:T(128)} %bitcast.row_ref, ...), custom_call_target="tpu_custom_call" | custom-call | tf_op jit(solution)/shard_map/pallas_call | solution.py:348
  15.2 0.7 copy-done.13
  15.9 0.7 copy-done.15
  16.7 0.7 copy-done.17
  17.4 0.6 copy-done.25
  18.0 8.8 %collective-permute-start = (bf16[36,1024]{1,0:T(8,128)(2,1)S(1)}, bf16[36,1024]{1,0:T(8,128)(2,1)S(1)}, u32[]{:S(2)}, u32[]{:S(2)}) collective-permute-start(bf16[36,1024]{1,0:T(8,128)(2,1)S(1)} %get-tuple-element.27), channel_id=1, source_target_pairs={{0,496},{16,0},{32,16},{48,32},{64,48},{80,64},{96,80},{112,96},{1... | collective-permute-start | bytes 221192 | tf_op jit(solution)/shard_map/ppermute | solution.py:360
  26.8 0.8 collective-permute-done.landed_ref
  27.8 10.5 %collective-permute-start.1 = (bf16[3,24,1024]{2,1,0:T(8,128)(2,1)S(1)}, bf16[3,24,1024]{2,1,0:T(8,128)(2,1)S(1)}, u32[]{:S(2)}, u32[]{:S(2)}) collective-permute-start(bf16[3,24,1024]{2,1,0:T(8,128)(2,1)S(1)} %pad_maximum_fusion), channel_id=1, source_target_pairs={{0,15},{1,0},{2,1},{3,2},{4,3},{5,4},{6,5},{7,6},{8,7},{9,8},{10,9... | collective-permute-start | bytes 442376 | tf_op jit(solution)/shard_map/ppermute | solution.py:360
  38.2 2.1 %collective-permute-done.1 = bf16[3,24,1024]{2,1,0:T(8,128)(2,1)S(1)} collective-permute-done((bf16[3,24,1024]{2,1,0:T(8,128)(2,1)S(1)}, bf16[3,24,1024]{2,1,0:T(8,128)(2,1)S(1)}, u32[]{:S(2)}, u32[]{:S(2)}) %collective-permute-start.1) | collective-permute-done | bytes 147488 | tf_op jit(solution)/shard_map/ppermute | solution.py:360
  40.4 0.9 copy-done.20
  41.3 0.9 copy-done.27
  42.2 0.8 copy-done.30
  42.9 0.8 copy-done.31
  43.7 0.7 copy-done.34
  44.4 0.7 copy-done.41
  45.1 5.7 %shard_map.238 = (bf16[144,1024]{1,0:T(8,128)(2,1)S(1)}, bf16[36,1024]{1,0:T(8,128)(2,1)S(1)}, bf16[256,512]{1,0:T(8,128)(2,1)S(1)}) custom-call(s32[1]{0:T(128)} %bitcast.row_ref, s32[96]{0:T(128)S(1)} %copy-done.41, bf16[144,512]{1,0:T(8,128)(2,1)S(1)} %get-tuple-element.26.normed_ref, bf16[144,512]{1,0:T(8,128)(2,1)S(1)} %bitcast.11, ...), custom_call_target="tpu_custom_call" | custom-call | tf_op jit(solution)/shard_map/pallas_call | solution.py:348
  50.8 4.0 %collective-permute-start.2 = (bf16[36,1024]{1,0:T(8,128)(2,1)S(1)}, bf16[36,1024]{1,0:T(8,128)(2,1)S(1)}, u32[]{:S(2)}, u32[]{:S(2)}) collective-permute-start(bf16[36,1024]{1,0:T(8,128)(2,1)S(1)} %get-tuple-element.29), channel_id=1, source_target_pairs={{0,16},{16,32},{32,48},{48,64},{64,80},{80,96},{96,112},{112,128},... | collective-permute-start | bytes 221192 | tf_op jit(solution)/shard_map/ppermute | solution.py:360
  54.8 4.0 %collective-permute-done.2.landed_ref = bf16[36,1024]{1,0:T(8,128)(2,1)S(1)} collective-permute-done((bf16[36,1024]{1,0:T(8,128)(2,1)S(1)}, bf16[36,1024]{1,0:T(8,128)(2,1)S(1)}, u32[]{:S(2)}, u32[]{:S(2)}) %collective-permute-start.2) | collective-permute-done | bytes 73760 | tf_op jit(solution)/shard_map/ppermute | solution.py:360
  59.0 1.9 %collective-permute-start.3 = (bf16[3,24,1024]{2,1,0:T(8,128)(2,1)S(1)}, bf16[3,24,1024]{2,1,0:T(8,128)(2,1)S(1)}, u32[]{:S(2)}, u32[]{:S(2)}) collective-permute-start(bf16[3,24,1024]{2,1,0:T(8,128)(2,1)S(1)} %pad_maximum_fusion.1), channel_id=1, source_target_pairs={{0,1},{1,2},{2,3},{3,4},{4,5},{5,6},{6,7},{7,8},{8,9},{9,10},{10,1... | collective-permute-start | bytes 442376 | tf_op jit(solution)/shard_map/ppermute | solution.py:360
  60.9 11.1 %collective-permute-done.3 = bf16[3,24,1024]{2,1,0:T(8,128)(2,1)S(1)} collective-permute-done((bf16[3,24,1024]{2,1,0:T(8,128)(2,1)S(1)}, bf16[3,24,1024]{2,1,0:T(8,128)(2,1)S(1)}, u32[]{:S(2)}, u32[]{:S(2)}) %collective-permute-start.3) | collective-permute-done | bytes 147488 | tf_op jit(solution)/shard_map/ppermute | solution.py:360
  72.0 1.0 copy-done.14
  73.0 1.0 copy-done.16
  73.9 0.9 copy-done.18
  74.9 0.9 copy-done.22
  75.8 0.9 copy-done.24
  76.6 0.9 copy-done.26
  77.5 0.8 copy-done.32
  78.3 0.8 copy-done.33
  79.1 5.2 %shard_map.239 = (f32[144,512]{1,0:T(8,128)}, bf16[144,512]{1,0:T(8,128)(2,1)}, bf16[32,16,640]{2,1,0:T(8,128)(2,1)}) custom-call(f32[144,512]{1,0:T(8,128)S(1)} %copy-done.14, f32[144,512]{1,0:T(8,128)S(1)} %copy-done.16, f32[144,128]{1,0:T(8,128)S(1)} %copy-done.24, bf16[144,768]{1,0:T(8,128)(2,1)S(1)} %copy-done.18, bf16[144,256]{1,0:T(8,128)(2,1)S(1)} %copy-done.26, ...), custom_call_target="tpu_custom_call" | custom-call | tf_op jit(solution)/shard_map/pallas_call | solution.py:348
  84.3 30.9 %all_to_all.15.parts_ref = bf16[32,16,640]{2,1,0:T(8,128)(2,1)S(1)} all-to-all(bf16[32,16,640]{2,1,0:T(8,128)(2,1)} %get-tuple-element.33), channel_id=1, replica_groups=mesh['lon'=32,'lat'=16] {'lon'}, dimensions={0} | all-to-all | bytes 1310720 | tf_op jit(solution)/shard_map/all_to_all | solution.py:426
  115.2 0.1 shard_map.240
  115.3 18.1 %all_to_all.16.parts_ref = bf16[16,16,640]{2,1,0:T(8,128)(2,1)S(1)} all-to-all(bf16[16,16,640]{2,1,0:T(8,128)(2,1)S(1)} %shard_map.240), channel_id=1, replica_groups=mesh['lon'=32,'lat'=16] {'lat'}, dimensions={0} | all-to-all | bytes 655360 | tf_op jit(solution)/shard_map/all_to_all | solution.py:428
  133.4 0.6 shard_map.241
  134.0 20.9 %all_to_all.17 = bf16[32,16,512]{2,1,0:T(8,128)(2,1)S(1)} all-to-all(bf16[32,16,512]{2,1,0:T(8,128)(2,1)S(1)} %get-tuple-element.34), channel_id=1, replica_groups=mesh['lon'=32,'lat'=16] {'lon'}, dimensions={0} | all-to-all | bytes 1048576 | tf_op jit(solution)/shard_map/all_to_all | solution.py:432
  154.9 0.8 copy.27
  (62 shorter events, 0.3 us)
Async XLA Ops:
  0.6 1.1 copy-start
  1.7 1.0 copy-start.2
  2.7 0.9 copy-start.4
  3.7 1.0 copy-start.6
  4.7 0.9 copy-start.9
  5.6 0.9 copy-start.11
  6.5 0.9 copy-start.21
  7.4 0.7 copy-start.28
  8.1 0.7 copy-start.35
  8.8 0.7 copy-start.36
  9.5 0.7 copy-start.38
  10.2 0.7 copy-start.39
  10.9 0.7 copy-start.40
  11.5 28.8 %copy-start.1 = (bf16[1152,144]{1,0:T(8,128)(2,1)S(1)}, bf16[1152,144]{1,0:T(8,128)(2,1)}, u32[]{:S(2)}) copy-start(bf16[1152,144]{1,0:T(8,128)(2,1)} %constant.34.clone.spread_ref) | copy-start | bytes 995332
  11.5 28.8 %copy-start.3 = (bf16[2,256,512]{2,1,0:T(8,128)(2,1)S(1)}, bf16[2,256,512]{2,1,0:T(8,128)(2,1)}, u32[]{:S(2)}) copy-start(bf16[2,256,512]{2,1,0:T(8,128)(2,1)} %w_proj_ref.5) | copy-start | bytes 1572868
  11.5 28.8 %copy-start.5 = (bf16[6,24,512]{2,1,0:T(8,128)(2,1)S(1)}, bf16[6,24,512]{2,1,0:T(8,128)(2,1)}, u32[]{:S(2)}) copy-start(bf16[6,24,512]{2,1,0:T(8,128)(2,1)} %param.30) | copy-start | bytes 442372
  11.5 28.8 %copy-start.7 = (bf16[138,1536]{1,0:T(8,128)(2,1)S(1)}, bf16[138,1536]{1,0:T(8,128)(2,1)}, u32[]{:S(2)}) copy-start(bf16[138,1536]{1,0:T(8,128)(2,1)} %constant.36.clone.reach_ref) | copy-start | bytes 1271812
  11.5 28.8 %copy-start.8 = (bf16[144,1152]{1,0:T(8,128)(2,1)S(1)}, bf16[144,1152]{1,0:T(8,128)(2,1)}, u32[]{:S(2)}) copy-start(bf16[144,1152]{1,0:T(8,128)(2,1)} %constant.35.clone.spread_back_ref) | copy-start | bytes 995332
  11.6 28.8 %copy-start.10 = (bf16[256,144]{1,0:T(8,128)(2,1)S(1)}, bf16[256,144]{1,0:T(8,128)(2,1)}, u32[]{:S(2)}) copy-start(bf16[256,144]{1,0:T(8,128)(2,1)} %constant.32.clone.order_ref) | copy-start | bytes 221188
  11.6 28.8 %copy-start.12 = (bf16[144,256]{1,0:T(8,128)(2,1)S(1)}, bf16[144,256]{1,0:T(8,128)(2,1)}, u32[]{:S(2)}) copy-start(bf16[144,256]{1,0:T(8,128)(2,1)} %constant.33.clone.order_back_ref) | copy-start | bytes 221188
  11.6 28.8 %copy-start.29 = (f32[2,8,253]{2,1,0:T(8,128)S(1)}, f32[2,8,253]{2,1,0:T(8,128)}, u32[]{:S(2)}) copy-start(f32[2,8,253]{2,1,0:T(8,128)} %table_ref.3) | copy-start | bytes 48580
  15.2 0.7 copy-start.13
  15.9 0.7 copy-start.15
  16.7 0.7 copy-start.17
  17.4 0.6 copy-start.25
  18.0 9.7 %copy-start.23 = (f32[144,128]{1,0:T(8,128)}, f32[144,128]{1,0:T(8,128)S(1)}, u32[]{:S(2)}) copy-start(f32[144,128]{1,0:T(8,128)S(1)} %get-tuple-element.22.inv_one_ref) | copy-start | bytes 221188
  18.0 9.7 %collective-permute-start = (bf16[36,1024]{1,0:T(8,128)(2,1)S(1)}, bf16[36,1024]{1,0:T(8,128)(2,1)S(1)}, u32[]{:S(2)}, u32[]{:S(2)}) collective-permute-start(bf16[36,1024]{1,0:T(8,128)(2,1)S(1)} %get-tuple-element.27), channel_id=1, source_target_pairs={{0,496},{16,0},{32,16},{48,32},{64,48},{80,64},{96,80},{112,96},{1... | collective-permute-start | bytes 221192 | tf_op jit(solution)/shard_map/ppermute | solution.py:360
  27.7 12.6 %copy-start.19 = (bf16[36,1024]{1,0:T(8,128)(2,1)}, bf16[36,1024]{1,0:T(8,128)(2,1)S(1)}, u32[]{:S(2)}) copy-start(bf16[36,1024]{1,0:T(8,128)(2,1)S(1)} %collective-permute-done.landed_ref) | copy-start | bytes 221188
  27.8 12.6 %collective-permute-start.1 = (bf16[3,24,1024]{2,1,0:T(8,128)(2,1)S(1)}, bf16[3,24,1024]{2,1,0:T(8,128)(2,1)S(1)}, u32[]{:S(2)}, u32[]{:S(2)}) collective-permute-start(bf16[3,24,1024]{2,1,0:T(8,128)(2,1)S(1)} %pad_maximum_fusion), channel_id=1, source_target_pairs={{0,15},{1,0},{2,1},{3,2},{4,3},{5,4},{6,5},{7,6},{8,7},{9,8},{10,9... | collective-permute-start | bytes 442376 | tf_op jit(solution)/shard_map/ppermute | solution.py:360
  40.4 0.9 copy-start.20
  41.3 0.9 copy-start.27
  42.2 0.8 copy-start.30
  42.9 0.8 copy-start.31
  43.7 0.7 copy-start.34
  44.4 0.7 copy-start.41
  45.1 26.9 %copy-start.37 = (f32[2,512]{1,0:T(2,128)S(1)}, f32[2,512]{1,0:T(2,128)}, u32[]{:S(2)}) copy-start(f32[2,512]{1,0:T(2,128)} %gains_ref.3) | copy-start | bytes 12292
  50.8 8.1 %collective-permute-start.2 = (bf16[36,1024]{1,0:T(8,128)(2,1)S(1)}, bf16[36,1024]{1,0:T(8,128)(2,1)S(1)}, u32[]{:S(2)}, u32[]{:S(2)}) collective-permute-start(bf16[36,1024]{1,0:T(8,128)(2,1)S(1)} %get-tuple-element.29), channel_id=1, source_target_pairs={{0,16},{16,32},{32,48},{48,64},{64,80},{80,96},{96,112},{112,128},... | collective-permute-start | bytes 221192 | tf_op jit(solution)/shard_map/ppermute | solution.py:360
  59.0 13.0 %collective-permute-start.3 = (bf16[3,24,1024]{2,1,0:T(8,128)(2,1)S(1)}, bf16[3,24,1024]{2,1,0:T(8,128)(2,1)S(1)}, u32[]{:S(2)}, u32[]{:S(2)}) collective-permute-start(bf16[3,24,1024]{2,1,0:T(8,128)(2,1)S(1)} %pad_maximum_fusion.1), channel_id=1, source_target_pairs={{0,1},{1,2},{2,3},{3,4},{4,5},{5,6},{6,7},{7,8},{8,9},{9,10},{10,1... | collective-permute-start | bytes 442376 | tf_op jit(solution)/shard_map/ppermute | solution.py:360
  72.0 1.0 copy-start.14
  73.0 1.0 copy-start.16
  73.9 0.9 copy-start.18
  74.9 0.9 copy-start.22
  75.8 0.9 copy-start.24
  76.6 0.9 copy-start.26
  77.5 0.8 copy-start.32
  78.3 0.8 copy-start.33

commit v2 on v1

v2 whole, which is shorter than its diff:
```python
import functools

import jax
import jax.numpy as jnp
import numpy as np
from jax import lax
from jax.experimental import pallas as pl
from jax.experimental.pallas import tpu as pltpu
from jax.sharding import Mesh
from jax.sharding import PartitionSpec as P

D = 512
HEAD_DIM = 32
HEADS = 8
INNER = HEADS * HEAD_DIM
WIN_LAT = 6
WIN_LON = 12
HALF_LAT = WIN_LAT // 2
HALF_LON = WIN_LON // 2
WIN = WIN_LAT * WIN_LON
SPAN_LON = 2 * WIN_LON - 1
REACH = WIN_LAT * SPAN_LON
QPAD = 128
STACK = WIN * HEADS
GAIN_ROWS = 8

NORM_EPS = 1e-05
SCALE = HEAD_DIM ** (-0.5)
SHUT = -1e30

F32 = jnp.float32
BF16 = jnp.bfloat16


def dot_nn(left, right):
    return lax.dot_general(left, right, (((1,), (0,)), ((), ())), preferred_element_type=F32)


def dot_nt(left, right):
    return lax.dot_general(left, right, (((1,), (1,)), ((), ())), preferred_element_type=F32)


def dot_tn(left, right):
    return lax.dot_general(left, right, (((0,), (0,)), ((), ())), preferred_element_type=F32)


def window_matrices(cols):
    cells, count = WIN_LAT * cols, cols // WIN_LON
    order = np.zeros((count, QPAD, cells), np.float32)
    spread = np.zeros((count, WIN, HEADS, cells), np.float32)
    for w in range(count):
        for a in range(WIN_LAT):
            for e in range(WIN_LON):
                cell = a * cols + w * WIN_LON + e
                order[w, e * WIN_LAT + a, cell] = 1
                spread[w, e * WIN_LAT + a, :, cell] = 1
    return order.reshape(-1, cells), spread.reshape(-1, cells)


def reach_matrix():
    reach = np.zeros((REACH, WIN_LON, QPAD), np.float32)
    for e2 in range(WIN_LON):
        for a in range(WIN_LAT):
            for e in range(WIN_LON):
                reach[a * SPAN_LON + e - e2 + WIN_LON - 1, e2, e * WIN_LAT + a] = 1
    return reach.reshape(REACH, -1)


def roll_matrices(cols, direction):
    cells = WIN_LAT * cols
    own = np.zeros((cells, cells), np.float32)
    side = np.zeros((cells, WIN_LAT * HALF_LON), np.float32)
    far = np.zeros((cells, HALF_LAT * cols), np.float32)
    for i in range(WIN_LAT):
        for j in range(cols):
            row = i * cols + j
            from_i, from_j = i + direction * HALF_LAT, j + direction * HALF_LON
            if not 0 <= from_i < WIN_LAT:
                far[row, (from_i % WIN_LAT - (0 if direction > 0 else HALF_LAT)) * cols + j] = 1
            elif not 0 <= from_j < cols:
                side[row, from_i * HALF_LON + (from_j - cols if direction > 0 else from_j + HALF_LON)] = 1
            else:
                own[row, from_i * cols + from_j] = 1
    return own, side, far


def edge_matrix(cols, direction):
    edge = np.zeros((WIN_LAT, HALF_LON, WIN_LAT * cols), np.float32)
    for i in range(WIN_LAT):
        for j in range(HALF_LON):
            edge[i, j, i * cols + (j if direction > 0 else cols - HALF_LON + j)] = 1
    return edge.reshape(-1, WIN_LAT * cols)


def fixed(matrix):
    return jnp.asarray(matrix, BF16)


def norm_stats(values):
    row_mean = jnp.sum(values, axis=-1, keepdims=True) * (1.0 / D)
    centred = values - row_mean
    row_var = jnp.sum(centred * centred, axis=-1, keepdims=True) * (1.0 / D)
    inv_std = lax.rsqrt(row_var + NORM_EPS)
    return centred * inv_std, inv_std


def norm_back(d_float, unit_rows, inv_std, gain_row):
    d_unit = d_float * gain_row
    mean_grad = jnp.sum(d_unit, axis=-1, keepdims=True) * (1.0 / D)
    mean_proj = jnp.sum(d_unit * unit_rows, axis=-1, keepdims=True) * (1.0 / D)
    d_input = inv_std * (d_unit - mean_grad - unit_rows * mean_proj)
    return d_input, jnp.sum(d_float * unit_rows, axis=0, keepdims=True)


def masked_bias(table, reach, keep_of, split_rows):
    shifted = jnp.concatenate(
        [
            table[:, (WIN_LAT - 1 - a2) * SPAN_LON : (WIN_LAT - 1 - a2) * SPAN_LON + REACH]
            for a2 in range(WIN_LAT)
        ],
        axis=0,
    )
    high = shifted.astype(BF16)
    rest = shifted - high.astype(F32)
    middle = rest.astype(BF16)
    low = (rest - middle.astype(F32)).astype(BF16)
    spread = dot_nn(high, reach) + (dot_nn(middle, reach) + dot_nn(low, reach))
    place = lax.broadcasted_iota(jnp.int32, (HEADS, QPAD), 1)
    query_late = jnp.where(place % WIN_LAT >= HALF_LAT, 1, 0)
    tiles = []
    for a2 in range(WIN_LAT):
        key_late = 1 if a2 >= HALF_LAT else 0
        apart = jnp.where(query_late == key_late, 0, 1) * split_rows
        shut = apart + jnp.where(keep_of(a2) == 1, 0, 1)
        tiles.append(jnp.where(shut > 0, SHUT, 0.0).astype(F32))
    tile = jnp.concatenate(tiles, axis=0)
    blocks = [spread[:, QPAD * e2 : QPAD * (e2 + 1)] + tile for e2 in range(WIN_LON)]
    return jnp.concatenate(blocks, axis=0).reshape(WIN, HEADS, QPAD)


def lay_out(qkv, order, spread):
    count = order.shape[0] // QPAD
    queries = dot_nn(order, qkv[:, :INNER]).astype(BF16)
    stacked = dot_nn(spread, qkv[:, INNER:])
    head = lax.broadcasted_iota(jnp.int32, (HEADS, 2 * INNER), 0)
    lane = lax.broadcasted_iota(jnp.int32, (HEADS, 2 * INNER), 1)
    own = jnp.where((lane // HEAD_DIM) % HEADS == head, 1.0, 0.0).astype(F32)
    stacked = stacked.reshape(count * WIN, HEADS, 2 * INNER) * own[None]
    stacked = stacked.reshape(count * STACK, 2 * INNER).astype(BF16)
    return queries, stacked[:, :INNER], stacked[:, INNER:], own


def attend(queries, keys, values, bias, order_back):
    count = queries.shape[0] // QPAD
    all_probs, outs = [], []
    for w in range(count):
        rows = slice(w * STACK, (w + 1) * STACK)
        scores = dot_nt(keys[rows], queries[w * QPAD : (w + 1) * QPAD])
        scores = scores.reshape(WIN, HEADS, QPAD) * SCALE + bias
        exp_scores = jnp.exp(scores - jnp.max(scores, axis=0, keepdims=True))
        probs = exp_scores * (1.0 / jnp.sum(exp_scores, axis=0, keepdims=True))
        all_probs.append(probs)
        low = probs.reshape(STACK, QPAD).astype(BF16)
        outs.append(dot_tn(low, values[rows]).astype(BF16))
    heads = dot_nn(order_back, jnp.concatenate(outs, axis=0)).astype(BF16)
    return heads, all_probs


def attend_back(d_heads, all_probs, queries, keys, values, own, order, order_back, spread_back):
    d_out = dot_nn(order, d_heads).astype(BF16)
    d_queries, d_stack = [], []
    for w, probs in enumerate(all_probs):
        rows = slice(w * STACK, (w + 1) * STACK)
        here = slice(w * QPAD, (w + 1) * QPAD)
        d_probs = dot_nt(values[rows], d_out[here]).reshape(WIN, HEADS, QPAD)
        total = jnp.sum(d_probs * probs, axis=0, keepdims=True)
        d_low = (probs * (d_probs - total) * SCALE).reshape(STACK, QPAD).astype(BF16)
        low = probs.reshape(STACK, QPAD).astype(BF16)
        d_queries.append(dot_tn(d_low, keys[rows]).astype(BF16))
        d_keys = dot_nn(d_low, queries[here])
        d_values = dot_nn(low, d_out[here])
        both = jnp.concatenate([d_keys, d_values], axis=1).reshape(WIN, HEADS, 2 * INNER) * own[None]
        d_stack.append(both.reshape(STACK, 2 * INNER).astype(BF16))
    d_query_grid = dot_nn(order_back, jnp.concatenate(d_queries, axis=0)).astype(BF16)
    d_rest = dot_nn(spread_back, jnp.concatenate(d_stack, axis=0)).astype(BF16)
    return jnp.concatenate([d_query_grid, d_rest], axis=1)


def first_kernel(
    row_ref, keep_ref, tokens_ref, mask_ref, embed_ref, gains_ref, w_qkv_ref, w_proj_ref, table_ref, cot_ref,
    order_ref, order_back_ref, spread_ref, reach_ref, edge_ref,
    wide_ref, saved_ref, probs_ref, rolling_ref, strip_ref,
):
    rows, cols = mask_ref.shape
    mask = mask_ref[...].astype(F32)
    spread_mask = jnp.concatenate([jnp.broadcast_to(mask[r : r + 1], (cols, cols)) for r in range(rows)], axis=0)
    cell = lax.broadcasted_iota(jnp.int32, (rows * cols, cols), 0)
    lane = lax.broadcasted_iota(jnp.int32, (rows * cols, cols), 1)
    land = jnp.sum(jnp.where(cell % cols == lane, spread_mask, 0.0), axis=1, keepdims=True)
    embedded = tokens_ref[...].astype(F32) + jnp.where(land == 1.0, embed_ref[1:2], embed_ref[0:1])
    wide_ref[:, :D] = embedded
    unit_one, _ = norm_stats(embedded)
    normed_one = (unit_one * gains_ref[0:1]).astype(BF16)
    qkv = dot_nn(normed_one, w_qkv_ref[0]).astype(BF16)
    saved_ref[:, : 3 * INNER] = qkv
    bias = masked_bias(table_ref[0], reach_ref[...], lambda a2: keep_ref[row_ref[0] + a2], 0)
    queries, keys, values, own = lay_out(qkv, order_ref[...], spread_ref[...])
    heads, all_probs = attend(queries, keys, values, bias, order_back_ref[...])
    for w, probs in enumerate(all_probs):
        probs_ref[w] = probs
    saved_ref[:, 3 * INNER :] = heads
    branch = dot_nn(heads, w_proj_ref[0]).astype(BF16)
    stream = embedded + branch.astype(F32)
    wide_ref[:, D:] = stream
    unit_two, _ = norm_stats(stream)
    normed_two = (unit_two * gains_ref[1:2]).astype(BF16)
    d_heads_two = dot_nt(cot_ref[...], w_proj_ref[1]).astype(BF16)
    rolling = jnp.concatenate([normed_two, d_heads_two], axis=1)
    rolling_ref[...] = rolling
    strip_ref[...] = dot_nn(edge_ref[...], rolling).astype(BF16)


def second_kernel(
    row_ref, keep_ref, rolling_ref, landed_ref, arrived_ref, w_qkv_ref, table_ref,
    order_ref, order_back_ref, spread_ref, spread_back_ref, reach_ref, own_ref, side_ref, far_ref, edge_ref,
    back_ref, strip_ref,
):
    lat_count = keep_ref.shape[0]
    rolled = (
        dot_nn(own_ref[...], rolling_ref[...])
        + dot_nn(side_ref[...], landed_ref[...])
        + dot_nn(far_ref[...], arrived_ref[...])
    ).astype(BF16)
    normed, d_heads = rolled[:, :D], rolled[:, D:]
    last_band = jnp.where(row_ref[0] + WIN_LAT >= lat_count, 1, 0)

    def keep_of(a2):
        place = row_ref[0] + (a2 + HALF_LAT)
        return keep_ref[jnp.where(place >= lat_count, place - lat_count, place)]

    bias = masked_bias(table_ref[0], reach_ref[...], keep_of, last_band)
    order, order_back = order_ref[...], order_back_ref[...]
    qkv = dot_nn(normed, w_qkv_ref[0]).astype(BF16)
    queries, keys, values, own = lay_out(qkv, order, spread_ref[...])
    heads, all_probs = attend(queries, keys, values, bias, order_back)
    d_qkv = attend_back(d_heads, all_probs, queries, keys, values, own, order, order_back, spread_back_ref[...])
    d_normed = dot_nt(d_qkv, w_qkv_ref[0]).astype(BF16)
    both = jnp.concatenate([d_normed, heads], axis=1)
    back_ref[...] = both
    strip_ref[...] = dot_nn(edge_ref[...], both).astype(BF16)


def third_kernel(
    core_ref, wide_ref, saved_ref, probs_ref, cot_ref, back_ref, landed_ref, arrived_ref, gains_ref, w_qkv_ref, w_proj_ref,
    order_ref, order_back_ref, spread_ref, spread_back_ref, own_ref, side_ref, far_ref,
    output_ref, grad_ref, kept_ref, sent_ref,
):
    unrolled = (
        dot_nn(own_ref[...], back_ref[...])
        + dot_nn(side_ref[...], landed_ref[...])
        + dot_nn(far_ref[...], arrived_ref[...])
    )
    stream = wide_ref[:, D:]
    unit_two, inv_two = norm_stats(stream)
    d_branch, gain_two = norm_back(unrolled[:, :D], unit_two, inv_two, gains_ref[1:2])
    cotangent = cot_ref[...]
    d_stream = (cotangent.astype(F32) + d_branch).astype(BF16)
    qkv, heads_one = saved_ref[:, : 3 * INNER], saved_ref[:, 3 * INNER :]
    heads_two = unrolled[:, D:].astype(BF16)
    branch_two = dot_nn(heads_two, w_proj_ref[1]).astype(BF16)
    output_ref[...] = stream + branch_two.astype(F32)
    proj_one = dot_tn(heads_one, d_stream)
    proj_two = dot_tn(heads_two, cotangent)
    upper = core_ref[0] == 1
    kept_ref[:INNER] = jnp.where(upper, proj_two, proj_one).astype(BF16)
    sent_ref[:INNER] = jnp.where(upper, proj_one, proj_two).astype(BF16)
    d_heads = dot_nt(d_stream, w_proj_ref[0]).astype(BF16)
    order = order_ref[...]
    queries, keys, values, own = lay_out(qkv, order, spread_ref[...])
    all_probs = [probs_ref[w] for w in range(probs_ref.shape[0])]
    d_qkv = attend_back(
        d_heads, all_probs, queries, keys, values, own, order, order_back_ref[...], spread_back_ref[...]
    )
    d_normed = dot_nt(d_qkv, w_qkv_ref[0]).astype(BF16)
    unit_one, inv_one = norm_stats(wide_ref[:, :D])
    d_branch, gain_one = norm_back(d_normed.astype(F32), unit_one, inv_one, gains_ref[0:1])
    grad_ref[...] = (d_stream.astype(F32) + d_branch).astype(BF16)
    gain = jnp.concatenate(
        [row[:, 128 * j : 128 * (j + 1)] for row in (gain_one, gain_two) for j in range(D // 128)], axis=0
    )
    pair = jnp.concatenate([gain_pair(gain), jnp.zeros((2 * GAIN_ROWS, D - 128), BF16)], axis=1)
    kept_ref[INNER:] = pair
    sent_ref[INNER:] = pair


def gain_pair(gain):
    high = gain.astype(BF16).astype(F32)
    return jnp.concatenate([high, gain - high], axis=0).astype(BF16)


def pair_sum(pair):
    return pair[:GAIN_ROWS] + pair[GAIN_ROWS : 2 * GAIN_ROWS]


def core_sum_kernel(kept_ref, landed_ref, out_ref):
    total = kept_ref[...].astype(F32) + landed_ref[...].astype(F32)
    low = total[:INNER].astype(BF16)
    pair = gain_pair(pair_sum(total[INNER:, :128]))
    pieces, tall = out_ref.shape[0], out_ref.shape[1]
    for s in range(pieces):
        row, col = tall * (s // 2), D // 2 * (s % 2)
        out_ref[s, :, : D // 2] = low[row : row + tall, col : col + D // 2]
        out_ref[s, : 2 * GAIN_ROWS, D // 2 :] = pair
        if tall > 2 * GAIN_ROWS:
            out_ref[s, 2 * GAIN_ROWS :, D // 2 :] = jnp.zeros((tall - 2 * GAIN_ROWS, 128), BF16)


def added(parts_ref):
    total = parts_ref[0].astype(F32)
    for s in range(1, parts_ref.shape[0]):
        total = total + parts_ref[s].astype(F32)
    return total[:, : D // 2], pair_sum(total[:, D // 2 :])


def plane_sum_kernel(parts_ref, out_ref):
    proj, gain = added(parts_ref)
    low, pair = proj.astype(BF16), gain_pair(gain)
    tall = out_ref.shape[1]
    for s in range(out_ref.shape[0]):
        out_ref[s, :, : D // 2] = low
        out_ref[s, : 2 * GAIN_ROWS, D // 2 :] = pair
        if tall > 2 * GAIN_ROWS:
            out_ref[s, 2 * GAIN_ROWS :, D // 2 :] = jnp.zeros((tall - 2 * GAIN_ROWS, 128), BF16)


def depth_sum_kernel(scale, parts_ref, proj_ref, gains_ref):
    proj, gain = added(parts_ref)
    low = (proj * scale).astype(BF16)
    for s in range(proj_ref.shape[0]):
        proj_ref[s] = low
    gain = gain * scale
    per_row = D // 128
    for r in range(GAIN_ROWS):
        gains_ref[r // per_row : r // per_row + 1, 128 * (r % per_row) : 128 * (r % per_row + 1)] = gain[r : r + 1]


def join_kernel(core_ref, mine_ref, other_ref, out_ref):
    pieces, tall = mine_ref.shape[0], mine_ref.shape[1]
    upper = core_ref[0] == 1
    for s in range(pieces):
        row, col = tall * (s // 2), D // 2 * (s % 2)
        mine, other = mine_ref[s], other_ref[s]
        out_ref[0, row : row + tall, col : col + D // 2] = jnp.where(upper, other, mine)
        out_ref[1, row : row + tall, col : col + D // 2] = jnp.where(upper, mine, other)


def scalars(array):
    return array, pl.BlockSpec(memory_space=pltpu.SMEM)


def whole(array):
    return array, pl.BlockSpec(array.shape, functools.partial(lambda n, i: (0,) * n, array.ndim))


def in_hbm(array):
    return whole(pltpu.with_memory_space_constraint(array, pltpu.HBM))


def layer(array, index):
    spec = pl.BlockSpec((1,) + array.shape[1:], lambda i: (index,) + (0,) * (array.ndim - 1))
    return pltpu.with_memory_space_constraint(array, pltpu.HBM), spec


def hbm(*dims, dtype=BF16):
    return pltpu.HBM(dims, dtype)


def either(*dims, dtype=BF16):
    return jax.ShapeDtypeStruct(dims, dtype)


def call(kernel, outs, operands):
    arrays, specs = zip(*operands)
    out_specs = [pl.BlockSpec(o.shape, functools.partial(lambda n, i: (0,) * n, len(o.shape))) for o in outs]
    return pl.pallas_call(
        kernel,
        grid=(1,),
        in_specs=specs,
        out_specs=out_specs,
        out_shape=outs,
        compiler_params=pltpu.CompilerParams(vmem_limit_bytes=50 * 1024 * 1024),
    )(*arrays)


LON = ("z_lo", "x", "core")
LAT = ("z_hi", "y")
PLANE = ("x", "y")
DEPTH = ("z_lo", "z_hi")


def passed_along(array, axes, by):
    length = lax.axis_size(axes)
    return lax.ppermute(array, axes, [(i, (i + by) % length) for i in range(length)])


def local(tokens, land_mask, keep_rows, land_embed, norm_gains, w_qkv, w_proj, rel_bias, cotangent):
    rows, cols = tokens.shape[0], tokens.shape[1]
    cells, count = rows * cols, cols // WIN_LON
    half, wide = rows * HALF_LON, D + INNER
    scale_out = float(rows * lax.axis_size(LAT) * cols * lax.axis_size(LON)) ** (-0.5)
    row_first = scalars((lax.axis_index(LAT) * rows).astype(jnp.int32).reshape(1))
    core = scalars(lax.axis_index("core").astype(jnp.int32).reshape(1))
    keep_in = scalars(keep_rows)
    order, spread = window_matrices(cols)
    order, order_back, spread, spread_back = (in_hbm(fixed(m)) for m in (order, order.T, spread, spread.T))
    reach = in_hbm(fixed(reach_matrix()))
    cot_flat = in_hbm(cotangent.reshape(cells, D))

    wide_one, saved, probs, rolling, strip = call(
        first_kernel,
        [
            hbm(cells, 2 * D, dtype=F32), hbm(cells, 4 * INNER), hbm(count, WIN, HEADS, QPAD, dtype=F32),
            either(cells, wide), either(half, wide),
        ],
        [
            row_first, keep_in, in_hbm(tokens.reshape(cells, D)), in_hbm(land_mask), in_hbm(land_embed),
            in_hbm(norm_gains), layer(w_qkv, 0), in_hbm(w_proj), layer(rel_bias, 0), cot_flat,
            order, order_back, spread, reach, in_hbm(fixed(edge_matrix(cols, 1))),
        ],
    )

    landed = passed_along(strip, LON, -1)
    own_edge = rolling.reshape(rows, cols, wide)[:HALF_LAT, HALF_LON:]
    edge_rows = jnp.concatenate([own_edge, landed.reshape(rows, HALF_LON, wide)[:HALF_LAT]], axis=1)
    arrived = passed_along(edge_rows, LAT, -1).reshape(HALF_LAT * cols, wide)

    back, strip = call(
        second_kernel,
        [either(cells, wide), either(half, wide)],
        [
            row_first, keep_in, whole(rolling), whole(landed), whole(arrived), layer(w_qkv, 1), layer(rel_bias, 1),
            order, order_back, spread, spread_back, reach, *(in_hbm(fixed(m)) for m in roll_matrices(cols, 1)),
            in_hbm(fixed(edge_matrix(cols, -1))),
        ],
    )

    landed = passed_along(strip, LON, 1)
    own_edge = back.reshape(rows, cols, wide)[HALF_LAT:, : cols - HALF_LON]
    edge_rows = jnp.concatenate([landed.reshape(rows, HALF_LON, wide)[HALF_LAT:], own_edge], axis=1)
    arrived = passed_along(edge_rows, LAT, 1).reshape(HALF_LAT * cols, wide)

    output, grad_tokens, kept, sent = call(
        third_kernel,
        [hbm(cells, D, dtype=F32), hbm(cells, D), either(INNER + 2 * GAIN_ROWS, D), either(INNER + 2 * GAIN_ROWS, D)],
        [
            core, in_hbm(wide_one), in_hbm(saved), in_hbm(probs), cot_flat, whole(back), whole(landed), whole(arrived),
            in_hbm(norm_gains), layer(w_qkv, 0), in_hbm(w_proj), order, order_back, spread, spread_back,
            *(in_hbm(fixed(m)) for m in roll_matrices(cols, -1)),
        ],
    )

    planes, depths, cores = lax.axis_size(PLANE), lax.axis_size(DEPTH), lax.axis_size("core")
    tall = 2 * INNER // planes
    swap = [(i, (i + 1) % cores) for i in range(cores)]
    landed = lax.ppermute(sent, "core", swap)
    (pieces,) = call(core_sum_kernel, [either(planes, tall, D // 2 + 128)], [whole(kept), whole(landed)])
    parts = lax.all_to_all(pieces, PLANE, 0, 0, tiled=True)
    (pieces,) = call(plane_sum_kernel, [either(depths, tall, D // 2 + 128)], [whole(parts)])
    parts = lax.all_to_all(pieces, DEPTH, 0, 0, tiled=True)
    pieces, grad_gains = call(
        functools.partial(depth_sum_kernel, scale_out),
        [either(planes, tall, D // 2), either(2, D, dtype=F32)],
        [whole(parts)],
    )
    mine = lax.all_to_all(pieces, PLANE, 0, 0, tiled=True)
    other = lax.ppermute(mine, "core", swap)
    (grad_proj,) = call(join_kernel, [either(2, INNER, D)], [core, whole(mine), whole(other)])
    return output.reshape(rows, cols, D), grad_tokens.reshape(rows, cols, D), grad_proj, grad_gains


def chip_axes(lon, lat):
    x = min(4, lon // 2)
    y = min(8, lat)
    return (lon // (2 * x), x, 2, lat // y, y)


def solution(mesh):
    sizes = chip_axes(mesh.shape["lon"], mesh.shape["lat"])
    fine = Mesh(mesh.devices.reshape(sizes), LON + LAT)
    grid = P(LAT, LON, None)
    in_specs = (grid, P(LAT, LON), P(), P(), P(), P(), P(), P(), grid)
    out_specs = (grid, grid, P(), P())
    return jax.shard_map(local, mesh=fine, in_specs=in_specs, out_specs=out_specs, check_vma=False)
```

time: 157 us -> 119 us (0.76)
  blocking collectives: 69.9 us -> 41 us
  local copies, waits for them, and re-layouts: 26.3 us -> 0.74 us
  starting transfers between devices: 25.2 us -> 39.6 us
  Pallas kernels: 15.3 us -> 17.3 us
    all_to_all x3, blocking collectives: 69.9 us -> 41 us  [the longest x1 16.7 us: local(): mine = lax.all_to_all(pieces, PLANE, 0, 0, tiled=True)]
    unnamed x85 -> x4, local copies, waits for them, and re-layouts: 26.2 us -> 0.65 us
    ppermute x4 -> x6, starting transfers between devices: 25.2 us -> 39.6 us  [the longest x4 24.2 us: passed_along(): lax.ppermute(array, axes, [(i, (i + by) % length) for i in range(length)])]
    pallas_call x5 -> x7, Pallas kernels: 15.3 us -> 17.3 us  [call(): pl.pallas_call(kernel, grid=(1,), in_specs=specs, out_specs=out_specs, ou...]
    ppermute x4 -> x6, waiting for transfers between devices: 18.1 us -> 19.3 us  [the longest x4 17 us: passed_along(): lax.ppermute(array, axes, [(i, (i + by) % length) for i in range(length)])]
  transfers between devices with their start and end apart: 4 -> 6, of which waited for: 4 -> 6; matrix products, arithmetic and copies ran while one was open for 0% -> 0% of each run, Pallas kernels for 0% -> 0%
where the time goes in v2:
time: 119 us
  blocking collectives  41 us (34%)
  starting transfers between devices  39.6 us (33%)
  waiting for transfers between devices  19.3 us (16%)
  Pallas kernels  17.3 us (15%)
    ppermute x4, starting transfers between devices, passed_along(): lax.ppermute(array, axes, [(i, (i + by) % length) for i in range(length)])  24.2 us
    pallas_call x7, Pallas kernels, call(): pl.pallas_call(kernel, grid=(1,), in_specs=specs, out_specs=out_specs, ou...  17.3 us
    ppermute x4, waiting for transfers between devices, passed_along(): lax.ppermute(array, axes, [(i, (i + by) % length) for i in range(length)])  17 us
    all_to_all x1, blocking collectives, local(): mine = lax.all_to_all(pieces, PLANE, 0, 0, tiled=True)  16.7 us
    all_to_all x1, blocking collectives, local(): parts = lax.all_to_all(pieces, PLANE, 0, 0, tiled=True)  15.3 us
    ppermute x1, starting transfers between devices, local(): landed = lax.ppermute(sent, 'core', swap)  9.56 us
    all_to_all x1, blocking collectives, local(): parts = lax.all_to_all(pieces, DEPTH, 0, 0, tiled=True)  9.04 us
    ppermute x1, starting transfers between devices, local(): other = lax.ppermute(mine, 'core', swap)  5.88 us
  transfers between devices with their start and end apart: 6, of which 6 were waited for; matrix products, arithmetic and copies ran while one was open for 0% of the time, Pallas kernels for 0%

profile of v2, /device:TPU:1, one launch (start us, length us, event | category | flops | bytes accessed | tf_op | source)
XLA Modules:
  0.0 118.9 jit_solution(15760710455307349517)
XLA Ops:
  0.6 0.0 copy-start
  0.6 0.6 copy-done
  1.3 0.0 copy-start.1
  1.3 4.9 %shard_map.237 = (f32[144,1024]{1,0:T(8,128)}, bf16[144,1024]{1,0:T(8,128)(2,1)}, f32[2,72,8,128]{3,2,1,0:T(8,128)}, bf16[144,768]{1,0:T(8,128)(2,1)S(1)}, bf16[36,768]{1,0:T(8,128)(2,1)S(1)}) custom-call(s32[1]{0:T(128)} %bitcast.1.row_ref, s32[96]{0:T(128)S(1)} %copy-done, bf16[144,512]{1,0:T(8,128)(2,1)} %bitcast.16, s32[6,24]{1,0:T(8,128)} %mask_ref.1, ...), custom_call_target="tpu_custom_call" | custom-call | tf_op jit(solution)/shard_map/pallas_call | solution.py:385
  6.2 8.8 %collective-permute-start = (bf16[36,768]{1,0:T(8,128)(2,1)S(1)}, bf16[36,768]{1,0:T(8,128)(2,1)S(1)}, u32[]{:S(2)}, u32[]{:S(2)}) collective-permute-start(bf16[36,768]{1,0:T(8,128)(2,1)S(1)} %get-tuple-element.21), channel_id=1, source_target_pairs={{0,496},{16,0},{32,16},{48,32},{64,48},{80,64},{96,80},{112,96},{1... | collective-permute-start | bytes 165896 | tf_op jit(solution)/shard_map/ppermute | solution.py:403
  15.0 0.8 collective-permute-done.landed_ref
  15.9 10.3 %collective-permute-start.1 = (bf16[3,24,768]{2,1,0:T(8,128)(2,1)S(1)}, bf16[3,24,768]{2,1,0:T(8,128)(2,1)S(1)}, u32[]{:S(2)}, u32[]{:S(2)}) collective-permute-start(bf16[3,24,768]{2,1,0:T(8,128)(2,1)S(1)} %pad_maximum_fusion), channel_id=1, source_target_pairs={{0,15},{1,0},{2,1},{3,2},{4,3},{5,4},{6,5},{7,6},{8,7},{9,8},{10,9... | collective-permute-start | bytes 331784 | tf_op jit(solution)/shard_map/ppermute | solution.py:403
  26.2 1.7 %collective-permute-done.1 = bf16[3,24,768]{2,1,0:T(8,128)(2,1)S(1)} collective-permute-done((bf16[3,24,768]{2,1,0:T(8,128)(2,1)S(1)}, bf16[3,24,768]{2,1,0:T(8,128)(2,1)S(1)}, u32[]{:S(2)}, u32[]{:S(2)}) %collective-permute-start.1) | collective-permute-done | bytes 110624 | tf_op jit(solution)/shard_map/ppermute | solution.py:403
  27.9 0.0 copy-done.1
  27.9 5.1 %shard_map.238 = (bf16[144,768]{1,0:T(8,128)(2,1)S(1)}, bf16[36,768]{1,0:T(8,128)(2,1)S(1)}) custom-call(s32[1]{0:T(128)} %bitcast.1.row_ref, s32[96]{0:T(128)S(1)} %copy-done.1, bf16[144,768]{1,0:T(8,128)(2,1)S(1)} %get-tuple-element.20.rolling_ref, bf16[36,768]{1,0:T(8,128)(2,1)S(1)} %collective-permute-done.landed_ref, bf16[72,768]{1,0:T(8,128)(2,1)S(1)} %bitcast.13, ...), custom_call_target="tpu_custom_call" | custom-call | tf_op jit(solution)/shard_map/pallas_call | solution.py:385
  33.1 3.2 %collective-permute-start.2 = (bf16[36,768]{1,0:T(8,128)(2,1)S(1)}, bf16[36,768]{1,0:T(8,128)(2,1)S(1)}, u32[]{:S(2)}, u32[]{:S(2)}) collective-permute-start(bf16[36,768]{1,0:T(8,128)(2,1)S(1)} %get-tuple-element.23), channel_id=1, source_target_pairs={{0,16},{16,32},{32,48},{48,64},{64,80},{80,96},{96,112},{112,128},... | collective-permute-start | bytes 165896 | tf_op jit(solution)/shard_map/ppermute | solution.py:403
  36.3 4.2 %collective-permute-done.2.landed_ref = bf16[36,768]{1,0:T(8,128)(2,1)S(1)} collective-permute-done((bf16[36,768]{1,0:T(8,128)(2,1)S(1)}, bf16[36,768]{1,0:T(8,128)(2,1)S(1)}, u32[]{:S(2)}, u32[]{:S(2)}) %collective-permute-start.2) | collective-permute-done | bytes 55328 | tf_op jit(solution)/shard_map/ppermute | solution.py:403
  40.6 1.9 %collective-permute-start.3 = (bf16[3,24,768]{2,1,0:T(8,128)(2,1)S(1)}, bf16[3,24,768]{2,1,0:T(8,128)(2,1)S(1)}, u32[]{:S(2)}, u32[]{:S(2)}) collective-permute-start(bf16[3,24,768]{2,1,0:T(8,128)(2,1)S(1)} %pad_maximum_fusion.1), channel_id=1, source_target_pairs={{0,1},{1,2},{2,3},{3,4},{4,5},{5,6},{6,7},{7,8},{8,9},{9,10},{10,1... | collective-permute-start | bytes 331784 | tf_op jit(solution)/shard_map/ppermute | solution.py:403
  42.5 10.3 %collective-permute-done.3 = bf16[3,24,768]{2,1,0:T(8,128)(2,1)S(1)} collective-permute-done((bf16[3,24,768]{2,1,0:T(8,128)(2,1)S(1)}, bf16[3,24,768]{2,1,0:T(8,128)(2,1)S(1)}, u32[]{:S(2)}, u32[]{:S(2)}) %collective-permute-start.3) | collective-permute-done | bytes 110624 | tf_op jit(solution)/shard_map/ppermute | solution.py:403
  52.8 5.7 %shard_map.239 = (f32[144,512]{1,0:T(8,128)}, bf16[144,512]{1,0:T(8,128)(2,1)}, bf16[272,512]{1,0:T(8,128)(2,1)S(1)}, bf16[272,512]{1,0:T(8,128)(2,1)S(1)}) custom-call(s32[1]{0:T(128)} %bitcast.core_ref, f32[144,1024]{1,0:T(8,128)} %get-tuple-element.17.wide_ref, bf16[144,1024]{1,0:T(8,128)(2,1)} %get-tuple-element.18.saved_ref, ...), custom_call_target="tpu_custom_call" | custom-call | tf_op jit(solution)/shard_map/pallas_call | solution.py:385
  58.5 9.6 %collective-permute-start.4 = (bf16[272,512]{1,0:T(8,128)(2,1)S(1)}, bf16[272,512]{1,0:T(8,128)(2,1)S(1)}, u32[]{:S(2)}, u32[]{:S(2)}) collective-permute-start(bf16[272,512]{1,0:T(8,128)(2,1)S(1)} %get-tuple-element.27), channel_id=1, source_target_pairs={{0,16},{16,0},{1,17},{17,1},{2,18},{18,2},{3,19},{19,3},{4,20},{20... | collective-permute-start | bytes 835592 | tf_op jit(solution)/shard_map/ppermute | solution.py:465
  68.0 1.2 collective-permute-done.4.landed_ref
  69.2 0.1 shard_map.240
  69.3 15.3 %all_to_all.15.parts_ref = bf16[32,16,384]{2,1,0:T(8,128)(2,1)S(1)} all-to-all(bf16[32,16,384]{2,1,0:T(8,128)(2,1)S(1)} %shard_map.240), channel_id=1, replica_groups=mesh['z_lo'=4,'x'=4,'core'=2,'z_hi'=2,'y'=8] {'x','y'}, dimensions={0} | all-to-all | bytes 786432 | tf_op jit(solution)/shard_map/all_to_all | solution.py:467
  84.6 0.1 shard_map.241
  84.6 9.0 %all_to_all.16.parts_ref = bf16[8,16,384]{2,1,0:T(8,128)(2,1)S(1)} all-to-all(bf16[8,16,384]{2,1,0:T(8,128)(2,1)S(1)} %shard_map.241), channel_id=1, replica_groups=mesh['z_lo'=4,'x'=4,'core'=2,'z_hi'=2,'y'=8] {'z_lo','z_hi'}, dimensions={0} | all-to-all | bytes 196608 | tf_op jit(solution)/shard_map/all_to_all | solution.py:469
  93.7 0.6 shard_map.242
  94.3 16.7 %all_to_all.17.mine_ref = bf16[32,16,256]{2,1,0:T(8,128)(2,1)S(1)} all-to-all(bf16[32,16,256]{2,1,0:T(8,128)(2,1)S(1)} %get-tuple-element.28), channel_id=1, replica_groups=mesh['z_lo'=4,'x'=4,'core'=2,'z_hi'=2,'y'=8] {'x','y'}, dimensions={0} | all-to-all | bytes 524288 | tf_op jit(solution)/shard_map/all_to_all | solution.py:475
  111.0 5.9 %collective-permute-start.5 = (bf16[32,16,256]{2,1,0:T(8,128)(2,1)S(1)}, bf16[32,16,256]{2,1,0:T(8,128)(2,1)S(1)}, u32[]{:S(2)}, u32[]{:S(2)}) collective-permute-start(bf16[32,16,256]{2,1,0:T(8,128)(2,1)S(1)} %all_to_all.17.mine_ref), channel_id=1, source_target_pairs={{0,16},{16,0},{1,17},{17,1},{2,18},{18,2},{3,19},{19,3},{4,20},{20... | collective-permute-start | bytes 786440 | tf_op jit(solution)/shard_map/ppermute | solution.py:476
  116.9 1.1 collective-permute-done.5.other_ref
  118.0 0.8 shard_map.243
  (8 shorter events, 0.2 us)
Async XLA Ops:
  0.6 0.7 copy-start
  1.3 26.6 %copy-start.1 = (s32[96]{0:T(128)S(1)}, s32[96]{0:T(128)}, u32[]{:S(2)}) copy-start(s32[96]{0:T(128)} %keep_ref.3) | copy-start | bytes 1156
  6.2 9.7 %collective-permute-start = (bf16[36,768]{1,0:T(8,128)(2,1)S(1)}, bf16[36,768]{1,0:T(8,128)(2,1)S(1)}, u32[]{:S(2)}, u32[]{:S(2)}) collective-permute-start(bf16[36,768]{1,0:T(8,128)(2,1)S(1)} %get-tuple-element.21), channel_id=1, source_target_pairs={{0,496},{16,0},{32,16},{48,32},{64,48},{80,64},{96,80},{112,96},{1... | collective-permute-start | bytes 165896 | tf_op jit(solution)/shard_map/ppermute | solution.py:403
  15.9 12.0 %collective-permute-start.1 = (bf16[3,24,768]{2,1,0:T(8,128)(2,1)S(1)}, bf16[3,24,768]{2,1,0:T(8,128)(2,1)S(1)}, u32[]{:S(2)}, u32[]{:S(2)}) collective-permute-start(bf16[3,24,768]{2,1,0:T(8,128)(2,1)S(1)} %pad_maximum_fusion), channel_id=1, source_target_pairs={{0,15},{1,0},{2,1},{3,2},{4,3},{5,4},{6,5},{7,6},{8,7},{9,8},{10,9... | collective-permute-start | bytes 331784 | tf_op jit(solution)/shard_map/ppermute | solution.py:403
  33.1 7.4 %collective-permute-start.2 = (bf16[36,768]{1,0:T(8,128)(2,1)S(1)}, bf16[36,768]{1,0:T(8,128)(2,1)S(1)}, u32[]{:S(2)}, u32[]{:S(2)}) collective-permute-start(bf16[36,768]{1,0:T(8,128)(2,1)S(1)} %get-tuple-element.23), channel_id=1, source_target_pairs={{0,16},{16,32},{32,48},{48,64},{64,80},{80,96},{96,112},{112,128},... | collective-permute-start | bytes 165896 | tf_op jit(solution)/shard_map/ppermute | solution.py:403
  40.6 12.2 %collective-permute-start.3 = (bf16[3,24,768]{2,1,0:T(8,128)(2,1)S(1)}, bf16[3,24,768]{2,1,0:T(8,128)(2,1)S(1)}, u32[]{:S(2)}, u32[]{:S(2)}) collective-permute-start(bf16[3,24,768]{2,1,0:T(8,128)(2,1)S(1)} %pad_maximum_fusion.1), channel_id=1, source_target_pairs={{0,1},{1,2},{2,3},{3,4},{4,5},{5,6},{6,7},{7,8},{8,9},{9,10},{10,1... | collective-permute-start | bytes 331784 | tf_op jit(solution)/shard_map/ppermute | solution.py:403
  58.5 10.7 %collective-permute-start.4 = (bf16[272,512]{1,0:T(8,128)(2,1)S(1)}, bf16[272,512]{1,0:T(8,128)(2,1)S(1)}, u32[]{:S(2)}, u32[]{:S(2)}) collective-permute-start(bf16[272,512]{1,0:T(8,128)(2,1)S(1)} %get-tuple-element.27), channel_id=1, source_target_pairs={{0,16},{16,0},{1,17},{17,1},{2,18},{18,2},{3,19},{19,3},{4,20},{20... | collective-permute-start | bytes 835592 | tf_op jit(solution)/shard_map/ppermute | solution.py:465
  111.0 7.0 %collective-permute-start.5 = (bf16[32,16,256]{2,1,0:T(8,128)(2,1)S(1)}, bf16[32,16,256]{2,1,0:T(8,128)(2,1)S(1)}, u32[]{:S(2)}, u32[]{:S(2)}) collective-permute-start(bf16[32,16,256]{2,1,0:T(8,128)(2,1)S(1)} %all_to_all.17.mine_ref), channel_id=1, source_target_pairs={{0,16},{16,0},{1,17},{17,1},{2,18},{18,2},{3,19},{19,3},{4,20},{20... | collective-permute-start | bytes 786440 | tf_op jit(solution)/shard_map/ppermute | solution.py:476

commit v3 on v2

v3 whole, which is shorter than its diff:
```python
import functools

import jax
import jax.numpy as jnp
import numpy as np
from jax import lax
from jax.experimental import pallas as pl
from jax.experimental.pallas import tpu as pltpu
from jax.sharding import Mesh
from jax.sharding import PartitionSpec as P

D = 512
HEAD_DIM = 32
HEADS = 8
INNER = HEADS * HEAD_DIM
WIN_LAT = 6
WIN_LON = 12
HALF_LAT = WIN_LAT // 2
HALF_LON = WIN_LON // 2
WIN = WIN_LAT * WIN_LON
SPAN_LON = 2 * WIN_LON - 1
REACH = WIN_LAT * SPAN_LON
PLACES = 80
SIDE = 48
GROUP = 4
GROUPS = HEADS // GROUP
SHEET = GROUP * HEAD_DIM
TILES = WIN * GROUP // 8
LOG2E = 1.4426950408889634
STACK = WIN * GROUP
GAIN_ROWS = 8

NORM_EPS = 1e-05
SCALE = HEAD_DIM ** (-0.5)
SHUT = -1e30

F32 = jnp.float32
BF16 = jnp.bfloat16


def dot_nn(left, right):
    return lax.dot_general(left, right, (((1,), (0,)), ((), ())), preferred_element_type=F32)


def dot_nt(left, right):
    return lax.dot_general(left, right, (((1,), (1,)), ((), ())), preferred_element_type=F32)


def dot_tn(left, right):
    return lax.dot_general(left, right, (((0,), (0,)), ((), ())), preferred_element_type=F32)


def spread_matrix():
    spread = np.zeros((WIN, GROUP, PLACES), np.float32)
    for key in range(WIN):
        spread[key, :, key] = 1
    return spread.reshape(STACK, PLACES)


def reach_matrix():
    reach = np.zeros((REACH, WIN_LON, 128), np.float32)
    for e2 in range(WIN_LON):
        for a in range(WIN_LAT):
            for e in range(WIN_LON):
                reach[a * SPAN_LON + e - e2 + WIN_LON - 1, e2, e * WIN_LAT + a] = 1
    return reach.reshape(REACH, -1)


def own_windows(cols):
    order = np.zeros((cols // WIN_LON, PLACES, WIN_LAT * cols), np.float32)
    for w in range(cols // WIN_LON):
        for a in range(WIN_LAT):
            for e in range(WIN_LON):
                order[w, e * WIN_LAT + a, a * cols + w * WIN_LON + e] = 1
    return order.reshape(-1, WIN_LAT * cols)


def side_rows(cols, first):
    strip = np.zeros((SIDE, WIN_LAT * cols), np.float32)
    for i in range(WIN_LAT):
        for j in range(HALF_LON):
            strip[side_place(i, j), i * cols + first + j] = 1
    return strip


def side_place(i, j):
    return i // HALF_LAT * (SIDE // 2) + i % HALF_LAT * HALF_LON + j


def band_rows(cols):
    return -(-HALF_LAT * cols // 16) * 16


def near_place(i, j, cols):
    cells, band = WIN_LAT * cols, band_rows(cols)
    strip = band + SIDE
    left, own, right, below = strip, strip + SIDE, strip + SIDE + cells, strip + 2 * SIDE + cells
    inside = 0 <= j < cols
    corner = (j + HALF_LON) if j < 0 else (SIDE // 2 + j - cols)
    if i < 0:
        return (i + WIN_LAT) * cols + j - (cells - band) if inside else band + (i + HALF_LAT) * HALF_LON + corner
    if i >= WIN_LAT:
        row = i - WIN_LAT
        return below + (row * cols + j if inside else band + row * HALF_LON + corner)
    if inside:
        return own + i * cols + j
    return left + side_place(i, j + HALF_LON) if j < 0 else right + side_place(i, j - cols)


def near_windows(cols):
    cells, across = WIN_LAT * cols, cols // WIN_LON + 1
    near = 2 * (band_rows(cols) + 2 * SIDE) + cells
    order = np.zeros((2, across, PLACES, near), np.float32)
    back = np.zeros((cells, 2, across, PLACES), np.float32)
    for u in range(2):
        for v in range(across):
            for a in range(WIN_LAT):
                for e in range(WIN_LON):
                    i, j = u * WIN_LAT + a - HALF_LAT, v * WIN_LON + e - HALF_LON
                    place = e * WIN_LAT + a
                    order[u, v, place, near_place(i, j, cols)] = 1
                    if 0 <= i < WIN_LAT and 0 <= j < cols:
                        back[i * cols + j, u, v, place] = 1
    return order.reshape(-1, near), back.reshape(cells, -1)


def fixed(matrix):
    return jnp.asarray(matrix, BF16)


def norm_stats(values):
    row_mean = jnp.sum(values, axis=-1, keepdims=True) * (1.0 / D)
    centred = values - row_mean
    row_var = jnp.sum(centred * centred, axis=-1, keepdims=True) * (1.0 / D)
    inv_std = lax.rsqrt(row_var + NORM_EPS)
    return centred * inv_std, inv_std


def norm_back(d_float, unit_rows, inv_std, gain_row):
    d_unit = d_float * gain_row
    mean_grad = jnp.sum(d_unit, axis=-1, keepdims=True) * (1.0 / D)
    mean_proj = jnp.sum(d_unit * unit_rows, axis=-1, keepdims=True) * (1.0 / D)
    d_input = inv_std * (d_unit - mean_grad - unit_rows * mean_proj)
    return d_input, jnp.sum(d_float * unit_rows, axis=0, keepdims=True)


def position_bias(table, reach):
    table = table * LOG2E
    shifted = jnp.concatenate(
        [
            table[g * GROUP : (g + 1) * GROUP, (WIN_LAT - 1 - a2) * SPAN_LON : (WIN_LAT - 1 - a2) * SPAN_LON + REACH]
            for g in range(GROUPS)
            for a2 in range(WIN_LAT)
        ],
        axis=0,
    )
    high = shifted.astype(BF16)
    rest = shifted - high.astype(F32)
    middle = rest.astype(BF16)
    low = (rest - middle.astype(F32)).astype(BF16)
    spread = dot_nn(high, reach) + (dot_nn(middle, reach) + dot_nn(low, reach))
    return [spread[:, 128 * e2 : 128 * e2 + PLACES] for e2 in range(WIN_LON)]


def masked(blocks, keep_of, split_rows):
    rows = WIN_LAT * GROUP
    place = lax.broadcasted_iota(jnp.int32, (rows, PLACES), 1)
    key_row = lax.broadcasted_iota(jnp.int32, (rows, PLACES), 0) // GROUP
    query_late = jnp.where(place % WIN_LAT >= HALF_LAT, 1, 0)
    key_late = jnp.where(key_row >= HALF_LAT, 1, 0)
    shut = jnp.where(query_late == key_late, 0, 1) * split_rows
    for a2 in range(WIN_LAT):
        shut = shut + jnp.where(key_row == a2, 1, 0) * jnp.where(keep_of(a2) == 1, 0, 1)
    tile = jnp.where(shut > 0, SHUT, 0.0).astype(F32)
    return [
        jnp.concatenate([block[g * rows : (g + 1) * rows] + tile for block in blocks], axis=0).reshape(TILES, 8, PLACES)
        for g in range(GROUPS)
    ]


def own_head():
    head = lax.broadcasted_iota(jnp.int32, (8, 2 * INNER), 0) % GROUP
    lane = lax.broadcasted_iota(jnp.int32, (8, 2 * INNER), 1)
    return jnp.where((lane // HEAD_DIM) % GROUP == head, 1.0, 0.0).astype(F32)[None]


def sheet(array, g):
    return array[:, g * SHEET : (g + 1) * SHEET]


def own_parts(stacked, own):
    return (stacked.reshape(TILES, 8, 2 * INNER) * own).reshape(STACK, 2 * INNER).astype(BF16)


def stack_up(key_values, spread, own):
    stacks = [own_parts(stacked, own) for stacked in [dot_nn(spread, each) for each in key_values]]
    return [(stack[:, :INNER], stack[:, INNER:]) for stack in stacks]


def over_keys(combine, tiles):
    return combine(tiles, jnp.concatenate([tiles[GROUP:], tiles[:GROUP]], axis=0))


def attend(queries, stacks, biases):
    both = [(w, g) for w in range(len(queries)) for g in range(GROUPS)]
    scores = [dot_nt(sheet(stacks[w][0], g), sheet(queries[w], g)) for w, g in both]
    scores = [
        one.reshape(TILES, 8, PLACES) * (SCALE * LOG2E) + biases[w][g] for one, (w, g) in zip(scores, both)
    ]
    tops = [over_keys(jnp.maximum, jnp.max(one, axis=0)) for one in scores]
    exps = [jnp.exp2(one - top) for one, top in zip(scores, tops)]
    shares = [1.0 / over_keys(jnp.add, jnp.sum(one, axis=0)) for one in exps]
    probs = [one * share for one, share in zip(exps, shares)]
    lows = [one.reshape(STACK, PLACES).astype(BF16) for one in probs]
    outs = [dot_tn(low, sheet(stacks[w][1], g)).astype(BF16) for low, (w, g) in zip(lows, both)]
    per_window = [slice(w * GROUPS, (w + 1) * GROUPS) for w in range(len(queries))]
    return [probs[here] for here in per_window], [jnp.concatenate(outs[here], axis=1) for here in per_window]


def attend_back(d_outs, probs, queries, stacks, spread_back, own):
    both = [(w, g) for w in range(len(queries)) for g in range(GROUPS)]
    d_probs = [dot_nt(sheet(stacks[w][1], g), sheet(d_outs[w], g)) for w, g in both]
    d_probs = [one.reshape(TILES, 8, PLACES) for one in d_probs]
    totals = [over_keys(jnp.add, jnp.sum(one * probs[w][g], axis=0)) for one, (w, g) in zip(d_probs, both)]
    d_lows = [
        (probs[w][g] * (one - total) * SCALE).reshape(STACK, PLACES).astype(BF16)
        for one, total, (w, g) in zip(d_probs, totals, both)
    ]
    lows = [probs[w][g].reshape(STACK, PLACES).astype(BF16) for w, g in both]
    d_values = [dot_nn(low, sheet(d_outs[w], g)) for low, (w, g) in zip(lows, both)]
    d_keys = [dot_nn(d_low, sheet(queries[w], g)) for d_low, (w, g) in zip(d_lows, both)]
    d_queries = [dot_tn(d_low, sheet(stacks[w][0], g)).astype(BF16) for d_low, (w, g) in zip(d_lows, both)]
    per_window = [slice(w * GROUPS, (w + 1) * GROUPS) for w in range(len(queries))]
    d_stacks = [own_parts(jnp.concatenate(d_keys[here] + d_values[here], axis=1), own) for here in per_window]
    d_rest = [dot_nn(spread_back, d_stack).astype(BF16) for d_stack in d_stacks]
    return [jnp.concatenate(d_queries[here] + [rest], axis=1) for here, rest in zip(per_window, d_rest)]


def window_rows(array, w):
    return array[w * PLACES : (w + 1) * PLACES]


def first_kernel(
    row_ref, keep_ref, tokens_ref, mask_ref, embed_ref, gains_ref, w_qkv_ref, w_proj_ref, table_ref, cot_ref,
    order_ref, order_back_ref, spread_ref, reach_ref, left_ref, right_ref,
    wide_ref, qkv_ref, heads_ref, probs_ref, rolling_ref, to_left_ref, to_right_ref,
):
    rows, cols = mask_ref.shape
    mask = mask_ref[...].astype(F32)
    spread_mask = jnp.concatenate([jnp.broadcast_to(mask[r : r + 1], (cols, cols)) for r in range(rows)], axis=0)
    cell = lax.broadcasted_iota(jnp.int32, (rows * cols, cols), 0)
    lane = lax.broadcasted_iota(jnp.int32, (rows * cols, cols), 1)
    land = jnp.sum(jnp.where(cell % cols == lane, spread_mask, 0.0), axis=1, keepdims=True)
    embedded = tokens_ref[...].astype(F32) + jnp.where(land == 1.0, embed_ref[1:2], embed_ref[0:1])
    wide_ref[:, :D] = embedded
    unit_one, _ = norm_stats(embedded)
    normed_one = (unit_one * gains_ref[0:1]).astype(BF16)
    ordered = dot_nn(order_ref[...], normed_one).astype(BF16)
    qkv = dot_nn(ordered, w_qkv_ref[0]).astype(BF16)
    qkv_ref[...] = qkv
    bias = masked(position_bias(table_ref[0], reach_ref[...]), lambda a2: keep_ref[row_ref[0] + a2], 0)
    spread, own = spread_ref[...], own_head()
    windows = [window_rows(qkv, w) for w in range(cols // WIN_LON)]
    stacks = stack_up([here[:, INNER:] for here in windows], spread, own)
    all_probs, outs = attend([here[:, :INNER] for here in windows], stacks, [bias] * len(windows))
    for w, probs in enumerate(all_probs):
        for g in range(GROUPS):
            probs_ref[w, g] = probs[g]
    heads = dot_nn(order_back_ref[...], jnp.concatenate(outs, axis=0)).astype(BF16)
    heads_ref[...] = heads
    branch = dot_nn(heads, w_proj_ref[0]).astype(BF16)
    stream = embedded + branch.astype(F32)
    wide_ref[:, D:] = stream
    unit_two, _ = norm_stats(stream)
    normed_two = (unit_two * gains_ref[1:2]).astype(BF16)
    d_heads_two = dot_nt(cot_ref[...], w_proj_ref[1]).astype(BF16)
    rolling = jnp.concatenate([normed_two, d_heads_two], axis=1)
    rolling_ref[...] = rolling
    to_left_ref[...] = dot_nn(left_ref[...], rolling).astype(BF16)
    to_right_ref[...] = dot_nn(right_ref[...], rolling).astype(BF16)


def second_kernel(
    core_ref, row_ref, keep_ref, above_ref, left_ref, rolling_ref, right_ref, below_ref,
    wide_ref, qkv_ref, heads_ref, probs_ref, cot_ref, gains_ref, w_qkv_ref, w_proj_ref, table_ref,
    order_ref, order_back_ref, near_order_ref, near_back_ref, spread_ref, spread_back_ref, reach_ref,
    output_ref, grad_ref, kept_ref, sent_ref,
):
    lat_count = keep_ref.shape[0]
    row_first = row_ref[0]
    spread, spread_back, own = spread_ref[...], spread_back_ref[...], own_head()
    near = jnp.concatenate(
        [above_ref[...], left_ref[...], rolling_ref[...], right_ref[...], below_ref[...]], axis=0
    )
    ordered = dot_nn(near_order_ref[...], near).astype(BF16)
    qkv_two = dot_nn(ordered[:, :D], w_qkv_ref[1]).astype(BF16)
    blocks = position_bias(table_ref[0], reach_ref[...])
    across = near_order_ref.shape[0] // PLACES // 2
    biases = []
    for u in range(2):

        def keep_of(a2, u=u):
            place = row_first + (u * WIN_LAT - HALF_LAT + a2)
            place = jnp.where(place < 0, place + lat_count, place)
            return keep_ref[jnp.where(place >= lat_count, place - lat_count, place)]

        last_band = jnp.where((row_first + u * WIN_LAT) % lat_count == 0, 1, 0)
        biases += [masked(blocks, keep_of, last_band)] * across
    windows = [window_rows(qkv_two, w) for w in range(2 * across)]
    d_outs = [window_rows(ordered, w)[:, D:] for w in range(2 * across)]
    queries = [here[:, :INNER] for here in windows]
    stacks = stack_up([here[:, INNER:] for here in windows], spread, own)
    all_probs, outs = attend(queries, stacks, biases)
    d_windows = attend_back(d_outs, all_probs, queries, stacks, spread_back, own)
    rows_two = jnp.concatenate([jnp.concatenate(d_windows, axis=0), jnp.concatenate(outs, axis=0)], axis=1)
    unrolled = dot_nn(near_back_ref[...], rows_two).astype(BF16)
    heads_two = unrolled[:, 3 * INNER :]
    d_normed_two = dot_nt(unrolled[:, : 3 * INNER], w_qkv_ref[1]).astype(BF16)

    stream = wide_ref[:, D:]
    unit_two, inv_two = norm_stats(stream)
    d_branch, gain_two = norm_back(d_normed_two.astype(F32), unit_two, inv_two, gains_ref[1:2])
    cotangent = cot_ref[...]
    d_stream = (cotangent.astype(F32) + d_branch).astype(BF16)
    branch_two = dot_nn(heads_two, w_proj_ref[1]).astype(BF16)
    output_ref[...] = stream + branch_two.astype(F32)
    proj_one = dot_tn(heads_ref[...], d_stream)
    proj_two = dot_tn(heads_two, cotangent)
    upper = core_ref[0] == 1
    kept_ref[:INNER] = jnp.where(upper, proj_two, proj_one).astype(BF16)
    sent_ref[:INNER] = jnp.where(upper, proj_one, proj_two).astype(BF16)

    d_heads = dot_nt(d_stream, w_proj_ref[0]).astype(BF16)
    d_outs = dot_nn(order_ref[...], d_heads).astype(BF16)
    qkv_one = qkv_ref[...]
    windows = [window_rows(qkv_one, w) for w in range(probs_ref.shape[0])]
    d_outs = [window_rows(d_outs, w) for w in range(probs_ref.shape[0])]
    stacks = stack_up([here[:, INNER:] for here in windows], spread, own)
    all_probs = [[probs_ref[w, g] for g in range(GROUPS)] for w in range(probs_ref.shape[0])]
    d_windows = attend_back(d_outs, all_probs, [here[:, :INNER] for here in windows], stacks, spread_back, own)
    d_qkv = dot_nn(order_back_ref[...], jnp.concatenate(d_windows, axis=0)).astype(BF16)
    d_normed = dot_nt(d_qkv, w_qkv_ref[0]).astype(BF16)
    unit_one, inv_one = norm_stats(wide_ref[:, :D])
    d_branch, gain_one = norm_back(d_normed.astype(F32), unit_one, inv_one, gains_ref[0:1])
    grad_ref[...] = (d_stream.astype(F32) + d_branch).astype(BF16)
    gain = jnp.concatenate(
        [row[:, 128 * j : 128 * (j + 1)] for row in (gain_one, gain_two) for j in range(D // 128)], axis=0
    )
    pair = jnp.concatenate([gain_pair(gain), jnp.zeros((2 * GAIN_ROWS, D - 128), BF16)], axis=1)
    kept_ref[INNER:] = pair
    sent_ref[INNER:] = pair


def gain_pair(gain):
    high = gain.astype(BF16).astype(F32)
    return jnp.concatenate([high, gain - high], axis=0).astype(BF16)


def pair_sum(pair):
    return pair[:GAIN_ROWS] + pair[GAIN_ROWS : 2 * GAIN_ROWS]


def core_sum_kernel(kept_ref, landed_ref, out_ref):
    total = kept_ref[...].astype(F32) + landed_ref[...].astype(F32)
    low = total[:INNER].astype(BF16)
    pair = gain_pair(pair_sum(total[INNER:, :128]))
    pieces, tall = out_ref.shape[0], out_ref.shape[1]
    for s in range(pieces):
        row, col = tall * (s // 2), D // 2 * (s % 2)
        out_ref[s, :, : D // 2] = low[row : row + tall, col : col + D // 2]
        out_ref[s, : 2 * GAIN_ROWS, D // 2 :] = pair
        if tall > 2 * GAIN_ROWS:
            out_ref[s, 2 * GAIN_ROWS :, D // 2 :] = jnp.zeros((tall - 2 * GAIN_ROWS, 128), BF16)


def added(parts_ref):
    total = parts_ref[0].astype(F32)
    for s in range(1, parts_ref.shape[0]):
        total = total + parts_ref[s].astype(F32)
    return total[:, : D // 2], pair_sum(total[:, D // 2 :])


def plane_sum_kernel(parts_ref, out_ref):
    proj, gain = added(parts_ref)
    low, pair = proj.astype(BF16), gain_pair(gain)
    tall = out_ref.shape[1]
    for s in range(out_ref.shape[0]):
        out_ref[s, :, : D // 2] = low
        out_ref[s, : 2 * GAIN_ROWS, D // 2 :] = pair
        if tall > 2 * GAIN_ROWS:
            out_ref[s, 2 * GAIN_ROWS :, D // 2 :] = jnp.zeros((tall - 2 * GAIN_ROWS, 128), BF16)


def depth_sum_kernel(scale, parts_ref, proj_ref, gains_ref):
    proj, gain = added(parts_ref)
    low = (proj * scale).astype(BF16)
    for s in range(proj_ref.shape[0]):
        proj_ref[s] = low
    gain = gain * scale
    per_row = D // 128
    for r in range(GAIN_ROWS):
        gains_ref[r // per_row : r // per_row + 1, 128 * (r % per_row) : 128 * (r % per_row + 1)] = gain[r : r + 1]


def join_kernel(core_ref, mine_ref, other_ref, out_ref):
    pieces, tall = mine_ref.shape[0], mine_ref.shape[1]
    upper = core_ref[0] == 1
    for s in range(pieces):
        row, col = tall * (s // 2), D // 2 * (s % 2)
        mine, other = mine_ref[s], other_ref[s]
        out_ref[0, row : row + tall, col : col + D // 2] = jnp.where(upper, other, mine)
        out_ref[1, row : row + tall, col : col + D // 2] = jnp.where(upper, mine, other)


def scalars(array):
    return array, pl.BlockSpec(memory_space=pltpu.SMEM)


def whole(array):
    return array, pl.BlockSpec(array.shape, functools.partial(lambda n, i: (0,) * n, array.ndim))


def in_hbm(array):
    return whole(pltpu.with_memory_space_constraint(array, pltpu.HBM))


def layer(array, index):
    spec = pl.BlockSpec((1,) + array.shape[1:], lambda i: (index,) + (0,) * (array.ndim - 1))
    return pltpu.with_memory_space_constraint(array, pltpu.HBM), spec


def hbm(*dims, dtype=BF16):
    return pltpu.HBM(dims, dtype)


def either(*dims, dtype=BF16):
    return jax.ShapeDtypeStruct(dims, dtype)


def call(kernel, outs, operands):
    arrays, specs = zip(*operands)
    out_specs = [pl.BlockSpec(o.shape, functools.partial(lambda n, i: (0,) * n, len(o.shape))) for o in outs]
    return pl.pallas_call(
        kernel,
        grid=(1,),
        in_specs=specs,
        out_specs=out_specs,
        out_shape=outs,
        compiler_params=pltpu.CompilerParams(vmem_limit_bytes=50 * 1024 * 1024),
    )(*arrays)


LON = ("z_lo", "x", "core")
LAT = ("z_hi", "y")
PLANE = ("x", "y")
DEPTH = ("z_lo", "z_hi")


def passed_along(array, axes, by):
    length = lax.axis_size(axes)
    return lax.ppermute(array, axes, [(i, (i + by) % length) for i in range(length)])


def local(tokens, land_mask, keep_rows, land_embed, norm_gains, w_qkv, w_proj, rel_bias, cotangent):
    rows, cols = tokens.shape[0], tokens.shape[1]
    cells, count = rows * cols, cols // WIN_LON
    band, wide = band_rows(cols), D + INNER
    scale_out = float(rows * lax.axis_size(LAT) * cols * lax.axis_size(LON)) ** (-0.5)
    row_first = scalars((lax.axis_index(LAT) * rows).astype(jnp.int32).reshape(1))
    core = scalars(lax.axis_index("core").astype(jnp.int32).reshape(1))
    keep_in = scalars(keep_rows)
    order = own_windows(cols)
    order, order_back = in_hbm(fixed(order)), in_hbm(fixed(order.T))
    near_order, near_back = (in_hbm(fixed(m)) for m in near_windows(cols))
    spread = spread_matrix()
    spread, spread_back = in_hbm(fixed(spread)), in_hbm(fixed(spread.T))
    reach = in_hbm(fixed(reach_matrix()))
    cot_flat = in_hbm(cotangent.reshape(cells, D))

    wide_one, qkv_one, heads_one, probs_one, rolling, to_left, to_right = call(
        first_kernel,
        [
            hbm(cells, 2 * D, dtype=F32), hbm(count * PLACES, 3 * INNER), hbm(cells, INNER),
            hbm(count, GROUPS, TILES, 8, PLACES, dtype=F32), either(cells, wide), either(SIDE, wide), either(SIDE, wide),
        ],
        [
            row_first, keep_in, in_hbm(tokens.reshape(cells, D)), in_hbm(land_mask), in_hbm(land_embed),
            in_hbm(norm_gains), layer(w_qkv, 0), in_hbm(w_proj), layer(rel_bias, 0), cot_flat,
            order, order_back, spread, reach,
            in_hbm(fixed(side_rows(cols, 0))), in_hbm(fixed(side_rows(cols, cols - HALF_LON))),
        ],
    )

    right = passed_along(to_left, LON, -1)
    left = passed_along(to_right, LON, 1)
    to_above = jnp.concatenate([rolling[:band], left[: SIDE // 2], right[: SIDE // 2]], axis=0)
    to_below = jnp.concatenate([rolling[cells - band :], left[SIDE // 2 :], right[SIDE // 2 :]], axis=0)
    below = passed_along(to_above, LAT, -1)
    above = passed_along(to_below, LAT, 1)

    output, grad_tokens, kept, sent = call(
        second_kernel,
        [hbm(cells, D, dtype=F32), hbm(cells, D), either(INNER + 2 * GAIN_ROWS, D), either(INNER + 2 * GAIN_ROWS, D)],
        [
            core, row_first, keep_in, whole(above), whole(left), whole(rolling), whole(right), whole(below),
            in_hbm(wide_one), in_hbm(qkv_one), in_hbm(heads_one), in_hbm(probs_one), cot_flat,
            in_hbm(norm_gains), in_hbm(w_qkv), in_hbm(w_proj), layer(rel_bias, 1),
            order, order_back, near_order, near_back, spread, spread_back, reach,
        ],
    )

    planes, depths, cores = lax.axis_size(PLANE), lax.axis_size(DEPTH), lax.axis_size("core")
    tall = 2 * INNER // planes
    swap = [(i, (i + 1) % cores) for i in range(cores)]
    landed = lax.ppermute(sent, "core", swap)
    (pieces,) = call(core_sum_kernel, [either(planes, tall, D // 2 + 128)], [whole(kept), whole(landed)])
    parts = lax.all_to_all(pieces, PLANE, 0, 0, tiled=True)
    (pieces,) = call(plane_sum_kernel, [either(depths, tall, D // 2 + 128)], [whole(parts)])
    parts = lax.all_to_all(pieces, DEPTH, 0, 0, tiled=True)
    pieces, grad_gains = call(
        functools.partial(depth_sum_kernel, scale_out),
        [either(planes, tall, D // 2), either(2, D, dtype=F32)],
        [whole(parts)],
    )
    mine = lax.all_to_all(pieces, PLANE, 0, 0, tiled=True)
    other = lax.ppermute(mine, "core", swap)
    (grad_proj,) = call(join_kernel, [either(2, INNER, D)], [core, whole(mine), whole(other)])
    return output.reshape(rows, cols, D), grad_tokens.reshape(rows, cols, D), grad_proj, grad_gains


def chip_axes(lon, lat):
    x = min(4, lon // 2)
    y = min(8, lat)
    return (lon // (2 * x), x, 2, lat // y, y)


def solution(mesh):
    sizes = chip_axes(mesh.shape["lon"], mesh.shape["lat"])
    fine = Mesh(mesh.devices.reshape(sizes), LON + LAT)
    grid = P(LAT, LON, None)
    in_specs = (grid, P(LAT, LON), P(), P(), P(), P(), P(), P(), grid)
    out_specs = (grid, grid, P(), P())
    return jax.shard_map(local, mesh=fine, in_specs=in_specs, out_specs=out_specs, check_vma=False)
```

time: 119 us -> 112 us (0.941)
  waiting for transfers between devices: 19.3 us -> 6.69 us
  blocking collectives: 41 us -> 50.5 us
  Pallas kernels: 17.3 us -> 15.4 us
  starting transfers between devices: 39.6 us -> 37.8 us
    ppermute x4, waiting for transfers between devices: 17 us -> 4.39 us  [passed_along(): lax.ppermute(array, axes, [(i, (i + by) % length) for i in range(length)])]
    all_to_all x1, blocking collectives: 15.3 us -> 24.3 us  [local(): parts = lax.all_to_all(pieces, PLANE, 0, 0, tiled=True)]
    ppermute x1, starting transfers between devices: 9.56 us -> 6.35 us  [local(): landed = lax.ppermute(sent, 'core', swap)]
    pallas_call x7 -> x6, Pallas kernels: 17.3 us -> 15.4 us  [call(): pl.pallas_call(kernel, grid=(1,), in_specs=specs, out_specs=out_specs, ou...]
  transfers between devices with their start and end apart: 6 -> 6, of which waited for: 6 -> 4; matrix products, arithmetic and copies ran while one was open for 0% -> 0% of each run, Pallas kernels for 0% -> 0%
where the time goes in v3:
time: 112 us
  blocking collectives  50.5 us (45%)
  starting transfers between devices  37.8 us (34%)
  Pallas kernels  15.4 us (14%)
  waiting for transfers between devices  6.69 us (6%)
    ppermute x4, starting transfers between devices, passed_along(): lax.ppermute(array, axes, [(i, (i + by) % length) for i in range(length)])  25 us
    all_to_all x1, blocking collectives, local(): parts = lax.all_to_all(pieces, PLANE, 0, 0, tiled=True)  24.3 us
    all_to_all x1, blocking collectives, local(): mine = lax.all_to_all(pieces, PLANE, 0, 0, tiled=True)  17.1 us
    pallas_call x6, Pallas kernels, call(): pl.pallas_call(kernel, grid=(1,), in_specs=specs, out_specs=out_specs, ou...  15.4 us
    all_to_all x1, blocking collectives, local(): parts = lax.all_to_all(pieces, DEPTH, 0, 0, tiled=True)  9.17 us
    ppermute x1, starting transfers between devices, local(): other = lax.ppermute(mine, 'core', swap)  6.42 us
    ppermute x1, starting transfers between devices, local(): landed = lax.ppermute(sent, 'core', swap)  6.35 us
    ppermute x4, waiting for transfers between devices, passed_along(): lax.ppermute(array, axes, [(i, (i + by) % length) for i in range(length)])  4.39 us
  transfers between devices with their start and end apart: 6, of which 4 were waited for; matrix products, arithmetic and copies ran while one was open for 0% of the time, Pallas kernels for 0%

profile of v3, /device:TPU:1, one launch (start us, length us, event | category | flops | bytes accessed | tf_op | source)
XLA Modules:
  0.0 111.9 jit_solution(15338450780730255188)
XLA Ops:
  0.6 0.0 copy-start
  0.7 0.6 copy-done
  1.3 4.3 %shard_map.201 = (f32[144,1024]{1,0:T(8,128)}, bf16[160,768]{1,0:T(8,128)(2,1)}, bf16[144,256]{1,0:T(8,128)(2,1)}, f32[2,2,36,8,80]{4,3,2,1,0:T(8,128)}, bf16[14...) custom-call(s32[1]{0:T(128)} %bitcast.1.row_ref, s32[96]{0:T(128)S(1)} %copy-done, ...), custom_call_target="tpu_custom_call" | custom-call | tf_op jit(solution)/shard_map/pallas_call | solution.py:443
  5.6 0.0 copy-start.1
  5.6 4.5 %collective-permute-start = (bf16[48,768]{1,0:T(8,128)(2,1)S(1)}, bf16[48,768]{1,0:T(8,128)(2,1)S(1)}, u32[]{:S(2)}, u32[]{:S(2)}) collective-permute-start(bf16[48,768]{1,0:T(8,128)(2,1)S(1)} %get-tuple-element.18), channel_id=1, source_target_pairs={{0,16},{16,32},{32,48},{48,64},{64,80},{80,96},{96,112},{112,128},... | collective-permute-start | bytes 221192 | tf_op jit(solution)/shard_map/ppermute | solution.py:461
  10.1 6.2 %collective-permute-start.1 = (bf16[48,768]{1,0:T(8,128)(2,1)S(1)}, bf16[48,768]{1,0:T(8,128)(2,1)S(1)}, u32[]{:S(2)}, u32[]{:S(2)}) collective-permute-start(bf16[48,768]{1,0:T(8,128)(2,1)S(1)} %get-tuple-element.19), channel_id=1, source_target_pairs={{0,496},{16,0},{32,16},{48,32},{64,48},{80,64},{96,80},{112,96},{1... | collective-permute-start | bytes 221192 | tf_op jit(solution)/shard_map/ppermute | solution.py:461
  16.3 0.0 collective-permute-done.left_ref
  16.4 0.8 collective-permute-done.1.right_ref
  17.2 1.9 %collective-permute-start.2 = (bf16[128,768]{1,0:T(8,128)(2,1)S(1)}, bf16[128,768]{1,0:T(8,128)(2,1)S(1)}, u32[]{:S(2)}, u32[]{:S(2)}) collective-permute-start(bf16[128,768]{1,0:T(8,128)(2,1)S(1)} %pad_maximum_fusion), channel_id=1, source_target_pairs={{0,1},{1,2},{2,3},{3,4},{4,5},{5,6},{6,7},{7,8},{8,9},{9,10},{10,1... | collective-permute-start | bytes 589832 | tf_op jit(solution)/shard_map/ppermute | solution.py:461
  19.2 12.4 %collective-permute-start.3 = (bf16[128,768]{1,0:T(8,128)(2,1)S(1)}, bf16[128,768]{1,0:T(8,128)(2,1)S(1)}, u32[]{:S(2)}, u32[]{:S(2)}) collective-permute-start(bf16[128,768]{1,0:T(8,128)(2,1)S(1)} %pad_maximum_fusion.1), channel_id=1, source_target_pairs={{0,15},{1,0},{2,1},{3,2},{4,3},{5,4},{6,5},{7,6},{8,7},{9,8},{10,9... | collective-permute-start | bytes 589832 | tf_op jit(solution)/shard_map/ppermute | solution.py:461
  31.6 3.5 %collective-permute-done.2.above_ref = bf16[128,768]{1,0:T(8,128)(2,1)S(1)} collective-permute-done((bf16[128,768]{1,0:T(8,128)(2,1)S(1)}, bf16[128,768]{1,0:T(8,128)(2,1)S(1)}, u32[]{:S(2)}, u32[]{:S(2)}) %collective-permute-start.2) | collective-permute-done | bytes 196640 | tf_op jit(solution)/shard_map/ppermute | solution.py:461
  35.1 0.0 collective-permute-done.3.below_ref
  35.1 0.0 copy-done.1
  35.1 9.5 %shard_map.202 = (f32[144,512]{1,0:T(8,128)}, bf16[144,512]{1,0:T(8,128)(2,1)}, bf16[272,512]{1,0:T(8,128)(2,1)S(1)}, bf16[272,512]{1,0:T(8,128)(2,1)S(1)}) custom-call(s32[1]{0:T(128)} %bitcast.core_ref, s32[1]{0:T(128)} %bitcast.1.row_ref, s32[96]{0:T(128)S(1)} %copy-done.1, bf16[128,768]{1,0:T(8,128)(2,1)S(1)} %collective-permute-done.2.above_ref, ...), custom_call_target="tpu_custom_call" | custom-call | tf_op jit(solution)/shard_map/pallas_call | solution.py:443
  44.7 6.4 %collective-permute-start.4 = (bf16[272,512]{1,0:T(8,128)(2,1)S(1)}, bf16[272,512]{1,0:T(8,128)(2,1)S(1)}, u32[]{:S(2)}, u32[]{:S(2)}) collective-permute-start(bf16[272,512]{1,0:T(8,128)(2,1)S(1)} %get-tuple-element.27), channel_id=1, source_target_pairs={{0,16},{16,0},{1,17},{17,1},{2,18},{18,2},{3,19},{19,3},{4,20},{20... | collective-permute-start | bytes 835592 | tf_op jit(solution)/shard_map/ppermute | solution.py:515
  51.0 1.2 %collective-permute-done.4.landed_ref = bf16[272,512]{1,0:T(8,128)(2,1)S(1)} collective-permute-done((bf16[272,512]{1,0:T(8,128)(2,1)S(1)}, bf16[272,512]{1,0:T(8,128)(2,1)S(1)}, u32[]{:S(2)}, u32[]{:S(2)}) %collective-permute-start.4) | collective-permute-done | bytes 278560 | tf_op jit(solution)/shard_map/ppermute | solution.py:515
  52.2 0.1 shard_map.203
  52.2 24.3 %all_to_all.15.parts_ref = bf16[32,16,384]{2,1,0:T(8,128)(2,1)S(1)} all-to-all(bf16[32,16,384]{2,1,0:T(8,128)(2,1)S(1)} %shard_map.203), channel_id=1, replica_groups=mesh['z_lo'=4,'x'=4,'core'=2,'z_hi'=2,'y'=8] {'x','y'}, dimensions={0} | all-to-all | bytes 786432 | tf_op jit(solution)/shard_map/all_to_all | solution.py:517
  76.5 0.1 shard_map.204
  76.6 9.2 %all_to_all.16.parts_ref = bf16[8,16,384]{2,1,0:T(8,128)(2,1)S(1)} all-to-all(bf16[8,16,384]{2,1,0:T(8,128)(2,1)S(1)} %shard_map.204), channel_id=1, replica_groups=mesh['z_lo'=4,'x'=4,'core'=2,'z_hi'=2,'y'=8] {'z_lo','z_hi'}, dimensions={0} | all-to-all | bytes 196608 | tf_op jit(solution)/shard_map/all_to_all | solution.py:519
  85.8 0.6 shard_map.205
  86.4 17.1 %all_to_all.17.mine_ref = bf16[32,16,256]{2,1,0:T(8,128)(2,1)S(1)} all-to-all(bf16[32,16,256]{2,1,0:T(8,128)(2,1)S(1)} %get-tuple-element.28), channel_id=1, replica_groups=mesh['z_lo'=4,'x'=4,'core'=2,'z_hi'=2,'y'=8] {'x','y'}, dimensions={0} | all-to-all | bytes 524288 | tf_op jit(solution)/shard_map/all_to_all | solution.py:525
  103.5 6.4 %collective-permute-start.5 = (bf16[32,16,256]{2,1,0:T(8,128)(2,1)S(1)}, bf16[32,16,256]{2,1,0:T(8,128)(2,1)S(1)}, u32[]{:S(2)}, u32[]{:S(2)}) collective-permute-start(bf16[32,16,256]{2,1,0:T(8,128)(2,1)S(1)} %all_to_all.17.mine_ref), channel_id=1, source_target_pairs={{0,16},{16,0},{1,17},{17,1},{2,18},{18,2},{3,19},{19,3},{4,20},{20... | collective-permute-start | bytes 786440 | tf_op jit(solution)/shard_map/ppermute | solution.py:526
  109.9 1.1 %collective-permute-done.5.other_ref = bf16[32,16,256]{2,1,0:T(8,128)(2,1)S(1)} collective-permute-done((bf16[32,16,256]{2,1,0:T(8,128)(2,1)S(1)}, bf16[32,16,256]{2,1,0:T(8,128)(2,1)S(1)}, u32[]{:S(2)}, u32[]{:S(2)}) %collective-permute-start.5) | collective-permute-done | bytes 262176 | tf_op jit(solution)/shard_map/ppermute | solution.py:526
  111.0 0.8 shard_map.206
  (5 shorter events, 0.1 us)
Async XLA Ops:
  0.6 0.7 copy-start
  5.6 29.6 %copy-start.1 = (s32[96]{0:T(128)S(1)}, s32[96]{0:T(128)}, u32[]{:S(2)}) copy-start(s32[96]{0:T(128)} %keep_ref.3) | copy-start | bytes 1156
  5.6 10.8 %collective-permute-start = (bf16[48,768]{1,0:T(8,128)(2,1)S(1)}, bf16[48,768]{1,0:T(8,128)(2,1)S(1)}, u32[]{:S(2)}, u32[]{:S(2)}) collective-permute-start(bf16[48,768]{1,0:T(8,128)(2,1)S(1)} %get-tuple-element.18), channel_id=1, source_target_pairs={{0,16},{16,32},{32,48},{48,64},{64,80},{80,96},{96,112},{112,128},... | collective-permute-start | bytes 221192 | tf_op jit(solution)/shard_map/ppermute | solution.py:461
  10.1 7.1 %collective-permute-start.1 = (bf16[48,768]{1,0:T(8,128)(2,1)S(1)}, bf16[48,768]{1,0:T(8,128)(2,1)S(1)}, u32[]{:S(2)}, u32[]{:S(2)}) collective-permute-start(bf16[48,768]{1,0:T(8,128)(2,1)S(1)} %get-tuple-element.19), channel_id=1, source_target_pairs={{0,496},{16,0},{32,16},{48,32},{64,48},{80,64},{96,80},{112,96},{1... | collective-permute-start | bytes 221192 | tf_op jit(solution)/shard_map/ppermute | solution.py:461
  17.2 17.9 %collective-permute-start.2 = (bf16[128,768]{1,0:T(8,128)(2,1)S(1)}, bf16[128,768]{1,0:T(8,128)(2,1)S(1)}, u32[]{:S(2)}, u32[]{:S(2)}) collective-permute-start(bf16[128,768]{1,0:T(8,128)(2,1)S(1)} %pad_maximum_fusion), channel_id=1, source_target_pairs={{0,1},{1,2},{2,3},{3,4},{4,5},{5,6},{6,7},{7,8},{8,9},{9,10},{10,1... | collective-permute-start | bytes 589832 | tf_op jit(solution)/shard_map/ppermute | solution.py:461
  19.2 16.0 %collective-permute-start.3 = (bf16[128,768]{1,0:T(8,128)(2,1)S(1)}, bf16[128,768]{1,0:T(8,128)(2,1)S(1)}, u32[]{:S(2)}, u32[]{:S(2)}) collective-permute-start(bf16[128,768]{1,0:T(8,128)(2,1)S(1)} %pad_maximum_fusion.1), channel_id=1, source_target_pairs={{0,15},{1,0},{2,1},{3,2},{4,3},{5,4},{6,5},{7,6},{8,7},{9,8},{10,9... | collective-permute-start | bytes 589832 | tf_op jit(solution)/shard_map/ppermute | solution.py:461
  44.7 7.5 %collective-permute-start.4 = (bf16[272,512]{1,0:T(8,128)(2,1)S(1)}, bf16[272,512]{1,0:T(8,128)(2,1)S(1)}, u32[]{:S(2)}, u32[]{:S(2)}) collective-permute-start(bf16[272,512]{1,0:T(8,128)(2,1)S(1)} %get-tuple-element.27), channel_id=1, source_target_pairs={{0,16},{16,0},{1,17},{17,1},{2,18},{18,2},{3,19},{19,3},{4,20},{20... | collective-permute-start | bytes 835592 | tf_op jit(solution)/shard_map/ppermute | solution.py:515
  103.5 7.6 %collective-permute-start.5 = (bf16[32,16,256]{2,1,0:T(8,128)(2,1)S(1)}, bf16[32,16,256]{2,1,0:T(8,128)(2,1)S(1)}, u32[]{:S(2)}, u32[]{:S(2)}) collective-permute-start(bf16[32,16,256]{2,1,0:T(8,128)(2,1)S(1)} %all_to_all.17.mine_ref), channel_id=1, source_target_pairs={{0,16},{16,0},{1,17},{17,1},{2,18},{18,2},{3,19},{19,3},{4,20},{20... | collective-permute-start | bytes 786440 | tf_op jit(solution)/shard_map/ppermute | solution.py:526

commit v4 on v3

--- a/solution.py
+++ b/solution.py
@@ -21,7 +21,7 @@
 SPAN_LON = 2 * WIN_LON - 1
 REACH = WIN_LAT * SPAN_LON
 PLACES = 80
-SIDE = 48
+SIDE = 80
 GROUP = 4
 GROUPS = HEADS // GROUP
 SHEET = GROUP * HEAD_DIM
@@ -75,41 +75,21 @@
     return order.reshape(-1, WIN_LAT * cols)
 
 
-def side_rows(cols, first):
-    strip = np.zeros((SIDE, WIN_LAT * cols), np.float32)
-    for i in range(WIN_LAT):
-        for j in range(HALF_LON):
-            strip[side_place(i, j), i * cols + first + j] = 1
-    return strip
-
-
-def side_place(i, j):
-    return i // HALF_LAT * (SIDE // 2) + i % HALF_LAT * HALF_LON + j
-
-
 def band_rows(cols):
     return -(-HALF_LAT * cols // 16) * 16
 
 
 def near_place(i, j, cols):
-    cells, band = WIN_LAT * cols, band_rows(cols)
-    strip = band + SIDE
-    left, own, right, below = strip, strip + SIDE, strip + SIDE + cells, strip + 2 * SIDE + cells
-    inside = 0 <= j < cols
-    corner = (j + HALF_LON) if j < 0 else (SIDE // 2 + j - cols)
-    if i < 0:
-        return (i + WIN_LAT) * cols + j - (cells - band) if inside else band + (i + HALF_LAT) * HALF_LON + corner
-    if i >= WIN_LAT:
-        row = i - WIN_LAT
-        return below + (row * cols + j if inside else band + row * HALF_LON + corner)
-    if inside:
-        return own + i * cols + j
-    return left + side_place(i, j + HALF_LON) if j < 0 else right + side_place(i, j - cols)
+    band = band_rows(cols)
+    if 0 <= j < cols:
+        return band - HALF_LAT * cols + (i + HALF_LAT) * cols + j
+    first = 2 * band + WIN_LAT * cols + (0 if j < 0 else SIDE)
+    return first + (i + HALF_LAT) * HALF_LON + (j + HALF_LON if j < 0 else j - cols)
 
 
 def near_windows(cols):
     cells, across = WIN_LAT * cols, cols // WIN_LON + 1
-    near = 2 * (band_rows(cols) + 2 * SIDE) + cells
+    near = 2 * (band_rows(cols) + SIDE) + cells
     order = np.zeros((2, across, PLACES, near), np.float32)
     back = np.zeros((cells, 2, across, PLACES), np.float32)
     for u in range(2):
@@ -241,9 +221,9 @@
 
 
 def first_kernel(
-    row_ref, keep_ref, tokens_ref, mask_ref, embed_ref, gains_ref, w_qkv_ref, w_proj_ref, table_ref, cot_ref,
-    order_ref, order_back_ref, spread_ref, reach_ref, left_ref, right_ref,
-    wide_ref, qkv_ref, heads_ref, probs_ref, rolling_ref, to_left_ref, to_right_ref,
+    odd_ref, row_ref, keep_ref, tokens_ref, mask_ref, embed_ref, gains_ref, w_qkv_ref, w_proj_ref, table_ref, cot_ref,
+    order_ref, order_back_ref, spread_ref, reach_ref,
+    wide_ref, qkv_ref, heads_ref, probs_ref, rolling_ref, one_ref, two_ref,
 ):
     rows, cols = mask_ref.shape
     mask = mask_ref[...].astype(F32)
@@ -276,12 +256,33 @@
     d_heads_two = dot_nt(cot_ref[...], w_proj_ref[1]).astype(BF16)
     rolling = jnp.concatenate([normed_two, d_heads_two], axis=1)
     rolling_ref[...] = rolling
-    to_left_ref[...] = dot_nn(left_ref[...], rolling).astype(BF16)
-    to_right_ref[...] = dot_nn(right_ref[...], rolling).astype(BF16)
+    band = one_ref.shape[0]
+    upper, lower = rolling[:band], rolling[rows * cols - band :]
+    odd = odd_ref[0] == 1
+    one_ref[...] = jnp.where(odd, lower, upper)
+    two_ref[...] = jnp.where(odd, upper, lower)
+
+
+def edge_kernel(cols, odd_ref, core_ref, one_ref, rolling_ref, two_ref, to_one_ref, to_two_ref):
+    band, cells = one_ref.shape[0], rolling_ref.shape[0]
+    tall = jnp.concatenate([one_ref[...], rolling_ref[...], two_ref[...]], axis=0)
+    shape = (SIDE, tall.shape[0])
+    row = lax.broadcasted_iota(jnp.int32, shape, 0)
+    place = lax.broadcasted_iota(jnp.int32, shape, 1)
+    i = row // HALF_LON
+    far = odd_ref[0] * (band + cells)
+    first = jnp.where(i < HALF_LAT, band - HALF_LAT * cols + far, band - HALF_LAT * cols)
+    first = jnp.where(i >= HALF_LAT + WIN_LAT, first - far, first)
+    source = first + i * cols + row % HALF_LON
+    source = jnp.where(i < 2 * WIN_LAT, source, -1)
+    shift = (cols - HALF_LON) * core_ref[0]
+    for out_ref, column in ((to_one_ref, shift), (to_two_ref, cols - HALF_LON - shift)):
+        pick = jnp.where(place == jnp.where(source < 0, -1, source + column), 1.0, 0.0).astype(BF16)
+        out_ref[...] = dot_nn(pick, tall).astype(BF16)
 
 
 def second_kernel(
-    core_ref, row_ref, keep_ref, above_ref, left_ref, rolling_ref, right_ref, below_ref,
+    odd_ref, core_ref, row_ref, keep_ref, one_ref, rolling_ref, two_ref, side_one_ref, side_two_ref,
     wide_ref, qkv_ref, heads_ref, probs_ref, cot_ref, gains_ref, w_qkv_ref, w_proj_ref, table_ref,
     order_ref, order_back_ref, near_order_ref, near_back_ref, spread_ref, spread_back_ref, reach_ref,
     output_ref, grad_ref, kept_ref, sent_ref,
@@ -289,8 +290,14 @@
     lat_count = keep_ref.shape[0]
     row_first = row_ref[0]
     spread, spread_back, own = spread_ref[...], spread_back_ref[...], own_head()
+    odd, upper = odd_ref[0] == 1, core_ref[0] == 1
+    one, two, side_one, side_two = one_ref[...], two_ref[...], side_one_ref[...], side_two_ref[...]
     near = jnp.concatenate(
-        [above_ref[...], left_ref[...], rolling_ref[...], right_ref[...], below_ref[...]], axis=0
+        [
+            jnp.where(odd, two, one), rolling_ref[...], jnp.where(odd, one, two),
+            jnp.where(upper, side_two, side_one), jnp.where(upper, side_one, side_two),
+        ],
+        axis=0,
     )
     ordered = dot_nn(near_order_ref[...], near).astype(BF16)
     qkv_two = dot_nn(ordered[:, :D], w_qkv_ref[1]).astype(BF16)
@@ -326,7 +333,6 @@
     output_ref[...] = stream + branch_two.astype(F32)
     proj_one = dot_tn(heads_ref[...], d_stream)
     proj_two = dot_tn(heads_two, cotangent)
-    upper = core_ref[0] == 1
     kept_ref[:INNER] = jnp.where(upper, proj_two, proj_one).astype(BF16)
     sent_ref[:INNER] = jnp.where(upper, proj_one, proj_two).astype(BF16)
 
@@ -456,9 +462,9 @@
 DEPTH = ("z_lo", "z_hi")
 
 
-def passed_along(array, axes, by):
+def swapped(array, axes, side):
     length = lax.axis_size(axes)
-    return lax.ppermute(array, axes, [(i, (i + by) % length) for i in range(length)])
+    return lax.ppermute(array, axes, [(i, (i + (side if i % 2 else -side)) % length) for i in range(length)])
 
 
 def local(tokens, land_mask, keep_rows, land_embed, norm_gains, w_qkv, w_proj, rel_bias, cotangent):
@@ -467,6 +473,7 @@
     band, wide = band_rows(cols), D + INNER
     scale_out = float(rows * lax.axis_size(LAT) * cols * lax.axis_size(LON)) ** (-0.5)
     row_first = scalars((lax.axis_index(LAT) * rows).astype(jnp.int32).reshape(1))
+    odd = scalars((lax.axis_index(LAT) % 2).astype(jnp.int32).reshape(1))
     core = scalars(lax.axis_index("core").astype(jnp.int32).reshape(1))
     keep_in = scalars(keep_rows)
     order = own_windows(cols)
@@ -477,32 +484,34 @@
     reach = in_hbm(fixed(reach_matrix()))
     cot_flat = in_hbm(cotangent.reshape(cells, D))
 
-    wide_one, qkv_one, heads_one, probs_one, rolling, to_left, to_right = call(
+    wide_one, qkv_one, heads_one, probs_one, rolling, to_one, to_two = call(
         first_kernel,
         [
             hbm(cells, 2 * D, dtype=F32), hbm(count * PLACES, 3 * INNER), hbm(cells, INNER),
-            hbm(count, GROUPS, TILES, 8, PLACES, dtype=F32), either(cells, wide), either(SIDE, wide), either(SIDE, wide),
+            hbm(count, GROUPS, TILES, 8, PLACES, dtype=F32), either(cells, wide), either(band, wide), either(band, wide),
         ],
         [
-            row_first, keep_in, in_hbm(tokens.reshape(cells, D)), in_hbm(land_mask), in_hbm(land_embed),
+            odd, row_first, keep_in, in_hbm(tokens.reshape(cells, D)), in_hbm(land_mask), in_hbm(land_embed),
             in_hbm(norm_gains), layer(w_qkv, 0), in_hbm(w_proj), layer(rel_bias, 0), cot_flat,
             order, order_back, spread, reach,
-            in_hbm(fixed(side_rows(cols, 0))), in_hbm(fixed(side_rows(cols, cols - HALF_LON))),
         ],
     )
 
-    right = passed_along(to_left, LON, -1)
-    left = passed_along(to_right, LON, 1)
-    to_above = jnp.concatenate([rolling[:band], left[: SIDE // 2], right[: SIDE // 2]], axis=0)
-    to_below = jnp.concatenate([rolling[cells - band :], left[SIDE // 2 :], right[SIDE // 2 :]], axis=0)
-    below = passed_along(to_above, LAT, -1)
-    above = passed_along(to_below, LAT, 1)
+    one = swapped(to_one, LAT, 1)
+    two = swapped(to_two, LAT, -1)
+    to_one, to_two = call(
+        functools.partial(edge_kernel, cols),
+        [either(SIDE, wide), either(SIDE, wide)],
+        [odd, core, whole(one), whole(rolling), whole(two)],
+    )
+    side_one = swapped(to_one, LON, 1)
+    side_two = swapped(to_two, LON, -1)
 
     output, grad_tokens, kept, sent = call(
         second_kernel,
         [hbm(cells, D, dtype=F32), hbm(cells, D), either(INNER + 2 * GAIN_ROWS, D), either(INNER + 2 * GAIN_ROWS, D)],
         [
-            core, row_first, keep_in, whole(above), whole(left), whole(rolling), whole(right), whole(below),
+            odd, core, row_first, keep_in, whole(one), whole(rolling), whole(two), whole(side_one), whole(side_two),
             in_hbm(wide_one), in_hbm(qkv_one), in_hbm(heads_one), in_hbm(probs_one), cot_flat,
             in_hbm(norm_gains), in_hbm(w_qkv), in_hbm(w_proj), layer(rel_bias, 1),
             order, order_back, near_order, near_back, spread, spread_back, reach,

time: 112 us -> 105 us (0.938)
  blocking collectives: 50.5 us -> 45 us
  starting transfers between devices: 37.8 us -> 35.8 us
    all_to_all x1, blocking collectives: 24.3 us -> 15.3 us  [local(): parts = lax.all_to_all(pieces, PLANE, 0, 0, tiled=True)]
    all_to_all x1, blocking collectives: 9.17 us -> 12.6 us  [local(): parts = lax.all_to_all(pieces, DEPTH, 0, 0, tiled=True)]
    ppermute x1, starting transfers between devices: 6.35 us -> 3.73 us  [local(): landed = lax.ppermute(sent, 'core', swap)]
    pallas_call x6 -> x7, Pallas kernels: 15.4 us -> 15.9 us  [call(): pl.pallas_call(kernel, grid=(1,), in_specs=specs, out_specs=out_specs, ou...]
  transfers between devices with their start and end apart: 6 -> 6, of which waited for: 4 -> 5; matrix products, arithmetic and copies ran while one was open for 0% -> 0% of each run, Pallas kernels for 0% -> 0%
where the time goes in v4:
time: 105 us
  blocking collectives  45 us (43%)
  starting transfers between devices  35.8 us (34%)
  Pallas kernels  15.9 us (15%)
  waiting for transfers between devices  6.94 us (7%)
    ppermute x4, starting transfers between devices, swapped(): lax.ppermute(array, axes, [(i, (i + (side if i % 2 else -side)) % length)...  25.7 us
    all_to_all x1, blocking collectives, local(): mine = lax.all_to_all(pieces, PLANE, 0, 0, tiled=True)  17.1 us
    pallas_call x7, Pallas kernels, call(): pl.pallas_call(kernel, grid=(1,), in_specs=specs, out_specs=out_specs, ou...  15.9 us
    all_to_all x1, blocking collectives, local(): parts = lax.all_to_all(pieces, PLANE, 0, 0, tiled=True)  15.3 us
    all_to_all x1, blocking collectives, local(): parts = lax.all_to_all(pieces, DEPTH, 0, 0, tiled=True)  12.6 us
    ppermute x1, starting transfers between devices, local(): other = lax.ppermute(mine, 'core', swap)  6.42 us
    ppermute x4, waiting for transfers between devices, swapped(): lax.ppermute(array, axes, [(i, (i + (side if i % 2 else -side)) % length)...  4.64 us
    ppermute x1, starting transfers between devices, local(): landed = lax.ppermute(sent, 'core', swap)  3.73 us
  transfers between devices with their start and end apart: 6, of which 5 were waited for; matrix products, arithmetic and copies ran while one was open for 0% of the time, Pallas kernels for 0%

profile of v4, /device:TPU:1, one launch (start us, length us, event | category | flops | bytes accessed | tf_op | source)
XLA Modules:
  0.0 105.1 jit_solution(17468928456366318186)
XLA Ops:
  0.6 0.0 copy-start
  0.7 0.6 copy-done
  1.3 0.0 copy-start.1
  1.3 4.4 %shard_map.183 = (f32[144,1024]{1,0:T(8,128)}, bf16[160,768]{1,0:T(8,128)(2,1)}, bf16[144,256]{1,0:T(8,128)(2,1)}, f32[2,2,36,8,80]{4,3,2,1,0:T(8,128)}, bf16[14...) custom-call(s32[1]{0:T(128)} %bitcast.odd_ref, s32[1]{0:T(128)} %bitcast.2.row_ref, ...), custom_call_target="tpu_custom_call" | custom-call | tf_op jit(solution)/shard_map/pallas_call | solution.py:449
  5.8 14.4 %collective-permute-start = (bf16[80,768]{1,0:T(8,128)(2,1)S(1)}, bf16[80,768]{1,0:T(8,128)(2,1)S(1)}, u32[]{:S(2)}, u32[]{:S(2)}) collective-permute-start(bf16[80,768]{1,0:T(8,128)(2,1)S(1)} %get-tuple-element.19), channel_id=1, source_target_pairs={{0,15},{1,2},{2,1},{3,4},{4,3},{5,6},{6,5},{7,8},{8,7},{9,10},{10,... | collective-permute-start | bytes 368648 | tf_op jit(solution)/shard_map/ppermute | solution.py:467
  20.1 1.9 %collective-permute-start.1 = (bf16[80,768]{1,0:T(8,128)(2,1)S(1)}, bf16[80,768]{1,0:T(8,128)(2,1)S(1)}, u32[]{:S(2)}, u32[]{:S(2)}) collective-permute-start(bf16[80,768]{1,0:T(8,128)(2,1)S(1)} %get-tuple-element.21), channel_id=1, source_target_pairs={{0,1},{1,0},{2,3},{3,2},{4,5},{5,4},{6,7},{7,6},{8,9},{9,8},{10,11... | collective-permute-start | bytes 368648 | tf_op jit(solution)/shard_map/ppermute | solution.py:467
  22.1 1.8 %collective-permute-done.one_ref = bf16[80,768]{1,0:T(8,128)(2,1)S(1)} collective-permute-done((bf16[80,768]{1,0:T(8,128)(2,1)S(1)}, bf16[80,768]{1,0:T(8,128)(2,1)S(1)}, u32[]{:S(2)}, u32[]{:S(2)}) %collective-permute-start) | collective-permute-done | bytes 122912 | tf_op jit(solution)/shard_map/ppermute | solution.py:467
  23.8 1.9 %collective-permute-done.1.two_ref = bf16[80,768]{1,0:T(8,128)(2,1)S(1)} collective-permute-done((bf16[80,768]{1,0:T(8,128)(2,1)S(1)}, bf16[80,768]{1,0:T(8,128)(2,1)S(1)}, u32[]{:S(2)}, u32[]{:S(2)}) %collective-permute-start.1) | collective-permute-done | bytes 122912 | tf_op jit(solution)/shard_map/ppermute | solution.py:467
  25.7 0.3 shard_map.184
  26.1 5.1 %collective-permute-start.2 = (bf16[80,768]{1,0:T(8,128)(2,1)S(1)}, bf16[80,768]{1,0:T(8,128)(2,1)S(1)}, u32[]{:S(2)}, u32[]{:S(2)}) collective-permute-start(bf16[80,768]{1,0:T(8,128)(2,1)S(1)} %get-tuple-element.22), channel_id=1, source_target_pairs={{0,496},{16,32},{32,16},{48,64},{64,48},{80,96},{96,80},{112,128},... | collective-permute-start | bytes 368648 | tf_op jit(solution)/shard_map/ppermute | solution.py:467
  31.2 4.3 %collective-permute-start.3 = (bf16[80,768]{1,0:T(8,128)(2,1)S(1)}, bf16[80,768]{1,0:T(8,128)(2,1)S(1)}, u32[]{:S(2)}, u32[]{:S(2)}) collective-permute-start(bf16[80,768]{1,0:T(8,128)(2,1)S(1)} %get-tuple-element.23), channel_id=1, source_target_pairs={{0,16},{16,0},{32,48},{48,32},{64,80},{80,64},{96,112},{112,96},{1... | collective-permute-start | bytes 368648 | tf_op jit(solution)/shard_map/ppermute | solution.py:467
  35.5 0.0 collective-permute-done.2.side_one_ref
  35.5 0.9 collective-permute-done.3.side_two_ref
  36.5 0.0 copy-done.1
  36.5 9.5 %shard_map.185 = (f32[144,512]{1,0:T(8,128)}, bf16[144,512]{1,0:T(8,128)(2,1)}, bf16[272,512]{1,0:T(8,128)(2,1)S(1)}, bf16[272,512]{1,0:T(8,128)(2,1)S(1)}) custom-call(s32[1]{0:T(128)} %bitcast.odd_ref, s32[1]{0:T(128)} %bitcast.1.core_ref, s32[1]{0:T(128)} %bitcast.2.row_ref, s32[96]{0:T(128)S(1)} %copy-done.1, ...), custom_call_target="tpu_custom_call" | custom-call | tf_op jit(solution)/shard_map/pallas_call | solution.py:449
  46.0 3.7 %collective-permute-start.4 = (bf16[272,512]{1,0:T(8,128)(2,1)S(1)}, bf16[272,512]{1,0:T(8,128)(2,1)S(1)}, u32[]{:S(2)}, u32[]{:S(2)}) collective-permute-start(bf16[272,512]{1,0:T(8,128)(2,1)S(1)} %get-tuple-element.31), channel_id=1, source_target_pairs={{0,16},{16,0},{1,17},{17,1},{2,18},{18,2},{3,19},{19,3},{4,20},{20... | collective-permute-start | bytes 835592 | tf_op jit(solution)/shard_map/ppermute | solution.py:524
  49.7 1.2 %collective-permute-done.4.landed_ref = bf16[272,512]{1,0:T(8,128)(2,1)S(1)} collective-permute-done((bf16[272,512]{1,0:T(8,128)(2,1)S(1)}, bf16[272,512]{1,0:T(8,128)(2,1)S(1)}, u32[]{:S(2)}, u32[]{:S(2)}) %collective-permute-start.4) | collective-permute-done | bytes 278560 | tf_op jit(solution)/shard_map/ppermute | solution.py:524
  50.9 0.1 shard_map.186
  51.0 15.3 %all_to_all.15.parts_ref = bf16[32,16,384]{2,1,0:T(8,128)(2,1)S(1)} all-to-all(bf16[32,16,384]{2,1,0:T(8,128)(2,1)S(1)} %shard_map.186), channel_id=1, replica_groups=mesh['z_lo'=4,'x'=4,'core'=2,'z_hi'=2,'y'=8] {'x','y'}, dimensions={0} | all-to-all | bytes 786432 | tf_op jit(solution)/shard_map/all_to_all | solution.py:526
  66.2 0.1 shard_map.187
  66.3 12.6 %all_to_all.16.parts_ref = bf16[8,16,384]{2,1,0:T(8,128)(2,1)S(1)} all-to-all(bf16[8,16,384]{2,1,0:T(8,128)(2,1)S(1)} %shard_map.187), channel_id=1, replica_groups=mesh['z_lo'=4,'x'=4,'core'=2,'z_hi'=2,'y'=8] {'z_lo','z_hi'}, dimensions={0} | all-to-all | bytes 196608 | tf_op jit(solution)/shard_map/all_to_all | solution.py:528
  79.0 0.6 shard_map.188
  79.6 17.1 %all_to_all.17.mine_ref = bf16[32,16,256]{2,1,0:T(8,128)(2,1)S(1)} all-to-all(bf16[32,16,256]{2,1,0:T(8,128)(2,1)S(1)} %get-tuple-element.32), channel_id=1, replica_groups=mesh['z_lo'=4,'x'=4,'core'=2,'z_hi'=2,'y'=8] {'x','y'}, dimensions={0} | all-to-all | bytes 524288 | tf_op jit(solution)/shard_map/all_to_all | solution.py:534
  96.7 6.4 %collective-permute-start.5 = (bf16[32,16,256]{2,1,0:T(8,128)(2,1)S(1)}, bf16[32,16,256]{2,1,0:T(8,128)(2,1)S(1)}, u32[]{:S(2)}, u32[]{:S(2)}) collective-permute-start(bf16[32,16,256]{2,1,0:T(8,128)(2,1)S(1)} %all_to_all.17.mine_ref), channel_id=1, source_target_pairs={{0,16},{16,0},{1,17},{17,1},{2,18},{18,2},{3,19},{19,3},{4,20},{20... | collective-permute-start | bytes 786440 | tf_op jit(solution)/shard_map/ppermute | solution.py:535
  103.1 1.1 %collective-permute-done.5.other_ref = bf16[32,16,256]{2,1,0:T(8,128)(2,1)S(1)} collective-permute-done((bf16[32,16,256]{2,1,0:T(8,128)(2,1)S(1)}, bf16[32,16,256]{2,1,0:T(8,128)(2,1)S(1)}, u32[]{:S(2)}, u32[]{:S(2)}) %collective-permute-start.5) | collective-permute-done | bytes 262176 | tf_op jit(solution)/shard_map/ppermute | solution.py:535
  104.2 0.8 shard_map.189
Async XLA Ops:
  0.6 0.7 copy-start
  1.3 35.2 %copy-start.1 = (s32[96]{0:T(128)S(1)}, s32[96]{0:T(128)}, u32[]{:S(2)}) copy-start(s32[96]{0:T(128)} %keep_ref.3) | copy-start | bytes 1156
  5.8 18.1 %collective-permute-start = (bf16[80,768]{1,0:T(8,128)(2,1)S(1)}, bf16[80,768]{1,0:T(8,128)(2,1)S(1)}, u32[]{:S(2)}, u32[]{:S(2)}) collective-permute-start(bf16[80,768]{1,0:T(8,128)(2,1)S(1)} %get-tuple-element.19), channel_id=1, source_target_pairs={{0,15},{1,2},{2,1},{3,4},{4,3},{5,6},{6,5},{7,8},{8,7},{9,10},{10,... | collective-permute-start | bytes 368648 | tf_op jit(solution)/shard_map/ppermute | solution.py:467
  20.1 5.6 %collective-permute-start.1 = (bf16[80,768]{1,0:T(8,128)(2,1)S(1)}, bf16[80,768]{1,0:T(8,128)(2,1)S(1)}, u32[]{:S(2)}, u32[]{:S(2)}) collective-permute-start(bf16[80,768]{1,0:T(8,128)(2,1)S(1)} %get-tuple-element.21), channel_id=1, source_target_pairs={{0,1},{1,0},{2,3},{3,2},{4,5},{5,4},{6,7},{7,6},{8,9},{9,8},{10,11... | collective-permute-start | bytes 368648 | tf_op jit(solution)/shard_map/ppermute | solution.py:467
  26.1 9.4 %collective-permute-start.2 = (bf16[80,768]{1,0:T(8,128)(2,1)S(1)}, bf16[80,768]{1,0:T(8,128)(2,1)S(1)}, u32[]{:S(2)}, u32[]{:S(2)}) collective-permute-start(bf16[80,768]{1,0:T(8,128)(2,1)S(1)} %get-tuple-element.22), channel_id=1, source_target_pairs={{0,496},{16,32},{32,16},{48,64},{64,48},{80,96},{96,80},{112,128},... | collective-permute-start | bytes 368648 | tf_op jit(solution)/shard_map/ppermute | solution.py:467
  31.2 5.3 %collective-permute-start.3 = (bf16[80,768]{1,0:T(8,128)(2,1)S(1)}, bf16[80,768]{1,0:T(8,128)(2,1)S(1)}, u32[]{:S(2)}, u32[]{:S(2)}) collective-permute-start(bf16[80,768]{1,0:T(8,128)(2,1)S(1)} %get-tuple-element.23), channel_id=1, source_target_pairs={{0,16},{16,0},{32,48},{48,32},{64,80},{80,64},{96,112},{112,96},{1... | collective-permute-start | bytes 368648 | tf_op jit(solution)/shard_map/ppermute | solution.py:467
  46.0 4.9 %collective-permute-start.4 = (bf16[272,512]{1,0:T(8,128)(2,1)S(1)}, bf16[272,512]{1,0:T(8,128)(2,1)S(1)}, u32[]{:S(2)}, u32[]{:S(2)}) collective-permute-start(bf16[272,512]{1,0:T(8,128)(2,1)S(1)} %get-tuple-element.31), channel_id=1, source_target_pairs={{0,16},{16,0},{1,17},{17,1},{2,18},{18,2},{3,19},{19,3},{4,20},{20... | collective-permute-start | bytes 835592 | tf_op jit(solution)/shard_map/ppermute | solution.py:524
  96.7 7.6 %collective-permute-start.5 = (bf16[32,16,256]{2,1,0:T(8,128)(2,1)S(1)}, bf16[32,16,256]{2,1,0:T(8,128)(2,1)S(1)}, u32[]{:S(2)}, u32[]{:S(2)}) collective-permute-start(bf16[32,16,256]{2,1,0:T(8,128)(2,1)S(1)} %all_to_all.17.mine_ref), channel_id=1, source_target_pairs={{0,16},{16,0},{1,17},{17,1},{2,18},{18,2},{3,19},{19,3},{4,20},{20... | collective-permute-start | bytes 786440 | tf_op jit(solution)/shard_map/ppermute | solution.py:535

commit v5 on v4

--- a/solution.py
+++ b/solution.py
@@ -372,32 +372,32 @@
     pair = gain_pair(pair_sum(total[INNER:, :128]))
     pieces, tall = out_ref.shape[0], out_ref.shape[1]
     for s in range(pieces):
-        row, col = tall * (s // 2), D // 2 * (s % 2)
-        out_ref[s, :, : D // 2] = low[row : row + tall, col : col + D // 2]
-        out_ref[s, : 2 * GAIN_ROWS, D // 2 :] = pair
-        if tall > 2 * GAIN_ROWS:
-            out_ref[s, 2 * GAIN_ROWS :, D // 2 :] = jnp.zeros((tall - 2 * GAIN_ROWS, 128), BF16)
+        fill_piece(out_ref, s, low[s * tall : (s + 1) * tall], pair)
+
+
+def fill_piece(out_ref, s, low, pair):
+    tall = out_ref.shape[1]
+    out_ref[s, :, :D] = low
+    out_ref[s, : 2 * GAIN_ROWS, D:] = pair
+    if tall > 2 * GAIN_ROWS:
+        out_ref[s, 2 * GAIN_ROWS :, D:] = jnp.zeros((tall - 2 * GAIN_ROWS, 128), BF16)
 
 
 def added(parts_ref):
     total = parts_ref[0].astype(F32)
     for s in range(1, parts_ref.shape[0]):
         total = total + parts_ref[s].astype(F32)
-    return total[:, : D // 2], pair_sum(total[:, D // 2 :])
-
-
-def plane_sum_kernel(parts_ref, out_ref):
+    return total[:, :D], pair_sum(total[:, D:])
+
+
+def near_sum_kernel(parts_ref, out_ref):
     proj, gain = added(parts_ref)
     low, pair = proj.astype(BF16), gain_pair(gain)
-    tall = out_ref.shape[1]
     for s in range(out_ref.shape[0]):
-        out_ref[s, :, : D // 2] = low
-        out_ref[s, : 2 * GAIN_ROWS, D // 2 :] = pair
-        if tall > 2 * GAIN_ROWS:
-            out_ref[s, 2 * GAIN_ROWS :, D // 2 :] = jnp.zeros((tall - 2 * GAIN_ROWS, 128), BF16)
-
-
-def depth_sum_kernel(scale, parts_ref, proj_ref, gains_ref):
+        fill_piece(out_ref, s, low, pair)
+
+
+def far_sum_kernel(scale, parts_ref, proj_ref, gains_ref):
     proj, gain = added(parts_ref)
     low = (proj * scale).astype(BF16)
     for s in range(proj_ref.shape[0]):
@@ -409,17 +409,14 @@
 
 
 def join_kernel(core_ref, mine_ref, other_ref, out_ref):
-    pieces, tall = mine_ref.shape[0], mine_ref.shape[1]
     upper = core_ref[0] == 1
-    for s in range(pieces):
-        row, col = tall * (s // 2), D // 2 * (s % 2)
-        mine, other = mine_ref[s], other_ref[s]
-        out_ref[0, row : row + tall, col : col + D // 2] = jnp.where(upper, other, mine)
-        out_ref[1, row : row + tall, col : col + D // 2] = jnp.where(upper, mine, other)
+    mine, other = mine_ref[...], other_ref[...]
+    out_ref[0] = jnp.where(upper, other, mine)
+    out_ref[1] = jnp.where(upper, mine, other)
 
 
 def scalars(array):
-    return array, pl.BlockSpec(memory_space=pltpu.SMEM)
+    return pltpu.with_memory_space_constraint(array, pltpu.HBM), pl.BlockSpec(memory_space=pltpu.SMEM)
 
 
 def whole(array):
@@ -452,14 +449,14 @@
         in_specs=specs,
         out_specs=out_specs,
         out_shape=outs,
-        compiler_params=pltpu.CompilerParams(vmem_limit_bytes=50 * 1024 * 1024),
+        compiler_params=pltpu.CompilerParams(vmem_limit_bytes=30 * 1024 * 1024),
     )(*arrays)
 
 
-LON = ("z_lo", "x", "core")
-LAT = ("z_hi", "y")
-PLANE = ("x", "y")
-DEPTH = ("z_lo", "z_hi")
+LON = ("z_mid", "z_low", "x", "core")
+LAT = ("z_hi", "y_hi", "y_low")
+NEAR = ("z_low", "x", "y_low")
+FAR = ("z_mid", "z_hi", "y_hi")
 
 
 def swapped(array, axes, side):
@@ -487,8 +484,8 @@
     wide_one, qkv_one, heads_one, probs_one, rolling, to_one, to_two = call(
         first_kernel,
         [
-            hbm(cells, 2 * D, dtype=F32), hbm(count * PLACES, 3 * INNER), hbm(cells, INNER),
-            hbm(count, GROUPS, TILES, 8, PLACES, dtype=F32), either(cells, wide), either(band, wide), either(band, wide),
+            either(cells, 2 * D, dtype=F32), either(count * PLACES, 3 * INNER), either(cells, INNER),
+            either(count, GROUPS, TILES, 8, PLACES, dtype=F32), either(cells, wide), either(band, wide), either(band, wide),
         ],
         [
             odd, row_first, keep_in, in_hbm(tokens.reshape(cells, D)), in_hbm(land_mask), in_hbm(land_embed),
@@ -512,35 +509,39 @@
         [hbm(cells, D, dtype=F32), hbm(cells, D), either(INNER + 2 * GAIN_ROWS, D), either(INNER + 2 * GAIN_ROWS, D)],
         [
             odd, core, row_first, keep_in, whole(one), whole(rolling), whole(two), whole(side_one), whole(side_two),
-            in_hbm(wide_one), in_hbm(qkv_one), in_hbm(heads_one), in_hbm(probs_one), cot_flat,
+            whole(wide_one), whole(qkv_one), whole(heads_one), whole(probs_one), cot_flat,
             in_hbm(norm_gains), in_hbm(w_qkv), in_hbm(w_proj), layer(rel_bias, 1),
             order, order_back, near_order, near_back, spread, spread_back, reach,
         ],
     )
 
-    planes, depths, cores = lax.axis_size(PLANE), lax.axis_size(DEPTH), lax.axis_size("core")
-    tall = 2 * INNER // planes
-    swap = [(i, (i + 1) % cores) for i in range(cores)]
+    near, far = lax.axis_size(NEAR), lax.axis_size(FAR)
+    tall = INNER // near
+    swap = [(0, 1), (1, 0)]
     landed = lax.ppermute(sent, "core", swap)
-    (pieces,) = call(core_sum_kernel, [either(planes, tall, D // 2 + 128)], [whole(kept), whole(landed)])
-    parts = lax.all_to_all(pieces, PLANE, 0, 0, tiled=True)
-    (pieces,) = call(plane_sum_kernel, [either(depths, tall, D // 2 + 128)], [whole(parts)])
-    parts = lax.all_to_all(pieces, DEPTH, 0, 0, tiled=True)
+    (pieces,) = call(core_sum_kernel, [either(near, tall, D + 128)], [whole(kept), whole(landed)])
+    parts = lax.all_to_all(pieces, NEAR, 0, 0, tiled=True)
+    (pieces,) = call(near_sum_kernel, [either(far, tall, D + 128)], [whole(parts)])
+    parts = lax.all_to_all(pieces, FAR, 0, 0, tiled=True)
     pieces, grad_gains = call(
-        functools.partial(depth_sum_kernel, scale_out),
-        [either(planes, tall, D // 2), either(2, D, dtype=F32)],
+        functools.partial(far_sum_kernel, scale_out),
+        [either(near, tall, D), either(2, D, dtype=F32)],
         [whole(parts)],
     )
-    mine = lax.all_to_all(pieces, PLANE, 0, 0, tiled=True)
+    mine = lax.all_to_all(pieces, NEAR, 0, 0, tiled=True).reshape(INNER, D)
     other = lax.ppermute(mine, "core", swap)
     (grad_proj,) = call(join_kernel, [either(2, INNER, D)], [core, whole(mine), whole(other)])
     return output.reshape(rows, cols, D), grad_tokens.reshape(rows, cols, D), grad_proj, grad_gains
 
 
+def halved(length):
+    return (length // 2, 2) if length % 2 == 0 else (length, 1)
+
+
 def chip_axes(lon, lat):
     x = min(4, lon // 2)
     y = min(8, lat)
-    return (lon // (2 * x), x, 2, lat // y, y)
+    return (*halved(lon // (2 * x)), x, 2, lat // y, *halved(y))
 
 
 def solution(mesh):

time: 105 us -> 99.2 us (0.945)
  blocking collectives: 45 us -> 42.4 us
  starting transfers between devices: 35.8 us -> 34.2 us
  Pallas kernels: 15.9 us -> 14.6 us
    all_to_all x3, blocking collectives: 45 us -> 42.4 us  [the longest x1 21.1 us: local(): parts = lax.all_to_all(pieces, FAR, 0, 0, tiled=True)]
    ppermute x1, starting transfers between devices: 6.42 us -> 4.72 us  [local(): other = lax.ppermute(mine, 'core', swap)]
    pallas_call x7, Pallas kernels: 15.9 us -> 14.6 us  [call(): pl.pallas_call(kernel, grid=(1,), in_specs=specs, out_specs=out_specs, ou...]
where the time goes in v5:
time: 99.2 us; the launch traced here: 98.8 us
  blocking collectives  42.4 us (43%)
  starting transfers between devices  34.2 us (34%)
  Pallas kernels  14.6 us (15%)
  waiting for transfers between devices  6.94 us (7%)
    ppermute x4, starting transfers between devices, swapped(): lax.ppermute(array, axes, [(i, (i + (side if i % 2 else -side)) % length)...  25.7 us
    all_to_all x1, blocking collectives, local(): parts = lax.all_to_all(pieces, FAR, 0, 0, tiled=True)  21.1 us
    pallas_call x7, Pallas kernels, call(): pl.pallas_call(kernel, grid=(1,), in_specs=specs, out_specs=out_specs, ou...  14.6 us
    all_to_all x1, blocking collectives, local(): mine = lax.all_to_all(pieces, NEAR, 0, 0, tiled=True).reshape(INNER, D)  11.7 us
    all_to_all x1, blocking collectives, local(): parts = lax.all_to_all(pieces, NEAR, 0, 0, tiled=True)  9.59 us
    ppermute x1, starting transfers between devices, local(): other = lax.ppermute(mine, 'core', swap)  4.72 us
    ppermute x4, waiting for transfers between devices, swapped(): lax.ppermute(array, axes, [(i, (i + (side if i % 2 else -side)) % length)...  4.64 us
    ppermute x1, starting transfers between devices, local(): landed = lax.ppermute(sent, 'core', swap)  3.72 us
  transfers between devices with their start and end apart: 6, of which 5 were waited for; matrix products, arithmetic and copies ran while one was open for 0% of the time, Pallas kernels for 0%

profile of v5, /device:TPU:1, one launch (start us, length us, event | category | flops | bytes accessed | tf_op | source)
XLA Modules:
  0.0 98.8 jit_solution(3010926910940228638)
XLA Ops:
  0.6 3.6 %shard_map.183 = (f32[144,1024]{1,0:T(8,128)S(1)}, bf16[160,768]{1,0:T(8,128)(2,1)S(1)}, bf16[144,256]{1,0:T(8,128)(2,1)S(1)}, f32[2,2,36,8,80]{4,3,2,1,0:T(8,12...) custom-call(s32[1]{0:T(128)} %bitcast.odd_ref, s32[1]{0:T(128)} %bitcast.2.row_ref, ...), custom_call_target="tpu_custom_call" | custom-call | tf_op jit(solution)/shard_map/pallas_call | solution.py:446
  4.3 14.4 %collective-permute-start = (bf16[80,768]{1,0:T(8,128)(2,1)S(1)}, bf16[80,768]{1,0:T(8,128)(2,1)S(1)}, u32[]{:S(2)}, u32[]{:S(2)}) collective-permute-start(bf16[80,768]{1,0:T(8,128)(2,1)S(1)} %get-tuple-element.19), channel_id=1, source_target_pairs={{0,15},{1,2},{2,1},{3,4},{4,3},{5,6},{6,5},{7,8},{8,7},{9,10},{10,... | collective-permute-start | bytes 368648 | tf_op jit(solution)/shard_map/ppermute | solution.py:464
  18.7 1.9 %collective-permute-start.1 = (bf16[80,768]{1,0:T(8,128)(2,1)S(1)}, bf16[80,768]{1,0:T(8,128)(2,1)S(1)}, u32[]{:S(2)}, u32[]{:S(2)}) collective-permute-start(bf16[80,768]{1,0:T(8,128)(2,1)S(1)} %get-tuple-element.21), channel_id=1, source_target_pairs={{0,1},{1,0},{2,3},{3,2},{4,5},{5,4},{6,7},{7,6},{8,9},{9,8},{10,11... | collective-permute-start | bytes 368648 | tf_op jit(solution)/shard_map/ppermute | solution.py:464
  20.6 1.8 %collective-permute-done.one_ref = bf16[80,768]{1,0:T(8,128)(2,1)S(1)} collective-permute-done((bf16[80,768]{1,0:T(8,128)(2,1)S(1)}, bf16[80,768]{1,0:T(8,128)(2,1)S(1)}, u32[]{:S(2)}, u32[]{:S(2)}) %collective-permute-start) | collective-permute-done | bytes 122912 | tf_op jit(solution)/shard_map/ppermute | solution.py:464
  22.4 1.9 %collective-permute-done.1.two_ref = bf16[80,768]{1,0:T(8,128)(2,1)S(1)} collective-permute-done((bf16[80,768]{1,0:T(8,128)(2,1)S(1)}, bf16[80,768]{1,0:T(8,128)(2,1)S(1)}, u32[]{:S(2)}, u32[]{:S(2)}) %collective-permute-start.1) | collective-permute-done | bytes 122912 | tf_op jit(solution)/shard_map/ppermute | solution.py:464
  24.3 0.3 shard_map.184
  24.6 5.1 %collective-permute-start.2 = (bf16[80,768]{1,0:T(8,128)(2,1)S(1)}, bf16[80,768]{1,0:T(8,128)(2,1)S(1)}, u32[]{:S(2)}, u32[]{:S(2)}) collective-permute-start(bf16[80,768]{1,0:T(8,128)(2,1)S(1)} %get-tuple-element.22), channel_id=1, source_target_pairs={{0,496},{16,32},{32,16},{48,64},{64,48},{80,96},{96,80},{112,128},... | collective-permute-start | bytes 368648 | tf_op jit(solution)/shard_map/ppermute | solution.py:464
  29.8 4.3 %collective-permute-start.3 = (bf16[80,768]{1,0:T(8,128)(2,1)S(1)}, bf16[80,768]{1,0:T(8,128)(2,1)S(1)}, u32[]{:S(2)}, u32[]{:S(2)}) collective-permute-start(bf16[80,768]{1,0:T(8,128)(2,1)S(1)} %get-tuple-element.23), channel_id=1, source_target_pairs={{0,16},{16,0},{32,48},{48,32},{64,80},{80,64},{96,112},{112,96},{1... | collective-permute-start | bytes 368648 | tf_op jit(solution)/shard_map/ppermute | solution.py:464
  34.1 0.0 collective-permute-done.2.side_one_ref
  34.1 0.9 collective-permute-done.3.side_two_ref
  35.0 9.1 %shard_map.185 = (f32[144,512]{1,0:T(8,128)}, bf16[144,512]{1,0:T(8,128)(2,1)}, bf16[272,512]{1,0:T(8,128)(2,1)S(1)}, bf16[272,512]{1,0:T(8,128)(2,1)S(1)}) custom-call(s32[1]{0:T(128)} %bitcast.odd_ref, s32[1]{0:T(128)} %bitcast.1.core_ref, s32[1]{0:T(128)} %bitcast.2.row_ref, s32[96]{0:T(128)} %keep_ref.3, ...), custom_call_target="tpu_custom_call" | custom-call | tf_op jit(solution)/shard_map/pallas_call | solution.py:446
  44.1 3.7 %collective-permute-start.4 = (bf16[272,512]{1,0:T(8,128)(2,1)S(1)}, bf16[272,512]{1,0:T(8,128)(2,1)S(1)}, u32[]{:S(2)}, u32[]{:S(2)}) collective-permute-start(bf16[272,512]{1,0:T(8,128)(2,1)S(1)} %get-tuple-element.31), channel_id=1, source_target_pairs={{0,16},{16,0},{1,17},{17,1},{2,18},{18,2},{3,19},{19,3},{4,20},{20... | collective-permute-start | bytes 835592 | tf_op jit(solution)/shard_map/ppermute | solution.py:521
  47.8 1.2 %collective-permute-done.4.landed_ref = bf16[272,512]{1,0:T(8,128)(2,1)S(1)} collective-permute-done((bf16[272,512]{1,0:T(8,128)(2,1)S(1)}, bf16[272,512]{1,0:T(8,128)(2,1)S(1)}, u32[]{:S(2)}, u32[]{:S(2)}) %collective-permute-start.4) | collective-permute-done | bytes 278560 | tf_op jit(solution)/shard_map/ppermute | solution.py:521
  49.0 0.1 shard_map.186
  49.1 9.6 %all_to_all.15.parts_ref = bf16[16,16,640]{2,1,0:T(8,128)(2,1)S(1)} all-to-all(bf16[16,16,640]{2,1,0:T(8,128)(2,1)S(1)} %shard_map.186), channel_id=1, replica_groups=mesh['z_mid'=2,'z_low'=2,'x'=4,'core'=2,'z_hi'=2,'y_hi'=4,'y_low'=2] {'z..., dimensions={0} | all-to-all | bytes 655360 | tf_op jit(solution)/shard_map/all_to_all | solution.py:523
  58.7 0.1 shard_map.187
  58.7 21.1 %all_to_all.16.parts_ref = bf16[16,16,640]{2,1,0:T(8,128)(2,1)S(1)} all-to-all(bf16[16,16,640]{2,1,0:T(8,128)(2,1)S(1)} %shard_map.187), channel_id=1, replica_groups=mesh['z_mid'=2,'z_low'=2,'x'=4,'core'=2,'z_hi'=2,'y_hi'=4,'y_low'=2] {'z..., dimensions={0} | all-to-all | bytes 655360 | tf_op jit(solution)/shard_map/all_to_all | solution.py:525
  79.8 0.6 shard_map.188
  80.4 11.7 %all_to_all.17 = bf16[16,16,512]{2,1,0:T(8,128)(2,1)S(1)} all-to-all(bf16[16,16,512]{2,1,0:T(8,128)(2,1)S(1)} %get-tuple-element.32), channel_id=1, replica_groups=mesh['z_mid'=2,'z_low'=2,'x'=4,'core'=2,'z_hi'=2,'y_hi'=4,'y_low'=2] {'z..., dimensions={0} | all-to-all | bytes 524288 | tf_op jit(solution)/shard_map/all_to_all | solution.py:531
  92.1 4.7 %collective-permute-start.5 = (bf16[256,512]{1,0:T(8,128)(2,1)S(1)}, bf16[256,512]{1,0:T(8,128)(2,1)S(1)}, u32[]{:S(2)}, u32[]{:S(2)}) collective-permute-start(bf16[256,512]{1,0:T(8,128)(2,1)S(1)} %bitcast.8), channel_id=1, source_target_pairs={{0,16},{16,0},{1,17},{17,1},{2,18},{18,2},{3,19},{19,3},{4,20},{20... | collective-permute-start | bytes 786440 | tf_op jit(solution)/shard_map/ppermute | solution.py:532
  96.8 1.1 %collective-permute-done.5.other_ref = bf16[256,512]{1,0:T(8,128)(2,1)S(1)} collective-permute-done((bf16[256,512]{1,0:T(8,128)(2,1)S(1)}, bf16[256,512]{1,0:T(8,128)(2,1)S(1)}, u32[]{:S(2)}, u32[]{:S(2)}) %collective-permute-start.5) | collective-permute-done | bytes 262176 | tf_op jit(solution)/shard_map/ppermute | solution.py:532
  98.0 0.8 shard_map.189
Async XLA Ops:
  4.3 18.1 %collective-permute-start = (bf16[80,768]{1,0:T(8,128)(2,1)S(1)}, bf16[80,768]{1,0:T(8,128)(2,1)S(1)}, u32[]{:S(2)}, u32[]{:S(2)}) collective-permute-start(bf16[80,768]{1,0:T(8,128)(2,1)S(1)} %get-tuple-element.19), channel_id=1, source_target_pairs={{0,15},{1,2},{2,1},{3,4},{4,3},{5,6},{6,5},{7,8},{8,7},{9,10},{10,... | collective-permute-start | bytes 368648 | tf_op jit(solution)/shard_map/ppermute | solution.py:464
  18.7 5.6 %collective-permute-start.1 = (bf16[80,768]{1,0:T(8,128)(2,1)S(1)}, bf16[80,768]{1,0:T(8,128)(2,1)S(1)}, u32[]{:S(2)}, u32[]{:S(2)}) collective-permute-start(bf16[80,768]{1,0:T(8,128)(2,1)S(1)} %get-tuple-element.21), channel_id=1, source_target_pairs={{0,1},{1,0},{2,3},{3,2},{4,5},{5,4},{6,7},{7,6},{8,9},{9,8},{10,11... | collective-permute-start | bytes 368648 | tf_op jit(solution)/shard_map/ppermute | solution.py:464
  24.6 9.4 %collective-permute-start.2 = (bf16[80,768]{1,0:T(8,128)(2,1)S(1)}, bf16[80,768]{1,0:T(8,128)(2,1)S(1)}, u32[]{:S(2)}, u32[]{:S(2)}) collective-permute-start(bf16[80,768]{1,0:T(8,128)(2,1)S(1)} %get-tuple-element.22), channel_id=1, source_target_pairs={{0,496},{16,32},{32,16},{48,64},{64,48},{80,96},{96,80},{112,128},... | collective-permute-start | bytes 368648 | tf_op jit(solution)/shard_map/ppermute | solution.py:464
  29.8 5.3 %collective-permute-start.3 = (bf16[80,768]{1,0:T(8,128)(2,1)S(1)}, bf16[80,768]{1,0:T(8,128)(2,1)S(1)}, u32[]{:S(2)}, u32[]{:S(2)}) collective-permute-start(bf16[80,768]{1,0:T(8,128)(2,1)S(1)} %get-tuple-element.23), channel_id=1, source_target_pairs={{0,16},{16,0},{32,48},{48,32},{64,80},{80,64},{96,112},{112,96},{1... | collective-permute-start | bytes 368648 | tf_op jit(solution)/shard_map/ppermute | solution.py:464
  44.1 4.9 %collective-permute-start.4 = (bf16[272,512]{1,0:T(8,128)(2,1)S(1)}, bf16[272,512]{1,0:T(8,128)(2,1)S(1)}, u32[]{:S(2)}, u32[]{:S(2)}) collective-permute-start(bf16[272,512]{1,0:T(8,128)(2,1)S(1)} %get-tuple-element.31), channel_id=1, source_target_pairs={{0,16},{16,0},{1,17},{17,1},{2,18},{18,2},{3,19},{19,3},{4,20},{20... | collective-permute-start | bytes 835592 | tf_op jit(solution)/shard_map/ppermute | solution.py:521
  92.1 5.9 %collective-permute-start.5 = (bf16[256,512]{1,0:T(8,128)(2,1)S(1)}, bf16[256,512]{1,0:T(8,128)(2,1)S(1)}, u32[]{:S(2)}, u32[]{:S(2)}) collective-permute-start(bf16[256,512]{1,0:T(8,128)(2,1)S(1)} %bitcast.8), channel_id=1, source_target_pairs={{0,16},{16,0},{1,17},{17,1},{2,18},{18,2},{3,19},{19,3},{4,20},{20... | collective-permute-start | bytes 786440 | tf_op jit(solution)/shard_map/ppermute | solution.py:532

commit v6 on v5

--- a/solution.py
+++ b/solution.py
@@ -263,6 +263,12 @@
     two_ref[...] = jnp.where(odd, upper, lower)
 
 
+def turn_kernel(after_ref, w_qkv_ref, w_proj_ref, qkv_back_ref, proj_back_ref):
+    qkv_back_ref[0] = w_qkv_ref[0].T
+    qkv_back_ref[1] = w_qkv_ref[1].T
+    proj_back_ref[...] = w_proj_ref[0].T
+
+
 def edge_kernel(cols, odd_ref, core_ref, one_ref, rolling_ref, two_ref, to_one_ref, to_two_ref):
     band, cells = one_ref.shape[0], rolling_ref.shape[0]
     tall = jnp.concatenate([one_ref[...], rolling_ref[...], two_ref[...]], axis=0)
@@ -283,7 +289,7 @@
 
 def second_kernel(
     odd_ref, core_ref, row_ref, keep_ref, one_ref, rolling_ref, two_ref, side_one_ref, side_two_ref,
-    wide_ref, qkv_ref, heads_ref, probs_ref, cot_ref, gains_ref, w_qkv_ref, w_proj_ref, table_ref,
+    wide_ref, qkv_ref, heads_ref, probs_ref, cot_ref, gains_ref, w_qkv_ref, qkv_back_ref, w_proj_ref, proj_back_ref, table_ref,
     order_ref, order_back_ref, near_order_ref, near_back_ref, spread_ref, spread_back_ref, reach_ref,
     output_ref, grad_ref, kept_ref, sent_ref,
 ):
@@ -300,7 +306,7 @@
         axis=0,
     )
     ordered = dot_nn(near_order_ref[...], near).astype(BF16)
-    qkv_two = dot_nn(ordered[:, :D], w_qkv_ref[1]).astype(BF16)
+    qkv_two = dot_nn(ordered[:, :D], w_qkv_ref[0]).astype(BF16)
     blocks = position_bias(table_ref[0], reach_ref[...])
     across = near_order_ref.shape[0] // PLACES // 2
     biases = []
@@ -322,21 +328,21 @@
     rows_two = jnp.concatenate([jnp.concatenate(d_windows, axis=0), jnp.concatenate(outs, axis=0)], axis=1)
     unrolled = dot_nn(near_back_ref[...], rows_two).astype(BF16)
     heads_two = unrolled[:, 3 * INNER :]
-    d_normed_two = dot_nt(unrolled[:, : 3 * INNER], w_qkv_ref[1]).astype(BF16)
+    d_normed_two = dot_nn(unrolled[:, : 3 * INNER], qkv_back_ref[1]).astype(BF16)
 
     stream = wide_ref[:, D:]
     unit_two, inv_two = norm_stats(stream)
     d_branch, gain_two = norm_back(d_normed_two.astype(F32), unit_two, inv_two, gains_ref[1:2])
     cotangent = cot_ref[...]
     d_stream = (cotangent.astype(F32) + d_branch).astype(BF16)
-    branch_two = dot_nn(heads_two, w_proj_ref[1]).astype(BF16)
+    branch_two = dot_nn(heads_two, w_proj_ref[0]).astype(BF16)
     output_ref[...] = stream + branch_two.astype(F32)
     proj_one = dot_tn(heads_ref[...], d_stream)
     proj_two = dot_tn(heads_two, cotangent)
     kept_ref[:INNER] = jnp.where(upper, proj_two, proj_one).astype(BF16)
     sent_ref[:INNER] = jnp.where(upper, proj_one, proj_two).astype(BF16)
 
-    d_heads = dot_nt(d_stream, w_proj_ref[0]).astype(BF16)
+    d_heads = dot_nn(d_stream, proj_back_ref[...]).astype(BF16)
     d_outs = dot_nn(order_ref[...], d_heads).astype(BF16)
     qkv_one = qkv_ref[...]
     windows = [window_rows(qkv_one, w) for w in range(probs_ref.shape[0])]
@@ -345,7 +351,7 @@
     all_probs = [[probs_ref[w, g] for g in range(GROUPS)] for w in range(probs_ref.shape[0])]
     d_windows = attend_back(d_outs, all_probs, [here[:, :INNER] for here in windows], stacks, spread_back, own)
     d_qkv = dot_nn(order_back_ref[...], jnp.concatenate(d_windows, axis=0)).astype(BF16)
-    d_normed = dot_nt(d_qkv, w_qkv_ref[0]).astype(BF16)
+    d_normed = dot_nn(d_qkv, qkv_back_ref[0]).astype(BF16)
     unit_one, inv_one = norm_stats(wide_ref[:, :D])
     d_branch, gain_one = norm_back(d_normed.astype(F32), unit_one, inv_one, gains_ref[0:1])
     grad_ref[...] = (d_stream.astype(F32) + d_branch).astype(BF16)
@@ -402,13 +408,13 @@
     low = (proj * scale).astype(BF16)
     for s in range(proj_ref.shape[0]):
         proj_ref[s] = low
-    gain = gain * scale
-    per_row = D // 128
+    gains_ref[...] = gain * scale
+
+
+def join_kernel(core_ref, mine_ref, other_ref, gain_ref, out_ref, gains_ref):
+    gain, per_row = gain_ref[...], D // 128
     for r in range(GAIN_ROWS):
         gains_ref[r // per_row : r // per_row + 1, 128 * (r % per_row) : 128 * (r % per_row + 1)] = gain[r : r + 1]
-
-
-def join_kernel(core_ref, mine_ref, other_ref, out_ref):
     upper = core_ref[0] == 1
     mine, other = mine_ref[...], other_ref[...]
     out_ref[0] = jnp.where(upper, other, mine)
@@ -496,6 +502,11 @@
 
     one = swapped(to_one, LAT, 1)
     two = swapped(to_two, LAT, -1)
+    qkv_back, proj_back = call(
+        turn_kernel,
+        [either(2, 3 * INNER, D), either(D, INNER)],
+        [(to_two, pl.BlockSpec(memory_space=pl.ANY)), in_hbm(w_qkv), in_hbm(w_proj)],
+    )
     to_one, to_two = call(
         functools.partial(edge_kernel, cols),
         [either(SIDE, wide), either(SIDE, wide)],
@@ -510,7 +521,7 @@
         [
             odd, core, row_first, keep_in, whole(one), whole(rolling), whole(two), whole(side_one), whole(side_two),
             whole(wide_one), whole(qkv_one), whole(heads_one), whole(probs_one), cot_flat,
-            in_hbm(norm_gains), in_hbm(w_qkv), in_hbm(w_proj), layer(rel_bias, 1),
+            in_hbm(norm_gains), layer(w_qkv, 1), whole(qkv_back), layer(w_proj, 1), whole(proj_back), layer(rel_bias, 1),
             order, order_back, near_order, near_back, spread, spread_back, reach,
         ],
     )
@@ -523,14 +534,16 @@
     parts = lax.all_to_all(pieces, NEAR, 0, 0, tiled=True)
     (pieces,) = call(near_sum_kernel, [either(far, tall, D + 128)], [whole(parts)])
     parts = lax.all_to_all(pieces, FAR, 0, 0, tiled=True)
-    pieces, grad_gains = call(
+    pieces, gain = call(
         functools.partial(far_sum_kernel, scale_out),
-        [either(near, tall, D), either(2, D, dtype=F32)],
+        [either(near, tall, D), either(GAIN_ROWS, 128, dtype=F32)],
         [whole(parts)],
     )
     mine = lax.all_to_all(pieces, NEAR, 0, 0, tiled=True).reshape(INNER, D)
     other = lax.ppermute(mine, "core", swap)
-    (grad_proj,) = call(join_kernel, [either(2, INNER, D)], [core, whole(mine), whole(other)])
+    grad_proj, grad_gains = call(
+        join_kernel, [hbm(2, INNER, D), hbm(2, D, dtype=F32)], [core, whole(mine), whole(other), whole(gain)]
+    )
     return output.reshape(rows, cols, D), grad_tokens.reshape(rows, cols, D), grad_proj, grad_gains
 
 

time: 99.2 us -> 98.2 us (0.990)
  starting transfers between devices: 34.2 us -> 33 us
  Pallas kernels: 14.6 us -> 15.6 us
    ppermute x1, starting transfers between devices: 3.72 us -> 2.55 us  [local(): landed = lax.ppermute(sent, 'core', swap)]
    pallas_call x7 -> x8, Pallas kernels: 14.6 us -> 15.6 us  [call(): pl.pallas_call(kernel, grid=(1,), in_specs=specs, out_specs=out_specs, ou...]
  transfers between devices with their start and end apart: 6 -> 6, of which waited for: 5 -> 4; matrix products, arithmetic and copies ran while one was open for 0% -> 0% of each run, Pallas kernels for 0% -> 2%
where the time goes in v6:
time: 98.2 us; the launch traced here: 97.7 us
  blocking collectives  42.4 us (43%)
  starting transfers between devices  33 us (34%)
  Pallas kernels  15.6 us (16%)
  waiting for transfers between devices  6 us (6%)
    ppermute x4, starting transfers between devices, swapped(): lax.ppermute(array, axes, [(i, (i + (side if i % 2 else -side)) % length)...  25.7 us
    all_to_all x1, blocking collectives, local(): parts = lax.all_to_all(pieces, FAR, 0, 0, tiled=True)  21.1 us
    pallas_call x8, Pallas kernels, call(): pl.pallas_call(kernel, grid=(1,), in_specs=specs, out_specs=out_specs, ou...  15.6 us
    all_to_all x1, blocking collectives, local(): mine = lax.all_to_all(pieces, NEAR, 0, 0, tiled=True).reshape(INNER, D)  11.7 us
    all_to_all x1, blocking collectives, local(): parts = lax.all_to_all(pieces, NEAR, 0, 0, tiled=True)  9.59 us
    ppermute x1, starting transfers between devices, local(): other = lax.ppermute(mine, 'core', swap)  4.73 us
    ppermute x4, waiting for transfers between devices, swapped(): lax.ppermute(array, axes, [(i, (i + (side if i % 2 else -side)) % length)...  3.7 us
    ppermute x1, starting transfers between devices, local(): landed = lax.ppermute(sent, 'core', swap)  2.55 us
  transfers between devices with their start and end apart: 6, of which 4 were waited for; matrix products, arithmetic and copies ran while one was open for 0% of the time, Pallas kernels for 2%

profile of v6, /device:TPU:1, one launch (start us, length us, event | category | flops | bytes accessed | tf_op | source)
XLA Modules:
  0.0 97.7 jit_solution(10362176688842312194)
XLA Ops:
  0.6 3.6 %shard_map.183 = (f32[144,1024]{1,0:T(8,128)S(1)}, bf16[160,768]{1,0:T(8,128)(2,1)S(1)}, bf16[144,256]{1,0:T(8,128)(2,1)S(1)}, f32[2,2,36,8,80]{4,3,2,1,0:T(8,12...) custom-call(s32[1]{0:T(128)} %bitcast.odd_ref, s32[1]{0:T(128)} %bitcast.2.row_ref, ...), custom_call_target="tpu_custom_call" | custom-call | tf_op jit(solution)/shard_map/pallas_call | solution.py:452
  4.3 14.4 %collective-permute-start = (bf16[80,768]{1,0:T(8,128)(2,1)S(1)}, bf16[80,768]{1,0:T(8,128)(2,1)S(1)}, u32[]{:S(2)}, u32[]{:S(2)}) collective-permute-start(bf16[80,768]{1,0:T(8,128)(2,1)S(1)} %get-tuple-element.23), channel_id=1, source_target_pairs={{0,15},{1,2},{2,1},{3,4},{4,3},{5,6},{6,5},{7,8},{8,7},{9,10},{10,... | collective-permute-start | bytes 368648 | tf_op jit(solution)/shard_map/ppermute | solution.py:470
  18.7 1.9 %collective-permute-start.1 = (bf16[80,768]{1,0:T(8,128)(2,1)S(1)}, bf16[80,768]{1,0:T(8,128)(2,1)S(1)}, u32[]{:S(2)}, u32[]{:S(2)}) collective-permute-start(bf16[80,768]{1,0:T(8,128)(2,1)S(1)} %get-tuple-element.25.after_ref), channel_id=1, source_target_pairs={{0,1},{1,0},{2,3},{3,2},{4,5},{5,4},{6,7},{7,6},{8,9},{9,8},{10,11... | collective-permute-start | bytes 368648 | tf_op jit(solution)/shard_map/ppermute | solution.py:470
  20.6 1.8 %collective-permute-done.one_ref = bf16[80,768]{1,0:T(8,128)(2,1)S(1)} collective-permute-done((bf16[80,768]{1,0:T(8,128)(2,1)S(1)}, bf16[80,768]{1,0:T(8,128)(2,1)S(1)}, u32[]{:S(2)}, u32[]{:S(2)}) %collective-permute-start) | collective-permute-done | bytes 122912 | tf_op jit(solution)/shard_map/ppermute | solution.py:470
  22.4 1.9 %collective-permute-done.1.two_ref = bf16[80,768]{1,0:T(8,128)(2,1)S(1)} collective-permute-done((bf16[80,768]{1,0:T(8,128)(2,1)S(1)}, bf16[80,768]{1,0:T(8,128)(2,1)S(1)}, u32[]{:S(2)}, u32[]{:S(2)}) %collective-permute-start.1) | collective-permute-done | bytes 122912 | tf_op jit(solution)/shard_map/ppermute | solution.py:470
  24.3 0.3 shard_map.184
  24.6 5.1 %collective-permute-start.2 = (bf16[80,768]{1,0:T(8,128)(2,1)S(1)}, bf16[80,768]{1,0:T(8,128)(2,1)S(1)}, u32[]{:S(2)}, u32[]{:S(2)}) collective-permute-start(bf16[80,768]{1,0:T(8,128)(2,1)S(1)} %get-tuple-element.26), channel_id=1, source_target_pairs={{0,496},{16,32},{32,16},{48,64},{64,48},{80,96},{96,80},{112,128},... | collective-permute-start | bytes 368648 | tf_op jit(solution)/shard_map/ppermute | solution.py:470
  29.8 4.3 %collective-permute-start.3 = (bf16[80,768]{1,0:T(8,128)(2,1)S(1)}, bf16[80,768]{1,0:T(8,128)(2,1)S(1)}, u32[]{:S(2)}, u32[]{:S(2)}) collective-permute-start(bf16[80,768]{1,0:T(8,128)(2,1)S(1)} %get-tuple-element.27), channel_id=1, source_target_pairs={{0,16},{16,0},{32,48},{48,32},{64,80},{80,64},{96,112},{112,96},{1... | collective-permute-start | bytes 368648 | tf_op jit(solution)/shard_map/ppermute | solution.py:470
  34.1 2.0 %shard_map.185 = (bf16[2,768,512]{2,1,0:T(8,128)(2,1)S(1)}, bf16[512,256]{1,0:T(8,128)(2,1)S(1)}) custom-call(bf16[80,768]{1,0:T(8,128)(2,1)S(1)} %get-tuple-element.25.after_ref, bf16[2,512,768]{2,1,0:T(8,128)(2,1)} %w_qkv_ref.5, bf16[2,256,512]{2,1,0:T(8,128)(2,1)} %w_proj_ref.5), custom_call_target="tpu_custom_call" | custom-call | tf_op jit(solution)/shard_map/pallas_call | solution.py:452
  36.1 0.0 collective-permute-done.2.side_one_ref
  36.1 0.0 collective-permute-done.3.side_two_ref
  36.1 8.6 %shard_map.186 = (f32[144,512]{1,0:T(8,128)}, bf16[144,512]{1,0:T(8,128)(2,1)}, bf16[272,512]{1,0:T(8,128)(2,1)S(1)}, bf16[272,512]{1,0:T(8,128)(2,1)S(1)}) custom-call(s32[1]{0:T(128)} %bitcast.odd_ref, s32[1]{0:T(128)} %bitcast.1.core_ref, s32[1]{0:T(128)} %bitcast.2.row_ref, s32[96]{0:T(128)} %keep_ref.3, ...), custom_call_target="tpu_custom_call" | custom-call | tf_op jit(solution)/shard_map/pallas_call | solution.py:452
  44.7 2.6 %collective-permute-start.4 = (bf16[272,512]{1,0:T(8,128)(2,1)S(1)}, bf16[272,512]{1,0:T(8,128)(2,1)S(1)}, u32[]{:S(2)}, u32[]{:S(2)}) collective-permute-start(bf16[272,512]{1,0:T(8,128)(2,1)S(1)} %get-tuple-element.37), channel_id=1, source_target_pairs={{0,16},{16,0},{1,17},{17,1},{2,18},{18,2},{3,19},{19,3},{4,20},{20... | collective-permute-start | bytes 835592 | tf_op jit(solution)/shard_map/ppermute | solution.py:532
  47.3 1.2 %collective-permute-done.4.landed_ref = bf16[272,512]{1,0:T(8,128)(2,1)S(1)} collective-permute-done((bf16[272,512]{1,0:T(8,128)(2,1)S(1)}, bf16[272,512]{1,0:T(8,128)(2,1)S(1)}, u32[]{:S(2)}, u32[]{:S(2)}) %collective-permute-start.4) | collective-permute-done | bytes 278560 | tf_op jit(solution)/shard_map/ppermute | solution.py:532
  48.4 0.1 shard_map.187
  48.5 9.6 %all_to_all.15.parts_ref = bf16[16,16,640]{2,1,0:T(8,128)(2,1)S(1)} all-to-all(bf16[16,16,640]{2,1,0:T(8,128)(2,1)S(1)} %shard_map.187), channel_id=1, replica_groups=mesh['z_mid'=2,'z_low'=2,'x'=4,'core'=2,'z_hi'=2,'y_hi'=4,'y_low'=2] {'z..., dimensions={0} | all-to-all | bytes 655360 | tf_op jit(solution)/shard_map/all_to_all | solution.py:534
  58.1 0.1 shard_map.188
  58.2 21.1 %all_to_all.16.parts_ref = bf16[16,16,640]{2,1,0:T(8,128)(2,1)S(1)} all-to-all(bf16[16,16,640]{2,1,0:T(8,128)(2,1)S(1)} %shard_map.188), channel_id=1, replica_groups=mesh['z_mid'=2,'z_low'=2,'x'=4,'core'=2,'z_hi'=2,'y_hi'=4,'y_low'=2] {'z..., dimensions={0} | all-to-all | bytes 655360 | tf_op jit(solution)/shard_map/all_to_all | solution.py:536
  79.3 0.1 shard_map.189
  79.3 11.7 %all_to_all.17 = bf16[16,16,512]{2,1,0:T(8,128)(2,1)S(1)} all-to-all(bf16[16,16,512]{2,1,0:T(8,128)(2,1)S(1)} %get-tuple-element.38), channel_id=1, replica_groups=mesh['z_mid'=2,'z_low'=2,'x'=4,'core'=2,'z_hi'=2,'y_hi'=4,'y_low'=2] {'z..., dimensions={0} | all-to-all | bytes 524288 | tf_op jit(solution)/shard_map/all_to_all | solution.py:542
  91.0 4.7 %collective-permute-start.5 = (bf16[256,512]{1,0:T(8,128)(2,1)S(1)}, bf16[256,512]{1,0:T(8,128)(2,1)S(1)}, u32[]{:S(2)}, u32[]{:S(2)}) collective-permute-start(bf16[256,512]{1,0:T(8,128)(2,1)S(1)} %bitcast.8), channel_id=1, source_target_pairs={{0,16},{16,0},{1,17},{17,1},{2,18},{18,2},{3,19},{19,3},{4,20},{20... | collective-permute-start | bytes 786440 | tf_op jit(solution)/shard_map/ppermute | solution.py:543
  95.8 1.1 %collective-permute-done.5.other_ref = bf16[256,512]{1,0:T(8,128)(2,1)S(1)} collective-permute-done((bf16[256,512]{1,0:T(8,128)(2,1)S(1)}, bf16[256,512]{1,0:T(8,128)(2,1)S(1)}, u32[]{:S(2)}, u32[]{:S(2)}) %collective-permute-start.5) | collective-permute-done | bytes 262176 | tf_op jit(solution)/shard_map/ppermute | solution.py:543
  96.9 0.8 shard_map.190
Async XLA Ops:
  4.3 18.1 %collective-permute-start = (bf16[80,768]{1,0:T(8,128)(2,1)S(1)}, bf16[80,768]{1,0:T(8,128)(2,1)S(1)}, u32[]{:S(2)}, u32[]{:S(2)}) collective-permute-start(bf16[80,768]{1,0:T(8,128)(2,1)S(1)} %get-tuple-element.23), channel_id=1, source_target_pairs={{0,15},{1,2},{2,1},{3,4},{4,3},{5,6},{6,5},{7,8},{8,7},{9,10},{10,... | collective-permute-start | bytes 368648 | tf_op jit(solution)/shard_map/ppermute | solution.py:470
  18.7 5.6 %collective-permute-start.1 = (bf16[80,768]{1,0:T(8,128)(2,1)S(1)}, bf16[80,768]{1,0:T(8,128)(2,1)S(1)}, u32[]{:S(2)}, u32[]{:S(2)}) collective-permute-start(bf16[80,768]{1,0:T(8,128)(2,1)S(1)} %get-tuple-element.25.after_ref), channel_id=1, source_target_pairs={{0,1},{1,0},{2,3},{3,2},{4,5},{5,4},{6,7},{7,6},{8,9},{9,8},{10,11... | collective-permute-start | bytes 368648 | tf_op jit(solution)/shard_map/ppermute | solution.py:470
  24.6 11.5 %collective-permute-start.2 = (bf16[80,768]{1,0:T(8,128)(2,1)S(1)}, bf16[80,768]{1,0:T(8,128)(2,1)S(1)}, u32[]{:S(2)}, u32[]{:S(2)}) collective-permute-start(bf16[80,768]{1,0:T(8,128)(2,1)S(1)} %get-tuple-element.26), channel_id=1, source_target_pairs={{0,496},{16,32},{32,16},{48,64},{64,48},{80,96},{96,80},{112,128},... | collective-permute-start | bytes 368648 | tf_op jit(solution)/shard_map/ppermute | solution.py:470
  29.8 6.4 %collective-permute-start.3 = (bf16[80,768]{1,0:T(8,128)(2,1)S(1)}, bf16[80,768]{1,0:T(8,128)(2,1)S(1)}, u32[]{:S(2)}, u32[]{:S(2)}) collective-permute-start(bf16[80,768]{1,0:T(8,128)(2,1)S(1)} %get-tuple-element.27), channel_id=1, source_target_pairs={{0,16},{16,0},{32,48},{48,32},{64,80},{80,64},{96,112},{112,96},{1... | collective-permute-start | bytes 368648 | tf_op jit(solution)/shard_map/ppermute | solution.py:470
  44.7 3.7 %collective-permute-start.4 = (bf16[272,512]{1,0:T(8,128)(2,1)S(1)}, bf16[272,512]{1,0:T(8,128)(2,1)S(1)}, u32[]{:S(2)}, u32[]{:S(2)}) collective-permute-start(bf16[272,512]{1,0:T(8,128)(2,1)S(1)} %get-tuple-element.37), channel_id=1, source_target_pairs={{0,16},{16,0},{1,17},{17,1},{2,18},{18,2},{3,19},{19,3},{4,20},{20... | collective-permute-start | bytes 835592 | tf_op jit(solution)/shard_map/ppermute | solution.py:532
  91.0 5.9 %collective-permute-start.5 = (bf16[256,512]{1,0:T(8,128)(2,1)S(1)}, bf16[256,512]{1,0:T(8,128)(2,1)S(1)}, u32[]{:S(2)}, u32[]{:S(2)}) collective-permute-start(bf16[256,512]{1,0:T(8,128)(2,1)S(1)} %bitcast.8), channel_id=1, source_target_pairs={{0,16},{16,0},{1,17},{17,1},{2,18},{18,2},{3,19},{19,3},{4,20},{20... | collective-permute-start | bytes 786440 | tf_op jit(solution)/shard_map/ppermute | solution.py:543

commit v7 on v6

--- a/solution.py
+++ b/solution.py
@@ -269,7 +269,7 @@
     proj_back_ref[...] = w_proj_ref[0].T
 
 
-def edge_kernel(cols, odd_ref, core_ref, one_ref, rolling_ref, two_ref, to_one_ref, to_two_ref):
+def edge_kernel(cols, odd_ref, core_ref, one_ref, rolling_ref, two_ref, after_ref, to_one_ref, to_two_ref):
     band, cells = one_ref.shape[0], rolling_ref.shape[0]
     tall = jnp.concatenate([one_ref[...], rolling_ref[...], two_ref[...]], axis=0)
     shape = (SIDE, tall.shape[0])
@@ -510,7 +510,7 @@
     to_one, to_two = call(
         functools.partial(edge_kernel, cols),
         [either(SIDE, wide), either(SIDE, wide)],
-        [odd, core, whole(one), whole(rolling), whole(two)],
+        [odd, core, whole(one), whole(rolling), whole(two), (proj_back, pl.BlockSpec(memory_space=pl.ANY))],
     )
     side_one = swapped(to_one, LON, 1)
     side_two = swapped(to_two, LON, -1)

time: 98.2 us -> 101 us (1.029)
  local copies, waits for them, and re-layouts: 0 us -> 1.64 us
  starting transfers between devices: 33 us -> 34.1 us
    unnamed x0 -> x4, local copies, waits for them, and re-layouts: none -> 1.64 us
    ppermute x1, starting transfers between devices: 2.55 us -> 3.73 us  [local(): landed = lax.ppermute(sent, 'core', swap)]
where the time goes in v7:
time: 101 us; the launch traced here: 100 us
  blocking collectives  42.4 us (42%)
  starting transfers between devices  34.1 us (34%)
  Pallas kernels  16.2 us (16%)
  waiting for transfers between devices  5.1 us (5%)
  local copies, waits for them, and re-layouts  1.64 us (2%)
    ppermute x4, starting transfers between devices, swapped(): lax.ppermute(array, axes, [(i, (i + (side if i % 2 else -side)) % length)...  25.7 us
    all_to_all x1, blocking collectives, local(): parts = lax.all_to_all(pieces, FAR, 0, 0, tiled=True)  21.1 us
    pallas_call x8, Pallas kernels, call(): pl.pallas_call(kernel, grid=(1,), in_specs=specs, out_specs=out_specs, ou...  16.2 us
    all_to_all x1, blocking collectives, local(): mine = lax.all_to_all(pieces, NEAR, 0, 0, tiled=True).reshape(INNER, D)  11.7 us
    all_to_all x1, blocking collectives, local(): parts = lax.all_to_all(pieces, NEAR, 0, 0, tiled=True)  9.59 us
    ppermute x1, starting transfers between devices, local(): other = lax.ppermute(mine, 'core', swap)  4.72 us
    ppermute x1, starting transfers between devices, local(): landed = lax.ppermute(sent, 'core', swap)  3.73 us
    ppermute x4, waiting for transfers between devices, swapped(): lax.ppermute(array, axes, [(i, (i + (side if i % 2 else -side)) % length)...  2.79 us
  transfers between devices with their start and end apart: 6, of which 4 were waited for; matrix products, arithmetic and copies ran while one was open for 0% of the time, Pallas kernels for 2%

profile of v7, /device:TPU:1, one launch (start us, length us, event | category | flops | bytes accessed | tf_op | source)
XLA Modules:
  0.0 100.2 jit_solution(3854510334160547334)
XLA Ops:
  0.6 4.3 %shard_map.183 = (f32[144,1024]{1,0:T(8,128)S(1)}, bf16[160,768]{1,0:T(8,128)(2,1)S(1)}, bf16[144,256]{1,0:T(8,128)(2,1)S(1)}, f32[2,2,36,8,80]{4,3,2,1,0:T(8,12...) custom-call(s32[1]{0:T(128)} %bitcast.odd_ref, s32[1]{0:T(128)} %bitcast.2.row_ref, ...), custom_call_target="tpu_custom_call" | custom-call | tf_op jit(solution)/shard_map/pallas_call | solution.py:452
  5.0 0.0 copy-start
  5.0 0.7 copy-done
  5.7 14.4 %collective-permute-start = (bf16[80,768]{1,0:T(8,128)(2,1)}, bf16[80,768]{1,0:T(8,128)(2,1)S(1)}, u32[]{:S(2)}, u32[]{:S(2)}) collective-permute-start(bf16[80,768]{1,0:T(8,128)(2,1)} %get-tuple-element.23), channel_id=1, source_target_pairs={{0,15},{1,2},{2,1},{3,4},{4,3},{5,6},{6,5},{7,8},{8,7},{9,10},{10,... | collective-permute-start | bytes 368648 | tf_op jit(solution)/shard_map/ppermute | solution.py:470
  20.0 1.9 %collective-permute-start.1 = (bf16[80,768]{1,0:T(8,128)(2,1)}, bf16[80,768]{1,0:T(8,128)(2,1)S(1)}, u32[]{:S(2)}, u32[]{:S(2)}) collective-permute-start(bf16[80,768]{1,0:T(8,128)(2,1)} %get-tuple-element.25.after_ref), channel_id=1, source_target_pairs={{0,1},{1,0},{2,3},{3,2},{4,5},{5,4},{6,7},{7,6},{8,9},{9,8},{10,11... | collective-permute-start | bytes 368648 | tf_op jit(solution)/shard_map/ppermute | solution.py:470
  22.0 2.0 %shard_map.184 = (bf16[2,768,512]{2,1,0:T(8,128)(2,1)S(1)}, bf16[512,256]{1,0:T(8,128)(2,1)S(1)}) custom-call(bf16[80,768]{1,0:T(8,128)(2,1)} %get-tuple-element.25.after_ref, bf16[2,512,768]{2,1,0:T(8,128)(2,1)} %w_qkv_ref.5, bf16[2,256,512]{2,1,0:T(8,128)(2,1)} %w_proj_ref.5), custom_call_target="tpu_custom_call" | custom-call | tf_op jit(solution)/shard_map/pallas_call | solution.py:452
  24.0 0.0 collective-permute-done.one_ref
  24.0 1.8 %collective-permute-done.1.two_ref = bf16[80,768]{1,0:T(8,128)(2,1)S(1)} collective-permute-done((bf16[80,768]{1,0:T(8,128)(2,1)}, bf16[80,768]{1,0:T(8,128)(2,1)S(1)}, u32[]{:S(2)}, u32[]{:S(2)}) %collective-permute-start.1) | collective-permute-done | bytes 122912 | tf_op jit(solution)/shard_map/ppermute | solution.py:470
  25.9 0.3 shard_map.185
  26.2 5.1 %collective-permute-start.2 = (bf16[80,768]{1,0:T(8,128)(2,1)S(1)}, bf16[80,768]{1,0:T(8,128)(2,1)S(1)}, u32[]{:S(2)}, u32[]{:S(2)}) collective-permute-start(bf16[80,768]{1,0:T(8,128)(2,1)S(1)} %get-tuple-element.27), channel_id=1, source_target_pairs={{0,496},{16,32},{32,16},{48,64},{64,48},{80,96},{96,80},{112,128},... | collective-permute-start | bytes 368648 | tf_op jit(solution)/shard_map/ppermute | solution.py:470
  31.3 4.3 %collective-permute-start.3 = (bf16[80,768]{1,0:T(8,128)(2,1)S(1)}, bf16[80,768]{1,0:T(8,128)(2,1)S(1)}, u32[]{:S(2)}, u32[]{:S(2)}) collective-permute-start(bf16[80,768]{1,0:T(8,128)(2,1)S(1)} %get-tuple-element.28), channel_id=1, source_target_pairs={{0,16},{16,0},{32,48},{48,32},{64,80},{80,64},{96,112},{112,96},{1... | collective-permute-start | bytes 368648 | tf_op jit(solution)/shard_map/ppermute | solution.py:470
  35.6 0.0 collective-permute-done.2.side_one_ref
  35.7 0.9 collective-permute-done.3.side_two_ref
  36.6 0.0 copy-start.1
  36.6 0.9 copy-done.1
  37.5 8.5 %shard_map.186 = (f32[144,512]{1,0:T(8,128)}, bf16[144,512]{1,0:T(8,128)(2,1)}, bf16[272,512]{1,0:T(8,128)(2,1)S(1)}, bf16[272,512]{1,0:T(8,128)(2,1)S(1)}) custom-call(s32[1]{0:T(128)} %bitcast.odd_ref, s32[1]{0:T(128)} %bitcast.1.core_ref, s32[1]{0:T(128)} %bitcast.2.row_ref, s32[96]{0:T(128)} %keep_ref.3, ...), custom_call_target="tpu_custom_call" | custom-call | tf_op jit(solution)/shard_map/pallas_call | solution.py:452
  46.1 3.7 %collective-permute-start.4 = (bf16[272,512]{1,0:T(8,128)(2,1)S(1)}, bf16[272,512]{1,0:T(8,128)(2,1)S(1)}, u32[]{:S(2)}, u32[]{:S(2)}) collective-permute-start(bf16[272,512]{1,0:T(8,128)(2,1)S(1)} %get-tuple-element.37), channel_id=1, source_target_pairs={{0,16},{16,0},{1,17},{17,1},{2,18},{18,2},{3,19},{19,3},{4,20},{20... | collective-permute-start | bytes 835592 | tf_op jit(solution)/shard_map/ppermute | solution.py:532
  49.8 1.2 %collective-permute-done.4.landed_ref = bf16[272,512]{1,0:T(8,128)(2,1)S(1)} collective-permute-done((bf16[272,512]{1,0:T(8,128)(2,1)S(1)}, bf16[272,512]{1,0:T(8,128)(2,1)S(1)}, u32[]{:S(2)}, u32[]{:S(2)}) %collective-permute-start.4) | collective-permute-done | bytes 278560 | tf_op jit(solution)/shard_map/ppermute | solution.py:532
  51.0 0.1 shard_map.187
  51.0 9.6 %all_to_all.15.parts_ref = bf16[16,16,640]{2,1,0:T(8,128)(2,1)S(1)} all-to-all(bf16[16,16,640]{2,1,0:T(8,128)(2,1)S(1)} %shard_map.187), channel_id=1, replica_groups=mesh['z_mid'=2,'z_low'=2,'x'=4,'core'=2,'z_hi'=2,'y_hi'=4,'y_low'=2] {'z..., dimensions={0} | all-to-all | bytes 655360 | tf_op jit(solution)/shard_map/all_to_all | solution.py:534
  60.6 0.1 shard_map.188
  60.7 21.1 %all_to_all.16.parts_ref = bf16[16,16,640]{2,1,0:T(8,128)(2,1)S(1)} all-to-all(bf16[16,16,640]{2,1,0:T(8,128)(2,1)S(1)} %shard_map.188), channel_id=1, replica_groups=mesh['z_mid'=2,'z_low'=2,'x'=4,'core'=2,'z_hi'=2,'y_hi'=4,'y_low'=2] {'z..., dimensions={0} | all-to-all | bytes 655360 | tf_op jit(solution)/shard_map/all_to_all | solution.py:536
  81.8 0.1 shard_map.189
  81.9 11.7 %all_to_all.17 = bf16[16,16,512]{2,1,0:T(8,128)(2,1)S(1)} all-to-all(bf16[16,16,512]{2,1,0:T(8,128)(2,1)S(1)} %get-tuple-element.38), channel_id=1, replica_groups=mesh['z_mid'=2,'z_low'=2,'x'=4,'core'=2,'z_hi'=2,'y_hi'=4,'y_low'=2] {'z..., dimensions={0} | all-to-all | bytes 524288 | tf_op jit(solution)/shard_map/all_to_all | solution.py:542
  93.5 4.7 %collective-permute-start.5 = (bf16[256,512]{1,0:T(8,128)(2,1)S(1)}, bf16[256,512]{1,0:T(8,128)(2,1)S(1)}, u32[]{:S(2)}, u32[]{:S(2)}) collective-permute-start(bf16[256,512]{1,0:T(8,128)(2,1)S(1)} %bitcast.8), channel_id=1, source_target_pairs={{0,16},{16,0},{1,17},{17,1},{2,18},{18,2},{3,19},{19,3},{4,20},{20... | collective-permute-start | bytes 786440 | tf_op jit(solution)/shard_map/ppermute | solution.py:543
  98.3 1.1 %collective-permute-done.5.other_ref = bf16[256,512]{1,0:T(8,128)(2,1)S(1)} collective-permute-done((bf16[256,512]{1,0:T(8,128)(2,1)S(1)}, bf16[256,512]{1,0:T(8,128)(2,1)S(1)}, u32[]{:S(2)}, u32[]{:S(2)}) %collective-permute-start.5) | collective-permute-done | bytes 262176 | tf_op jit(solution)/shard_map/ppermute | solution.py:543
  99.4 0.8 shard_map.190
Async XLA Ops:
  5.0 0.7 copy-start
  5.7 18.3 %collective-permute-start = (bf16[80,768]{1,0:T(8,128)(2,1)}, bf16[80,768]{1,0:T(8,128)(2,1)S(1)}, u32[]{:S(2)}, u32[]{:S(2)}) collective-permute-start(bf16[80,768]{1,0:T(8,128)(2,1)} %get-tuple-element.23), channel_id=1, source_target_pairs={{0,15},{1,2},{2,1},{3,4},{4,3},{5,6},{6,5},{7,8},{8,7},{9,10},{10,... | collective-permute-start | bytes 368648 | tf_op jit(solution)/shard_map/ppermute | solution.py:470
  20.0 5.8 %collective-permute-start.1 = (bf16[80,768]{1,0:T(8,128)(2,1)}, bf16[80,768]{1,0:T(8,128)(2,1)S(1)}, u32[]{:S(2)}, u32[]{:S(2)}) collective-permute-start(bf16[80,768]{1,0:T(8,128)(2,1)} %get-tuple-element.25.after_ref), channel_id=1, source_target_pairs={{0,1},{1,0},{2,3},{3,2},{4,5},{5,4},{6,7},{7,6},{8,9},{9,8},{10,11... | collective-permute-start | bytes 368648 | tf_op jit(solution)/shard_map/ppermute | solution.py:470
  26.2 9.4 %collective-permute-start.2 = (bf16[80,768]{1,0:T(8,128)(2,1)S(1)}, bf16[80,768]{1,0:T(8,128)(2,1)S(1)}, u32[]{:S(2)}, u32[]{:S(2)}) collective-permute-start(bf16[80,768]{1,0:T(8,128)(2,1)S(1)} %get-tuple-element.27), channel_id=1, source_target_pairs={{0,496},{16,32},{32,16},{48,64},{64,48},{80,96},{96,80},{112,128},... | collective-permute-start | bytes 368648 | tf_op jit(solution)/shard_map/ppermute | solution.py:470
  31.3 5.3 %collective-permute-start.3 = (bf16[80,768]{1,0:T(8,128)(2,1)S(1)}, bf16[80,768]{1,0:T(8,128)(2,1)S(1)}, u32[]{:S(2)}, u32[]{:S(2)}) collective-permute-start(bf16[80,768]{1,0:T(8,128)(2,1)S(1)} %get-tuple-element.28), channel_id=1, source_target_pairs={{0,16},{16,0},{32,48},{48,32},{64,80},{80,64},{96,112},{112,96},{1... | collective-permute-start | bytes 368648 | tf_op jit(solution)/shard_map/ppermute | solution.py:470
  36.6 0.9 copy-start.1
  46.1 4.9 %collective-permute-start.4 = (bf16[272,512]{1,0:T(8,128)(2,1)S(1)}, bf16[272,512]{1,0:T(8,128)(2,1)S(1)}, u32[]{:S(2)}, u32[]{:S(2)}) collective-permute-start(bf16[272,512]{1,0:T(8,128)(2,1)S(1)} %get-tuple-element.37), channel_id=1, source_target_pairs={{0,16},{16,0},{1,17},{17,1},{2,18},{18,2},{3,19},{19,3},{4,20},{20... | collective-permute-start | bytes 835592 | tf_op jit(solution)/shard_map/ppermute | solution.py:532
  93.5 5.9 %collective-permute-start.5 = (bf16[256,512]{1,0:T(8,128)(2,1)S(1)}, bf16[256,512]{1,0:T(8,128)(2,1)S(1)}, u32[]{:S(2)}, u32[]{:S(2)}) collective-permute-start(bf16[256,512]{1,0:T(8,128)(2,1)S(1)} %bitcast.8), channel_id=1, source_target_pairs={{0,16},{16,0},{1,17},{17,1},{2,18},{18,2},{3,19},{19,3},{4,20},{20... | collective-permute-start | bytes 786440 | tf_op jit(solution)/shard_map/ppermute | solution.py:543
